TPU v7x, 256 devices: a whole 4x4x8 slice. The times are simulated.
256 devices in a mesh: fsdp: 64 (over z, x, core), tp: 4 (over y).
Axes of the slice: x: 4, y: 4, z: 8, core: 2. Of those that a mesh axis runs over, the one named last changes fastest.
Arguments:
- weight: float32 [2, 8192, 8192], P(None, 'fsdp', 'tp'), may hold values from -6 to 6
- gradient: bfloat16 [2, 8192, 8192], P(None, 'fsdp', 'tp'), may hold values from -6 to 6
- momentum: float32 [2, 8192, 8192], P(None, 'fsdp', 'tp'), may hold values from -24 to 24
- right_basis: bfloat16 [2, 8192, 128], P(None, 'tp'), may hold values from -4 to 4
Outputs:
- new_weight: float32 [2, 8192, 8192], P(None, 'fsdp', 'tp')
- new_momentum: float32 [2, 8192, 8192], P(None, 'fsdp', 'tp')
- new_basis: bfloat16 [2, 8192, 128], P(None, 'tp')
All inputs are finite; a program needn't handle non-finite values.
Results may differ from a plain program's by a relative error of at most 0.001.
Values sent between devices are 32-bit elements; how exact they have to be, the bound alone decides.
No kernel may reach another device: no remote copies, remote signals or barrier semaphores. Data moves between devices by JAX's collectives and lax.ppermute only.
A program may use at most 64 MiB of HBM per device.

v0:
```python
import math

import jax
import jax.numpy as jnp
from jax import lax
from jax.sharding import PartitionSpec as P

D = 8192
R = 128


HIGH = lax.Precision.HIGHEST


def apply_factor(panel, gram):
    factor_low = jnp.linalg.cholesky(gram)

    def solve_one(factor_one, panel_one):
        return jax.scipy.linalg.solve_triangular(factor_one, panel_one.T, lower=True).T

    return jax.vmap(solve_one)(factor_low, panel)


def dion_block(weight, gradient, momentum, right_basis):
    buffer = momentum + gradient.astype(jnp.float32)
    panel_part = jnp.einsum("kmn,knr->kmr", buffer, right_basis.astype(jnp.float32), precision=HIGH)
    panel = lax.psum(panel_part, "tp")
    gram = lax.psum(jnp.einsum("kmr,kms->krs", panel, panel, precision=HIGH), "fsdp")
    basis_left = apply_factor(panel, gram)
    partial_terms = jnp.einsum("kmn,kmr->nkr", buffer, basis_left, precision=HIGH)
    reduced = lax.psum(partial_terms, "fsdp")
    squares = lax.psum(jnp.sum(reduced * reduced, axis=0), "tp")
    column = reduced / jnp.sqrt(squares / D + 1e-06)
    new_momentum = buffer - 0.05 * jnp.einsum("kmr,nkr->kmn", basis_left, reduced, precision=HIGH)
    update = jnp.einsum("kmr,nkr->kmn", basis_left, column, precision=HIGH) * math.sqrt(D / R)
    new_weight = (1.0 - 0.05 * 0.1) * weight - 0.05 * update
    new_basis = jnp.transpose(column, (1, 0, 2)).astype(jnp.bfloat16)
    return (new_weight, new_momentum, new_basis)


def body(weight, gradient, momentum, right_basis):
    results = []
    for layer_idx in range(weight.shape[0]):
        pick = slice(layer_idx, layer_idx + 1)
        results.append(dion_block(weight[pick], gradient[pick], momentum[pick], right_basis[pick]))
    new_weight = jnp.concatenate([item[0] for item in results], axis=0)
    new_momentum = jnp.concatenate([item[1] for item in results], axis=0)
    new_basis = jnp.concatenate([item[2] for item in results], axis=0)
    return (new_weight, new_momentum, new_basis)


def solution(mesh):
    return jax.shard_map(
        body,
        mesh=mesh,
        in_specs=(
            P(None, "fsdp", "tp"),
            P(None, "fsdp", "tp"),
            P(None, "fsdp", "tp"),
            P(None, "tp", None),
        ),
        out_specs=(P(None, "fsdp", "tp"), P(None, "fsdp", "tp"), P(None, "tp", None)),
        check_vma=False,
    )
```

profile of v0, /device:TPU:1, one launch (start us, length us, event | category | flops | bytes accessed | tf_op | source)
XLA Modules:
  0.0 516.4 jit_solution(3004581850716073623)
XLA Ops:
  7.2 2.9 convolution_bitcast_fusion.2
  10.2 2.6 convolution_bitcast_fusion.3
  12.8 48.3 %all-reduce.12.cloned.1.call-done = (f32[1,128,128]{2,1,0:T(8,128)}, f32[1,128,128]{2,1,0:T(8,128)}) async-done(((f32[1,128,128]{2,1,0:T(8,128)}, f32[1,128,128]{2,1,0:T(8,128)}), (f32[1,128,128]{2,1,0:T(8,128)}, f32[1,128,128]{2,1,0:T(8,128)})) %all-reduce.12.cloned.1.call-update) | async-done | bytes 131088 | tf_op jit(solution)/shard_map/psum | solution.py:27
  61.1 1.8 convolution_bitcast_fusion.4
  62.9 1.8 convolution_bitcast_fusion.5
  64.8 176.8 %all-reduce.10.cloned.1.call-done = (f32[1,128,128]{1,2,0:T(8,128)}, f32[1,128,128]{1,2,0:T(8,128)}) async-done(((f32[1,128,128]{1,2,0:T(8,128)}, f32[1,128,128]{1,2,0:T(8,128)}), (f32[1,128,128]{1,2,0:T(8,128)}, f32[1,128,128]{1,2,0:T(8,128)})) %all-reduce.10.cloned.1.call-update) | async-done | bytes 131088 | tf_op jit(solution)/shard_map/psum | solution.py:28
  241.6 0.9 copy.10
  242.6 0.9 copy.8
  243.5 0.9 fusion.27
  244.4 11.7 %custom-call.10 = f32[1,128,128]{2,1,0:T(8,128)S(1)} custom-call(f32[1,128,128]{2,1,0:T(8,128)S(1)} %get-tuple-element.16), custom_call_target="Cholesky" | custom-call | tf_op jit(solution)/shard_map/jit(cholesky)/cholesky | solution.py:16
  256.1 0.6 compare_reduce_fusion
  256.8 0.7 fusion.21
  257.5 9.8 %custom-call.11 = f32[1,1,128,128]{2,3,1,0:T(8,128)S(1)} custom-call(f32[1,1,128,128]{3,2,1,0:T(8,128)S(1)} %fusion.21), custom_call_target="InvertDiagBlocksLowerTriangular" | custom-call | tf_op jit(solution)/shard_map/vmap(jit(_solve_triangular))/triangular_solve | solution.py:19
  267.3 1.1 fusion.22
  268.4 11.7 %custom-call.8 = f32[1,128,128]{2,1,0:T(8,128)S(1)} custom-call(f32[1,128,128]{2,1,0:T(8,128)S(1)} %get-tuple-element.17), custom_call_target="Cholesky" | custom-call | tf_op jit(solution)/shard_map/jit(cholesky)/cholesky | solution.py:16
  280.8 0.7 fusion.20
  281.5 10.0 %custom-call.9 = f32[1,1,128,128]{2,3,1,0:T(8,128)S(1)} custom-call(f32[1,1,128,128]{3,2,1,0:T(8,128)S(1)} %fusion.20), custom_call_target="InvertDiagBlocksLowerTriangular" | custom-call | tf_op jit(solution)/shard_map/vmap(jit(_solve_triangular))/triangular_solve | solution.py:19
  291.4 1.1 fusion.24
  292.6 2.0 convolution_bitcast_fusion.1
  294.5 2.0 convolution_bitcast_fusion
  296.5 185.7 %all-reduce.8.cloned.1.call-done = (f32[2048,1,128]{0,2,1:T(8,128)}, f32[2048,1,128]{0,2,1:T(8,128)}) async-done(((f32[2048,1,128]{0,2,1:T(8,128)}, f32[2048,1,128]{0,2,1:T(8,128)}), (f32[2048,1,128]{0,2,1:T(8,128)}, f32[2048,1,128]{0,2,1:T(8,128)})) %all-reduce.8.cloned.1.call-update) | async-done | bytes 2097168 | tf_op jit(solution)/shard_map/psum | solution.py:31
  482.3 1.4 multiply_reduce_fusion
  483.6 3.5 fusion.7
  487.3 8.5 %all-reduce.2 = (f32[1,128]{1,0:T(1,128)S(1)}, f32[1,128]{1,0:T(1,128)S(1)}) all-reduce(f32[1,128]{1,0:T(1,128)S(1)} %bitcast.112, f32[1,128]{1,0:T(1,128)S(1)} %bitcast.113), channel_id=1, replica_groups=mesh['fsdp'=64,'tp'=4] {'tp'}, use_global_device_ids=true, to_apply=%region_11.14 | all-reduce | flops 256 | bytes 2048 | tf_op jit(solution)/shard_map/psum | solution.py:32
  496.0 1.0 copy-done.2
  497.7 2.1 fusion.5
  499.8 2.1 fusion.4
  502.0 2.2 fusion.6
  504.3 1.3 copy.11
  506.1 1.5 pad_maximum_fusion.1
  507.6 0.7 copy-done.8
  508.4 1.5 pad_maximum_fusion
  (33 shorter events, 2.5 us)
Async XLA Ops:
  7.2 3.0 copy-start
  7.2 53.9 %all-reduce.12.cloned.1.call-start = ((), (), s32[]{:S(2)}) async-start(), calls=%async_computation.2 | async-start | bytes 262144 | tf_op jit(solution)/shard_map/psum | solution.py:27
  10.2 282.4 %copy-start.3 = (bf16[2,128,2048]{2,1,0:T(8,128)(2,1)S(1)}, bf16[2,128,2048]{2,1,0:T(8,128)(2,1)}, u32[]{:S(2)}) copy-start(bf16[2,128,2048]{2,1,0:T(8,128)(2,1)} %param.8) | copy-start | bytes 3145732
  12.8 228.8 %all-reduce.10.cloned.1.call-start = ((), (), s32[]{:S(2)}) async-start(), calls=%async_computation.1 | async-start | bytes 262144 | tf_op jit(solution)/shard_map/psum | solution.py:28
  64.8 417.5 %all-reduce.8.cloned.1.call-start = ((), (), s32[]{:S(2)}) async-start(), calls=%async_computation | async-start | bytes 4194304 | tf_op jit(solution)/shard_map/psum | solution.py:31
  483.6 3.5 copy-start.1
  495.8 1.2 copy-start.2
  495.8 1.9 copy-start.9
  499.8 2.2 copy-start.4
  504.2 1.4 copy-start.5
  504.2 1.9 copy-start.6
  506.1 1.6 copy-start.7
  506.1 2.3 copy-start.8
Sparse Core Ops, SparseCore 0:
  12.9 48.1 all-reduce.11
  65.7 175.9 all-reduce.9
  296.7 185.5 all-reduce.7
where the time goes:
time: 519 us; the launch traced here: 516 us
  waiting for transfers between devices  411 us (79%)
  other arithmetic  51.7 us (10%)
  matrix products  25.4 us (5%)
  between operations  13.9 us (3%)
  blocking collectives  8.45 us (2%)
  local copies, waits for them, and re-layouts  6.03 us (1%)
    psum x1, waiting for transfers between devices, dion_block(): reduced = lax.psum(partial_terms, 'fsdp')  186 us
    psum x1, waiting for transfers between devices, dion_block(): lax.psum(jnp.einsum('kmr,kms->krs', panel, panel, precision=HIGH), 'fsdp')  177 us
    psum x1, waiting for transfers between devices, dion_block(): panel = lax.psum(panel_part, 'tp')  48.3 us
    another operation x6, other arithmetic, apply_factor(): factor_low = jnp.linalg.cholesky(gram)  24.8 us
    another operation x4, other arithmetic, solve_one(): jax.scipy.linalg.solve_triangular(factor_one, panel_one.T, lower=True)  21.1 us
  transfers between devices with their start and end apart: 3, of which 3 were waited for; matrix products, arithmetic and copies ran while one was open for 0% of the time, Pallas kernels for 0%

commit v1 on v0

v1 whole, which is shorter than its diff:
```python
import math

import jax
import jax.numpy as jnp
from jax import lax
from jax.experimental import pallas as pl
from jax.experimental.pallas import tpu as pltpu
from jax.sharding import PartitionSpec as P

D = 8192
R = 128
LAYERS = 2
ROWS = 128
COLS = 2048
PIECE = 256
BAND = 16
GRAM = 32
CHUNK = 2 * BAND + 8
BLOCK = 8

HIGHEST = lax.Precision.HIGHEST
F32 = jnp.float32
BF16 = jnp.bfloat16

VM = pl.BlockSpec(memory_space=pltpu.VMEM)
SM = pl.BlockSpec(memory_space=pltpu.SMEM)
ANY = pl.BlockSpec(memory_space=pl.ANY)
HBM = pl.BlockSpec(memory_space=pltpu.HBM)


def struct(*shape, dtype=F32):
    return jax.ShapeDtypeStruct(shape, dtype)


def call(kernel, outs, ins, args, flops=1 << 20, nbytes=1 << 20, scratch=(), out_specs=None, limit=16 << 20):
    return pl.pallas_call(
        kernel,
        out_shape=outs,
        in_specs=ins,
        out_specs=out_specs or jax.tree.map(lambda _: VM, outs),
        scratch_shapes=list(scratch),
        compiler_params=pltpu.CompilerParams(vmem_limit_bytes=limit),
        cost_estimate=pl.CostEstimate(flops=flops, bytes_accessed=nbytes, transcendentals=0),
    )(*args)


def split2(a):
    high = a.astype(BF16)
    return high, (a - high.astype(F32)).astype(BF16)


def split3(a):
    high = a.astype(BF16)
    rest = a - high.astype(F32)
    mid = rest.astype(BF16)
    return high, mid, (rest - mid.astype(F32)).astype(BF16)


def dot(a, b, dims):
    return lax.dot_general(a, b, (dims, ((), ())), preferred_element_type=F32)


def dot_x3(a, b, dims):
    ah, al = split2(a)
    bh, bl = split2(b)
    return dot(ah, bh, dims) + (dot(ah, bl, dims) + dot(al, bh, dims))


def panel_kernel(momentum, gradient, right, out, mom_v, grad_v, right_v, sems):
    pieces = 2
    width = COLS // pieces
    copies = []
    for layer in range(LAYERS):
        for piece in range(pieces):
            cut = slice(piece * width, (piece + 1) * width)
            slot = len(copies)
            group = [
                pltpu.make_async_copy(momentum.at[layer, :, cut], mom_v.at[layer, :, cut], sems.at[slot, 0]),
                pltpu.make_async_copy(gradient.at[layer, :, cut], grad_v.at[layer, :, cut], sems.at[slot, 1]),
                pltpu.make_async_copy(right.at[layer, cut, :], right_v.at[layer, cut, :], sems.at[slot, 2]),
            ]
            for item in group:
                item.start()
            copies.append(group)
    for layer in range(LAYERS):
        total = jnp.zeros((ROWS, R), F32)
        for piece in range(pieces):
            for item in copies[layer * pieces + piece]:
                item.wait()
            cut = slice(piece * width, (piece + 1) * width)
            buffer = mom_v[layer, :, cut] + grad_v[layer, :, cut].astype(F32)
            factor = right_v[layer, cut, :]
            high, low = split2(buffer)
            total += dot(high, factor, ((1,), (0,))) + dot(low, factor, ((1,), (0,)))
        out[layer] = total


def chunk_of(ids, core, rel):
    return core * 4 + lax.bitwise_xor(ids[1], rel)


def columns(ids, core, rel):
    return pl.ds(pl.multiple_of(chunk_of(ids, core, rel) * PIECE, PIECE), PIECE)


FIRST, SECOND = (1, 3), (3, 1)
NEAR, FAR = [(0, rel) for rel in SECOND], [(rel, 2) for rel in FIRST]


def gram_of(panel):
    return lax.dot_general(panel, panel, (((0,), (0,)), ((), ())), precision=HIGHEST, preferred_element_type=F32)


def product(ids, core, rels, panel, buffer, outs):
    for layer, out in enumerate(outs):
        left = wide_left(panel[layer].T)
        for slot, rel in enumerate(rels[layer]):
            out[slot * R : (slot + 1) * R] = wide_dot(left, buffer[layer, :, columns(ids, core, rel)])


def begin_kernel(ids, p0, p1, p2, p3, buffer, panel, packed, out0, out1):
    for layer, out in enumerate((out0, out1)):
        whole = (p0[layer] + p1[layer]) + (p2[layer] + p3[layer])
        panel[layer] = whole
        gram = gram_of(whole)
        packed[layer, :, 0:R] = gram[0 : R // 2]
        packed[layer, :, R:] = gram[R // 2 :]
        out[2 * R :] = packed[layer, pl.ds(pl.multiple_of((1 - ids[0]) * GRAM, GRAM), GRAM)]
    product(ids, 1 - ids[0], FAR, panel, buffer, (out0, out1))


def begin_own_kernel(ids, panel, packed, buffer, out0, out1):
    for layer, out in enumerate((out0, out1)):
        out[2 * R :] = packed[layer, pl.ds(pl.multiple_of(ids[0] * GRAM, GRAM), GRAM)]
    product(ids, ids[0], FAR, panel, buffer, (out0, out1))


def rest_kernel(flip, ids, panel, buffer, out0, out1):
    product(ids, 1 - ids[0] if flip else ids[0], NEAR, panel, buffer, (out0, out1))


def sum_x_kernel(a0, b0, a1, b1, out):
    for layer, (left, right) in enumerate(((a0, b0), (a1, b1))):
        total = left[...] + right[...]
        for z in range(8):
            out[z, layer * BAND : (layer + 1) * BAND] = total[z * BAND : (z + 1) * BAND]
            start = 2 * BAND + 4 * layer
            out[z, start : start + 4] = total[R + 4 * z : R + 4 * z + 4]


def sum_z_kernel(got, out):
    total = (got[0] + got[1]) + (got[2] + got[3]) + ((got[4] + got[5]) + (got[6] + got[7]))
    for z in range(8):
        out[z] = total


def spread_kernel(got, out0, out1, gram):
    for layer, out in enumerate((out0, out1)):
        for z in range(8):
            out[z * BAND : (z + 1) * BAND] = got[z, layer * BAND : (layer + 1) * BAND]
            start = 2 * BAND + 4 * layer
            gram[layer, 4 * z : 4 * z + 4] = got[z, start : start + 4]


def factor_first_kernel(ids, own, other, out, work):
    core = ids[0]
    for index, gram in ((core, own), (1 - core, other)):
        for half in range(2):
            rows = pl.ds(pl.multiple_of(index * GRAM + half * (R // 2), GRAM), GRAM)
            for layer in range(LAYERS):
                work[layer, rows, :] = gram[layer, :, half * R : (half + 1) * R]
    factor(work, out, 0, R // 2)


def factor_second_kernel(first, before, out, work):
    for layer in range(LAYERS):
        work[layer, R // 2 :] = before[layer, R // 2 :]
        out[layer, 0 : R // 2] = first[layer, 0 : R // 2]
    factor(work, out, R // 2, R)


def factor(work, out, begin, end):
    lane = lax.broadcasted_iota(jnp.int32, (1, R), 1)
    for base in range(begin, end, BLOCK):
        after = base + BLOCK
        inside = (lane >= base) & (lane < after)
        for layer in range(LAYERS):
            rows = [work[layer, base + i : base + i + 1, :] for i in range(BLOCK)]
            square = [
                [jnp.broadcast_to(rows[i][:, base + j : base + j + 1], (1, R)) for j in range(i + 1)] for i in range(BLOCK)
            ]
            rows = [jnp.where(inside, jnp.where(lane == base + i, 1.0, 0.0), rows[i]) for i in range(BLOCK)]
            for j in range(BLOCK):
                pivot = square[j][j]
                inverse = lax.rsqrt(pivot)
                rows[j] = rows[j] * inverse
                for i in range(j + 1, BLOCK):
                    square[i][j] = square[i][j] * inverse
                for i in range(j + 1, BLOCK):
                    for k in range(j + 1, i + 1):
                        square[i][k] = square[i][k] - square[i][j] * square[k][j]
                    rows[i] = rows[i] - square[i][j] * rows[j]
            done = jnp.concatenate(rows, axis=0)
            out[layer, base:after, :] = jnp.where(lane < after, done, 0.0)
            if after < R:
                high, mid, low = split3(done)
                left = jnp.concatenate([high, mid, high, mid, low, high], axis=0)
                right = jnp.concatenate([high, high, mid, mid, high, low], axis=0)
                change = dot(left, right, ((0,), (0,)))
                work[layer, after:, :] = jnp.where(inside, 0.0, work[layer, after:, :]) - change[after:, :]


def wide_left(a):
    high, low = split2(a)
    top = jnp.concatenate([high, high], axis=1)
    bottom = jnp.concatenate([low, jnp.zeros_like(low)], axis=1)
    return jnp.concatenate([top, bottom], axis=0)


def wide_dot(left, b):
    high, low = split2(b)
    both = dot(left, jnp.concatenate([high, low], axis=0), ((1,), (0,)))
    half = both.shape[0] // 2
    return both[0:half] + both[half:]


def pieces(ids, layer, rels):
    return [
        (2 * side + slot, columns(ids, core, rel))
        for side, core in enumerate((ids[0], 1 - ids[0]))
        for slot, rel in enumerate(rels[layer])
    ]


def reduce_layer(left, own, other, reduced, layer):
    total = jnp.zeros((R, R), F32)
    for side, source in enumerate((own, other)):
        for slot in range(2):
            part = wide_dot(left, source[slot * R : (slot + 1) * R])
            reduced[layer, 2 * side + slot] = part
            square = part * part
            total += square[:, 0:R] + square[:, R:]
    return total


def update_momentum(ids, layer, rels, basis, reduced, buffer, new_momentum, staged, sems):
    wide = wide_left(basis * 0.05)
    copies = []
    for slot, cut in pieces(ids, layer, rels):
        staged[layer, slot] = buffer[layer, :, cut] - wide_dot(wide, reduced[layer, slot])
        copies.append(
            pltpu.make_async_copy(staged.at[layer, slot], new_momentum.at[layer, :, cut], sems.at[layer, slot])
        )
        copies[-1].start()
    return copies


def near_kernel(ids, panel, inverse, a0, a1, b0, b1, buffer, left, reduced, total, new_momentum, staged, sems):
    copies = []
    for layer, (own, other) in enumerate(((a0, b0), (a1, b1))):
        total[layer] = reduce_layer(wide_left(inverse[layer]), own, other, reduced, layer)
        basis = lax.dot_general(
            panel[layer], inverse[layer], (((1,), (1,)), ((), ())), precision=HIGHEST, preferred_element_type=F32
        )
        left[layer] = basis
        copies += update_momentum(ids, layer, NEAR, basis, reduced, buffer, new_momentum, staged, sems)
    for item in copies:
        item.wait()


def far_kernel(inverse, a0, a1, b0, b1, before, reduced, squares):
    for layer, (own, other) in enumerate(((a0, b0), (a1, b1))):
        total = before[layer] + reduce_layer(wide_left(inverse[layer]), own, other, reduced, layer)
        squares[layer] = jnp.broadcast_to(jnp.sum(total.T, axis=0, keepdims=True), (8, R))


def momentum_kernel(ids, left, reduced, buffer, begun, new_momentum, staged, sems):
    del begun
    copies = []
    for layer in range(LAYERS):
        copies += update_momentum(ids, layer, FAR, left[layer], reduced, buffer, new_momentum, staged, sems)
    for item in copies:
        item.wait()


def turn_kernel(ids, near, far, out):
    for layer in range(LAYERS):
        for rels, source in ((NEAR, near), (FAR, far)):
            for slot, cut in pieces(ids, layer, rels):
                out[layer, cut, :] = source[layer, slot].T


def weight_kernel(
    ids, left, near, far, turned, s0, s1, weight, new_weight, new_basis, weight_v, basis_v, sems, basis_sems
):
    copies = []
    for layer in range(LAYERS):
        squares = s0[layer, 0:1, :] + s1[layer, 0:1, :]
        scale = lax.rsqrt(squares * (1.0 / D) + 1e-06)
        wide = wide_left(left[layer] * (scale * (0.05 * math.sqrt(D / R))))
        for rels, source in ((NEAR, near), (FAR, far)):
            for slot, cut in pieces(ids, layer, rels):
                index = len(copies) - layer
                change = wide_dot(wide, source[layer, slot])
                weight_v[index] = (1.0 - 0.05 * 0.1) * weight[layer, :, cut] - change
                copies.append(pltpu.make_async_copy(weight_v.at[index], new_weight.at[layer, :, cut], sems.at[index]))
                copies[-1].start()
        basis_v[layer] = (turned[layer] * scale).astype(BF16)
        copies.append(pltpu.make_async_copy(basis_v.at[layer], new_basis.at[layer], basis_sems.at[layer]))
        copies[-1].start()
    for item in copies:
        item.wait()


def place(z, x, core):
    return (z * 4 + x) * 2 + core


def move_core(a):
    return lax.ppermute(a, "fsdp", [(i, i ^ 1) for i in range(64)])


def move_x(a, flip):
    moves = [(place(z, x, c), place(z, x ^ flip, c)) for z in range(8) for x in range(4) for c in range(2)]
    return lax.ppermute(a, "fsdp", moves)


def swap_z(a):
    groups = [[place(z, x, c) for z in range(8)] for x in range(4) for c in range(2)]
    return lax.all_to_all(a, "fsdp", 0, 0, axis_index_groups=groups, tiled=True)


def move_tp(a, flip):
    return lax.ppermute(a, "tp", [(i, i ^ flip) for i in range(4)])


def body(weight, gradient, momentum, right_basis):
    index = lax.axis_index("fsdp")
    core = index % 2
    ids = jnp.stack([core, (index // 2) % 4]).astype(jnp.int32)

    with jax.named_scope("panel"):
        part = call(
            panel_kernel, struct(LAYERS, ROWS, R), [HBM] * 3, (momentum, gradient, right_basis), 300 << 20, 4 << 20,
            scratch=[
                pltpu.VMEM((LAYERS, ROWS, COLS), F32), pltpu.VMEM((LAYERS, ROWS, COLS), BF16),
                pltpu.VMEM((LAYERS, COLS, R), BF16), pltpu.SemaphoreType.DMA((4, 3)),
            ],
            limit=107 << 19,
        )
        parts = [move_tp(part, flip) for flip in (3, 2, 1)]
        buffer = momentum + gradient.astype(F32)
    with jax.named_scope("product"):
        long, short = struct(2 * R + GRAM, PIECE), struct(2 * R, PIECE)
        panel, packed, *begun = call(
            begin_kernel, (struct(LAYERS, ROWS, R), struct(LAYERS, R // 2, PIECE), long, long), [SM] + [VM] * 5,
            (ids, part, *parts, buffer), 300 << 20, 3 << 20,
        )
        begun_own = call(
            begin_own_kernel, (long, long), [SM] + [VM] * 3, (ids, panel, packed, buffer), 300 << 20, 2 << 20
        )
        sends = [own + move_core(other) for own, other in zip(begun_own, begun)]
        rest, rest_own = [
            call(
                lambda *refs, flip=flip: rest_kernel(flip, *refs), (short, short), [SM] + [VM] * 2,
                (ids, panel, buffer), 300 << 20, 2 << 20,
            )
            for flip in (True, False)
        ]
    with jax.named_scope("scatter"):
        pairs = []
        for layer in range(LAYERS):
            send = sends[layer]
            got = move_x(send, FIRST[layer])
            gram = send[2 * R :] + got[2 * R :]
            keep = rest_own[layer] + move_core(rest[layer]) + got[0 : 2 * R]
            pairs += [
                jnp.concatenate([keep[0:R], gram]),
                move_x(jnp.concatenate([keep[R:], gram]), SECOND[layer]),
            ]
        chunks = swap_z(call(sum_x_kernel, struct(8, CHUNK, PIECE), [VM] * 4, pairs))
    with jax.named_scope("gather"):
        chunks = swap_z(call(sum_z_kernel, struct(8, CHUNK, PIECE), [VM], (chunks,)))
        *mine, gram = call(
            spread_kernel, (struct(R, PIECE), struct(R, PIECE), struct(LAYERS, GRAM, PIECE)), [VM], (chunks,)
        )
        inverse, work = call(
            factor_first_kernel, (struct(LAYERS, R, R), struct(LAYERS, R, R)), [SM] + [VM] * 2,
            (ids, gram, move_core(gram)), 3 << 30,
        )
        near = [jnp.concatenate([own, move_x(own, flip)]) for own, flip in zip(mine, SECOND)]
        inverse, *near = lax.optimization_barrier((inverse, *near))
        far = [move_x(pair, flip) for pair, flip in zip(near, FIRST)]
        near_other = [move_core(item) for item in near]
        inverse = call(
            factor_second_kernel, struct(LAYERS, R, R), [VM] * 2, (inverse, work), 3 << 30,
            scratch=[pltpu.VMEM((LAYERS, R, R), F32)],
        )
        four = struct(LAYERS, 4, R, PIECE)
        moved = struct(LAYERS, ROWS, COLS)
        staging = [pltpu.VMEM((LAYERS, 4, ROWS, PIECE), F32), pltpu.SemaphoreType.DMA((LAYERS, 4))]
        left, near_reduced, total, new_momentum = call(
            near_kernel, (struct(LAYERS, ROWS, R), four, struct(LAYERS, R, R), moved), [SM] + [VM] * 7,
            (ids, panel, inverse, *near, *near_other, buffer), 2 << 30, 3 << 20,
            scratch=staging, out_specs=(VM, VM, VM, HBM),
        )
        total, *far = lax.optimization_barrier((total, *far))
        far_other = [move_core(item) for item in far]
    with jax.named_scope("update"):
        far_reduced, squares = call(
            far_kernel, (four, struct(LAYERS, 8, R)), [VM] * 6, (inverse, *far, *far_other, total), 1 << 30,
        )
        got = move_tp(squares, 1)
        new_momentum = pl.pallas_call(
            momentum_kernel,
            out_shape=moved,
            in_specs=[SM] + [VM] * 3 + [HBM],
            out_specs=HBM,
            scratch_shapes=staging,
            input_output_aliases={4: 0},
            compiler_params=pltpu.CompilerParams(vmem_limit_bytes=16 << 20),
            cost_estimate=pl.CostEstimate(flops=1 << 30, bytes_accessed=2 << 20, transcendentals=0),
        )(ids, left, far_reduced, buffer, new_momentum)
        new_momentum, squares, got = lax.optimization_barrier((new_momentum, squares, got))
        squares = squares + got
        got = move_tp(squares, 3)
        turned = call(
            turn_kernel, struct(LAYERS, COLS, R), [SM] + [VM] * 2, (ids, near_reduced, far_reduced), 1 << 30, 4 << 20
        )
        turned, squares, got = lax.optimization_barrier((turned, squares, got))
        new_weight, new_basis = call(
            weight_kernel, (moved, struct(LAYERS, COLS, R, dtype=BF16)), [SM] + [VM] * 7,
            (ids, left, near_reduced, far_reduced, turned, squares, got, weight), 800 << 20, 6 << 20,
            scratch=[
                pltpu.VMEM((16, ROWS, PIECE), F32), pltpu.VMEM((LAYERS, COLS, R), BF16),
                pltpu.SemaphoreType.DMA((16,)), pltpu.SemaphoreType.DMA((LAYERS,)),
            ],
            out_specs=(HBM,) * 2,
        )
    return (new_weight, new_momentum, new_basis)


def solution(mesh):
    return jax.shard_map(
        body,
        mesh=mesh,
        in_specs=(
            P(None, "fsdp", "tp"),
            P(None, "fsdp", "tp"),
            P(None, "fsdp", "tp"),
            P(None, "tp", None),
        ),
        out_specs=(P(None, "fsdp", "tp"), P(None, "fsdp", "tp"), P(None, "tp", None)),
        check_vma=False,
    )
```

time: 519 us -> 102 us (0.20)
  waiting for transfers between devices: 411 us -> 24.3 us
  other arithmetic: 51.7 us -> 0.61 us
  matrix products: 25.4 us -> 0 us
  starting transfers between devices: 0.12 us -> 22.7 us
  Pallas kernels: 0 us -> 22.2 us
  blocking collectives: 8.45 us -> 30.6 us
  between operations: 13.9 us -> 1.07 us
  local copies, waits for them, and re-layouts: 6.03 us -> 0.05 us
    psum x3 -> x0, waiting for transfers between devices: 411 us -> none  [the longest x1 186 us: dion_block(): reduced = lax.psum(partial_terms, 'fsdp')]
    another operation x10 -> x1, other arithmetic: 45.9 us -> 0.08 us  [body(): ids = jnp.stack([core, index // 2 % 4]).astype(jnp.int32)]
    all_to_all x0 -> x2, blocking collectives: none -> 30.6 us  [swap_z(): return lax.all_to_all(a, 'fsdp', 0, 0, axis_index_groups=groups, tiled=True)]
    ppermute x0 -> x22, waiting for transfers between devices: none -> 24.3 us  [the longest x8 11.3 us: move_x(): return lax.ppermute(a, 'fsdp', moves)]
    dot_general x10 -> x0, matrix products: 23.1 us -> none  [the longest x2 5.71 us: dion_block(): jnp.einsum('kmr,nkr->kmn', basis_left, reduced, precision=HIGH)]
    ppermute x0 -> x22, starting transfers between devices: none -> 22.7 us  [the longest x9 9.88 us: move_core(): return lax.ppermute(a, 'fsdp', [(i, i ^ 1) for i in range(64)])]
    pallas_call x0 -> x15, Pallas kernels: none -> 22.2 us  [the longest x14 20.4 us: call(): pl.pallas_call(kernel, out_shape=outs, in_specs=ins, out_specs=out_specs...]
    psum x1 -> x0, blocking collectives: 8.45 us -> none  [dion_block(): squares = lax.psum(jnp.sum(reduced * reduced, axis=0), 'tp')]
  transfers between devices with their start and end apart: 3 -> 22, of which waited for: 3 -> 15; matrix products, arithmetic and copies ran while one was open for 0% -> 0% of each run, Pallas kernels for 0% -> 15%
where the time goes in v1:
time: 102 us
  blocking collectives  30.6 us (30%)
  waiting for transfers between devices  24.3 us (24%)
  starting transfers between devices  22.7 us (22%)
  Pallas kernels  22.2 us (22%)
  between operations  1.07 us (1%)
    all_to_all x2, blocking collectives, swap_z(): return lax.all_to_all(a, 'fsdp', 0, 0, axis_index_groups=groups, tiled=True)  30.6 us
    pallas_call x14, Pallas kernels, call(): pl.pallas_call(kernel, out_shape=outs, in_specs=ins, out_specs=out_specs...  20.4 us
    ppermute x8, waiting for transfers between devices, move_x(): return lax.ppermute(a, 'fsdp', moves)  11.3 us
    ppermute x5, waiting for transfers between devices, move_tp(): return lax.ppermute(a, 'tp', [(i, i ^ flip) for i in range(4)])  10.8 us
    ppermute x9, starting transfers between devices, move_core(): return lax.ppermute(a, 'fsdp', [(i, i ^ 1) for i in range(64)])  9.88 us
    ppermute x8, starting transfers between devices, move_x(): return lax.ppermute(a, 'fsdp', moves)  7.58 us
    ppermute x5, starting transfers between devices, move_tp(): return lax.ppermute(a, 'tp', [(i, i ^ flip) for i in range(4)])  5.24 us
    ppermute x9, waiting for transfers between devices, move_core(): return lax.ppermute(a, 'fsdp', [(i, i ^ 1) for i in range(64)])  2.31 us
  transfers between devices with their start and end apart: 22, of which 15 were waited for; matrix products, arithmetic and copies ran while one was open for 0% of the time, Pallas kernels for 15%

profile of v1, /device:TPU:1, one launch (start us, length us, event | category | flops | bytes accessed | tf_op | source)
XLA Modules:
  0.0 101.5 jit_solution(9599267135839863401)
XLA Ops:
  0.7 2.7 %panel.1.p0 = f32[2,128,128]{2,1,0:T(8,128)S(1)} custom-call(f32[2,128,2048]{2,1,0:T(8,128)} %momentum.1, bf16[2,128,2048]{2,1,0:T(8,128)(2,1)} %gradient.1, bf16[2,2048,128]{2,1,0:T(8,128)(2,1)} %right.1), custom_call_target="tpu_custom_call" | custom-call | flops 314572800 | bytes 4194304 | tf_op jit(solution)/shard_map/panel/pallas_call | solution.py:36
  3.4 2.2 %collective-permute-start.2 = (f32[2,128,128]{2,1,0:T(8,128)S(1)}, f32[2,128,128]{2,1,0:T(8,128)S(1)}, u32[]{:S(2)}, u32[]{:S(2)}) collective-permute-start(f32[2,128,128]{2,1,0:T(8,128)S(1)} %panel.1.p0), channel_id=1, source_target_pairs={{0,1},{1,0},{2,3},{3,2},{4,5},{5,4},{6,7},{7,6},{8,9},{9,8},{10,11... | collective-permute-start | bytes 393224 | tf_op jit(solution)/shard_map/panel/ppermute | solution.py:334
  5.6 2.6 %collective-permute-start.1 = (f32[2,128,128]{2,1,0:T(8,128)S(1)}, f32[2,128,128]{2,1,0:T(8,128)S(1)}, u32[]{:S(2)}, u32[]{:S(2)}) collective-permute-start(f32[2,128,128]{2,1,0:T(8,128)S(1)} %panel.1.p0), channel_id=1, source_target_pairs={{0,2},{1,3},{2,0},{3,1},{4,6},{5,7},{6,4},{7,5},{8,10},{9,11},{10,... | collective-permute-start | bytes 393224 | tf_op jit(solution)/shard_map/panel/ppermute | solution.py:334
  8.6 5.3 %collective-permute-done.1.p2 = f32[2,128,128]{2,1,0:T(8,128)S(1)} collective-permute-done((f32[2,128,128]{2,1,0:T(8,128)S(1)}, f32[2,128,128]{2,1,0:T(8,128)S(1)}, u32[]{:S(2)}, u32[]{:S(2)}) %collective-permute-start.1) | collective-permute-done | bytes 131104 | tf_op jit(solution)/shard_map/panel/ppermute | solution.py:334
  13.9 2.5 %collective-permute-done.p1 = f32[2,128,128]{2,1,0:T(8,128)S(1)} collective-permute-done((f32[2,128,128]{2,1,0:T(8,128)S(1)}, f32[2,128,128]{2,1,0:T(8,128)S(1)}, u32[]{:S(2)}, u32[]{:S(2)}) %collective-permute-start) | collective-permute-done | bytes 131104 | tf_op jit(solution)/shard_map/panel/ppermute | solution.py:334
  16.4 1.0 %product.4 = (f32[2,128,128]{2,1,0:T(8,128)S(1)}, f32[2,64,256]{2,1,0:T(8,128)S(1)}, f32[288,256]{1,0:T(8,128)S(1)}, f32[288,256]{1,0:T(8,128)S(1)}) custom-call(s32[2]{0:T(128)S(1)} %pad_add_fusion.ids.refs_0_, f32[2,128,128]{2,1,0:T(8,128)S(1)} %panel.1.p0, f32[2,128,128]{2,1,0:T(8,128)S(1)} %collective-permute-done.p1, ...), custom_call_target="tpu_custom_call" | custom-call | flops 314572800 | bytes 3145728 | tf_op jit(solution)/shard_map/product/pallas_call | solution.py:36
  17.4 1.3 %collective-permute-start.8 = (f32[288,256]{1,0:T(8,128)S(1)}, f32[288,256]{1,0:T(8,128)S(1)}, u32[]{:S(2)}, u32[]{:S(2)}) collective-permute-start(f32[288,256]{1,0:T(8,128)S(1)} %get-tuple-element.47), channel_id=1, source_target_pairs={{0,4},{4,0},{8,12},{12,8},{16,20},{20,16},{24,28},{28,24},{32,36},... | collective-permute-start | bytes 884744 | tf_op jit(solution)/shard_map/product/ppermute | solution.py:320
  18.8 0.9 product.7
  20.0 2.6 %collective-permute-start.9 = (f32[288,256]{1,0:T(8,128)S(1)}, f32[288,256]{1,0:T(8,128)S(1)}, u32[]{:S(2)}, u32[]{:S(2)}) collective-permute-start(f32[288,256]{1,0:T(8,128)S(1)} %add.46), channel_id=1, source_target_pairs={{0,24},{4,28},{8,16},{12,20},{16,8},{20,12},{24,0},{28,4},{32,56},... | collective-permute-start | bytes 884744 | tf_op jit(solution)/shard_map/scatter/ppermute | solution.py:325
  22.7 0.9 product.6
  23.6 1.0 collective-permute-start.3
  26.1 3.4 %collective-permute-done.9 = f32[288,256]{1,0:T(8,128)S(1)} collective-permute-done((f32[288,256]{1,0:T(8,128)S(1)}, f32[288,256]{1,0:T(8,128)S(1)}, u32[]{:S(2)}, u32[]{:S(2)}) %collective-permute-start.9) | collective-permute-done | bytes 294944 | tf_op jit(solution)/shard_map/scatter/ppermute | solution.py:325
  29.5 1.1 %collective-permute-done.5 = f32[288,256]{1,0:T(8,128)S(1)} collective-permute-done((f32[288,256]{1,0:T(8,128)S(1)}, f32[288,256]{1,0:T(8,128)S(1)}, u32[]{:S(2)}, u32[]{:S(2)}) %collective-permute-start.5) | collective-permute-done | bytes 294944 | tf_op jit(solution)/shard_map/scatter/ppermute | solution.py:325
  31.0 1.4 %collective-permute-start.6 = (f32[160,256]{1,0:T(8,128)S(1)}, f32[160,256]{1,0:T(8,128)S(1)}, u32[]{:S(2)}, u32[]{:S(2)}) collective-permute-start(f32[160,256]{1,0:T(8,128)S(1)} %get-tuple-element.79), channel_id=1, source_target_pairs={{0,24},{4,28},{8,16},{12,20},{16,8},{20,12},{24,0},{28,4},{32,56},... | collective-permute-start | bytes 491528 | tf_op jit(solution)/shard_map/scatter/ppermute | solution.py:325
  32.4 2.6 %collective-permute-done.10.b1 = f32[160,256]{1,0:T(8,128)S(1)} collective-permute-done((f32[160,256]{1,0:T(8,128)S(1)}, f32[160,256]{1,0:T(8,128)S(1)}, u32[]{:S(2)}, u32[]{:S(2)}) %collective-permute-start.10) | collective-permute-done | bytes 163872 | tf_op jit(solution)/shard_map/scatter/ppermute | solution.py:325
  35.0 1.4 %collective-permute-done.6.b0 = f32[160,256]{1,0:T(8,128)S(1)} collective-permute-done((f32[160,256]{1,0:T(8,128)S(1)}, f32[160,256]{1,0:T(8,128)S(1)}, u32[]{:S(2)}, u32[]{:S(2)}) %collective-permute-start.6) | collective-permute-done | bytes 163872 | tf_op jit(solution)/shard_map/scatter/ppermute | solution.py:325
  36.5 18.0 %all_to_all.10.got = f32[8,40,256]{2,1,0:T(8,128)S(1)} all-to-all(f32[8,40,256]{2,1,0:T(8,128)S(1)} %scatter.1), channel_id=1, replica_groups={{0,32,64,96,128,160,192,224},{4,36,68,100,132,164,196,228},{8,40,72,104..., dimensions={0} | all-to-all | bytes 655360 | tf_op jit(solution)/shard_map/scatter/all_to_all | solution.py:330
  54.6 12.5 %all_to_all.11.got = f32[8,40,256]{2,1,0:T(8,128)S(1)} all-to-all(f32[8,40,256]{2,1,0:T(8,128)S(1)} %gather.5), channel_id=1, replica_groups={{0,32,64,96,128,160,192,224},{4,36,68,100,132,164,196,228},{8,40,72,104..., dimensions={0} | all-to-all | bytes 655360 | tf_op jit(solution)/shard_map/gather/all_to_all | solution.py:330
  67.1 5.4 %collective-permute-start.11 = (f32[2,32,256]{2,1,0:T(8,128)S(1)}, f32[2,32,256]{2,1,0:T(8,128)S(1)}, u32[]{:S(2)}, u32[]{:S(2)}) collective-permute-start(f32[2,32,256]{2,1,0:T(8,128)S(1)} %get-tuple-element.48.own), channel_id=1, source_target_pairs={{0,4},{4,0},{8,12},{12,8},{16,20},{20,16},{24,28},{28,24},{32,36},... | collective-permute-start | bytes 196616 | tf_op jit(solution)/shard_map/gather/ppermute | solution.py:320
  72.5 1.6 %collective-permute-start.12 = (f32[128,256]{1,0:T(8,128)S(1)}, f32[128,256]{1,0:T(8,128)S(1)}, u32[]{:S(2)}, u32[]{:S(2)}) collective-permute-start(f32[128,256]{1,0:T(8,128)S(1)} %get-tuple-element.50), channel_id=1, source_target_pairs={{0,24},{4,28},{8,16},{12,20},{16,8},{20,12},{24,0},{28,4},{32,56},... | collective-permute-start | bytes 393224 | tf_op jit(solution)/shard_map/gather/ppermute | solution.py:325
  74.1 3.8 %gather.7 = (f32[2,128,128]{2,1,0:T(8,128)S(1)}, f32[2,128,128]{2,1,0:T(8,128)S(1)}) custom-call(s32[2]{0:T(128)S(1)} %pad_add_fusion.ids.refs_0_, f32[2,32,256]{2,1,0:T(8,128)S(1)} %get-tuple-element.48.own, f32[2,32,256]{2,1,0:T(8,128)S(1)} %collective-permute-done.11.other), custom_call_target="tpu_custom_call" | custom-call | flops 3221225472 | bytes 1048576 | tf_op jit(solution)/shard_map/gather/pallas_call | solution.py:36
  77.9 0.9 collective-permute-done.12
  79.5 0.9 collective-permute-start.14
  80.4 1.1 %collective-permute-start.17 = (f32[256,256]{1,0:T(8,128)S(1)}, f32[256,256]{1,0:T(8,128)S(1)}, u32[]{:S(2)}, u32[]{:S(2)}) collective-permute-start(f32[256,256]{1,0:T(8,128)S(1)} %pad_maximum_fusion.1.a1), channel_id=1, source_target_pairs={{0,24},{4,28},{8,16},{12,20},{16,8},{20,12},{24,0},{28,4},{32,56},... | collective-permute-start | bytes 786440 | tf_op jit(solution)/shard_map/gather/ppermute | solution.py:325
  81.9 3.1 %gather.8.inverse = f32[2,128,128]{2,1,0:T(8,128)S(1)} custom-call(f32[2,128,128]{2,1,0:T(8,128)S(1)} %get-tuple-element.52.first, f32[2,128,128]{2,1,0:T(8,128)S(1)} %get-tuple-element.53.before), custom_call_target="tpu_custom_call" | custom-call | flops 3221225472 | bytes 1048576 | tf_op jit(solution)/shard_map/gather/pallas_call | solution.py:36
  85.0 2.8 %gather.9 = (f32[2,128,128]{2,1,0:T(8,128)S(1)}, f32[2,4,128,256]{3,2,1,0:T(8,128)S(1)}, f32[2,128,128]{2,1,0:T(8,128)S(1)}, f32[2,128,2048]{2,1,0:T(8,128)}) custom-call(s32[2]{0:T(128)S(1)} %pad_add_fusion.ids.refs_0_, f32[2,128,128]{2,1,0:T(8,128)S(1)} %get-tuple-element.38.refs_1_.panel, f32[2,128,128]{2,1,0:T(8,128)S(1)} %gather.8.inverse, ...), custom_call_target="tpu_custom_call" | custom-call | flops 2147483648 | bytes 3145728 | tf_op jit(solution)/shard_map/gather/pallas_call | solution.py:36
  87.8 1.8 %collective-permute-done.17.a1 = f32[256,256]{1,0:T(8,128)S(1)} collective-permute-done((f32[256,256]{1,0:T(8,128)S(1)}, f32[256,256]{1,0:T(8,128)S(1)}, u32[]{:S(2)}, u32[]{:S(2)}) %collective-permute-start.17) | collective-permute-done | bytes 262176 | tf_op jit(solution)/shard_map/gather/ppermute | solution.py:325
  90.4 1.2 %collective-permute-done.18.b0 = f32[256,256]{1,0:T(8,128)S(1)} collective-permute-done((f32[256,256]{1,0:T(8,128)S(1)}, f32[256,256]{1,0:T(8,128)S(1)}, u32[]{:S(2)}, u32[]{:S(2)}) %collective-permute-start.18) | collective-permute-done | bytes 262176 | tf_op jit(solution)/shard_map/gather/ppermute | solution.py:320
  92.5 1.8 %update.6 = f32[2,128,2048]{2,1,0:T(8,128)} custom-call(s32[2]{0:T(128)S(1)} %pad_add_fusion.ids.refs_0_, f32[2,128,128]{2,1,0:T(8,128)S(1)} %get-tuple-element.56.left, f32[2,4,128,256]{3,2,1,0:T(8,128)S(1)} %get-tuple-element.62.far.reduced, f32[2,128,2048]{2,1,0:T(8,128)S(1)} %convert_add_fusion.buffer.refs_2_, ...), custom_call_target="tpu_custom_call", output_to_operand_aliasing={{}: (4, {})} | custom-call | flops 1073741824 | bytes 2097152 | tf_op jit(solution)/shard_map/update/pallas_call | solution.py:414
  95.3 1.1 %update.5.turned = f32[2,2048,128]{2,1,0:T(8,128)S(1)} custom-call(s32[2]{0:T(128)S(1)} %pad_add_fusion.ids.refs_0_, f32[2,4,128,256]{3,2,1,0:T(8,128)S(1)} %get-tuple-element.57.near, f32[2,4,128,256]{3,2,1,0:T(8,128)S(1)} %get-tuple-element.62.far.reduced), custom_call_target="tpu_custom_call" | custom-call | flops 1073741824 | bytes 4194304 | tf_op jit(solution)/shard_map/update/pallas_call | solution.py:36
  96.5 2.3 %collective-permute-done.21.s1 = f32[2,8,128]{2,1,0:T(8,128)S(1)} collective-permute-done((f32[2,8,128]{2,1,0:T(8,128)S(1)}, f32[2,8,128]{2,1,0:T(8,128)S(1)}, u32[]{:S(2)}, u32[]{:S(2)}) %collective-permute-start.21) | collective-permute-done | bytes 8224 | tf_op jit(solution)/shard_map/update/ppermute | solution.py:334
  98.7 2.6 %update.7 = (f32[2,128,2048]{2,1,0:T(8,128)}, bf16[2,2048,128]{2,1,0:T(8,128)(2,1)}) custom-call(s32[2]{0:T(128)S(1)} %pad_add_fusion.ids.refs_0_, f32[2,128,128]{2,1,0:T(8,128)S(1)} %get-tuple-element.56.left, f32[2,4,128,256]{3,2,1,0:T(8,128)S(1)} %get-tuple-element.57.near, f32[2,4,128,256]{3,2,1,0:T(8,128)S(1)} %get-tuple-element.62.far.reduced, ...), custom_call_target="tpu_custom_call" | custom-call | flops 838860800 | bytes 6291456 | tf_op jit(solution)/shard_map/update/pallas_call | solution.py:36
  (49 shorter events, 6.5 us)
Async XLA Ops:
  0.6 7.6 %copy-start.1 = (f32[2,128,2048]{2,1,0:T(8,128)S(1)}, f32[2,128,2048]{2,1,0:T(8,128)}, u32[]{:S(2)}) copy-start(f32[2,128,2048]{2,1,0:T(8,128)} %momentum.1) | copy-start | bytes 6291460
  0.6 7.6 %copy-start.2 = (bf16[2,128,2048]{2,1,0:T(8,128)(2,1)S(1)}, bf16[2,128,2048]{2,1,0:T(8,128)(2,1)}, u32[]{:S(2)}) copy-start(bf16[2,128,2048]{2,1,0:T(8,128)(2,1)} %gradient.1) | copy-start | bytes 3145732
  3.4 5.2 %collective-permute-start.2 = (f32[2,128,128]{2,1,0:T(8,128)S(1)}, f32[2,128,128]{2,1,0:T(8,128)S(1)}, u32[]{:S(2)}, u32[]{:S(2)}) collective-permute-start(f32[2,128,128]{2,1,0:T(8,128)S(1)} %panel.1.p0), channel_id=1, source_target_pairs={{0,1},{1,0},{2,3},{3,2},{4,5},{5,4},{6,7},{7,6},{8,9},{9,8},{10,11... | collective-permute-start | bytes 393224 | tf_op jit(solution)/shard_map/panel/ppermute | solution.py:334
  5.6 8.3 %collective-permute-start.1 = (f32[2,128,128]{2,1,0:T(8,128)S(1)}, f32[2,128,128]{2,1,0:T(8,128)S(1)}, u32[]{:S(2)}, u32[]{:S(2)}) collective-permute-start(f32[2,128,128]{2,1,0:T(8,128)S(1)} %panel.1.p0), channel_id=1, source_target_pairs={{0,2},{1,3},{2,0},{3,1},{4,6},{5,7},{6,4},{7,5},{8,10},{9,11},{10,... | collective-permute-start | bytes 393224 | tf_op jit(solution)/shard_map/panel/ppermute | solution.py:334
  8.2 8.2 %collective-permute-start = (f32[2,128,128]{2,1,0:T(8,128)S(1)}, f32[2,128,128]{2,1,0:T(8,128)S(1)}, u32[]{:S(2)}, u32[]{:S(2)}) collective-permute-start(f32[2,128,128]{2,1,0:T(8,128)S(1)} %panel.1.p0), channel_id=1, source_target_pairs={{0,3},{1,2},{2,1},{3,0},{4,7},{5,6},{6,5},{7,4},{8,11},{9,10},{10,... | collective-permute-start | bytes 393224 | tf_op jit(solution)/shard_map/panel/ppermute | solution.py:334
  17.4 2.5 %collective-permute-start.8 = (f32[288,256]{1,0:T(8,128)S(1)}, f32[288,256]{1,0:T(8,128)S(1)}, u32[]{:S(2)}, u32[]{:S(2)}) collective-permute-start(f32[288,256]{1,0:T(8,128)S(1)} %get-tuple-element.47), channel_id=1, source_target_pairs={{0,4},{4,0},{8,12},{12,8},{16,20},{20,16},{24,28},{28,24},{32,36},... | collective-permute-start | bytes 884744 | tf_op jit(solution)/shard_map/product/ppermute | solution.py:320
  18.7 3.8 %collective-permute-start.4 = (f32[288,256]{1,0:T(8,128)S(1)}, f32[288,256]{1,0:T(8,128)S(1)}, u32[]{:S(2)}, u32[]{:S(2)}) collective-permute-start(f32[288,256]{1,0:T(8,128)S(1)} %get-tuple-element.43), channel_id=1, source_target_pairs={{0,4},{4,0},{8,12},{12,8},{16,20},{20,16},{24,28},{28,24},{32,36},... | collective-permute-start | bytes 884744 | tf_op jit(solution)/shard_map/product/ppermute | solution.py:320
  20.0 9.5 %collective-permute-start.9 = (f32[288,256]{1,0:T(8,128)S(1)}, f32[288,256]{1,0:T(8,128)S(1)}, u32[]{:S(2)}, u32[]{:S(2)}) collective-permute-start(f32[288,256]{1,0:T(8,128)S(1)} %add.46), channel_id=1, source_target_pairs={{0,24},{4,28},{8,16},{12,20},{16,8},{20,12},{24,0},{28,4},{32,56},... | collective-permute-start | bytes 884744 | tf_op jit(solution)/shard_map/scatter/ppermute | solution.py:325
  22.6 8.0 %collective-permute-start.5 = (f32[288,256]{1,0:T(8,128)S(1)}, f32[288,256]{1,0:T(8,128)S(1)}, u32[]{:S(2)}, u32[]{:S(2)}) collective-permute-start(f32[288,256]{1,0:T(8,128)S(1)} %add.42), channel_id=1, source_target_pairs={{0,8},{4,12},{8,0},{12,4},{16,24},{20,28},{24,16},{28,20},{32,40},... | collective-permute-start | bytes 884744 | tf_op jit(solution)/shard_map/scatter/ppermute | solution.py:325
  23.6 2.1 %collective-permute-start.3 = (f32[256,256]{1,0:T(8,128)S(1)}, f32[256,256]{1,0:T(8,128)S(1)}, u32[]{:S(2)}, u32[]{:S(2)}) collective-permute-start(f32[256,256]{1,0:T(8,128)S(1)} %get-tuple-element.40), channel_id=1, source_target_pairs={{0,4},{4,0},{8,12},{12,8},{16,20},{20,16},{24,28},{28,24},{32,36},... | collective-permute-start | bytes 786440 | tf_op jit(solution)/shard_map/scatter/ppermute | solution.py:320
  24.5 1.5 %collective-permute-start.7 = (f32[256,256]{1,0:T(8,128)S(1)}, f32[256,256]{1,0:T(8,128)S(1)}, u32[]{:S(2)}, u32[]{:S(2)}) collective-permute-start(f32[256,256]{1,0:T(8,128)S(1)} %get-tuple-element.45), channel_id=1, source_target_pairs={{0,4},{4,0},{8,12},{12,8},{16,20},{20,16},{24,28},{28,24},{32,36},... | collective-permute-start | bytes 786440 | tf_op jit(solution)/shard_map/scatter/ppermute | solution.py:320
  30.8 4.3 %collective-permute-start.10 = (f32[160,256]{1,0:T(8,128)S(1)}, f32[160,256]{1,0:T(8,128)S(1)}, u32[]{:S(2)}, u32[]{:S(2)}) collective-permute-start(f32[160,256]{1,0:T(8,128)S(1)} %get-tuple-element.77), channel_id=1, source_target_pairs={{0,8},{4,12},{8,0},{12,4},{16,24},{20,28},{24,16},{28,20},{32,40},... | collective-permute-start | bytes 491528 | tf_op jit(solution)/shard_map/scatter/ppermute | solution.py:325
  31.0 5.5 %collective-permute-start.6 = (f32[160,256]{1,0:T(8,128)S(1)}, f32[160,256]{1,0:T(8,128)S(1)}, u32[]{:S(2)}, u32[]{:S(2)}) collective-permute-start(f32[160,256]{1,0:T(8,128)S(1)} %get-tuple-element.79), channel_id=1, source_target_pairs={{0,24},{4,28},{8,16},{12,20},{16,8},{20,12},{24,0},{28,4},{32,56},... | collective-permute-start | bytes 491528 | tf_op jit(solution)/shard_map/scatter/ppermute | solution.py:325
  67.1 7.0 %collective-permute-start.11 = (f32[2,32,256]{2,1,0:T(8,128)S(1)}, f32[2,32,256]{2,1,0:T(8,128)S(1)}, u32[]{:S(2)}, u32[]{:S(2)}) collective-permute-start(f32[2,32,256]{2,1,0:T(8,128)S(1)} %get-tuple-element.48.own), channel_id=1, source_target_pairs={{0,4},{4,0},{8,12},{12,8},{16,20},{20,16},{24,28},{28,24},{32,36},... | collective-permute-start | bytes 196616 | tf_op jit(solution)/shard_map/gather/ppermute | solution.py:320
  72.5 6.3 %collective-permute-start.12 = (f32[128,256]{1,0:T(8,128)S(1)}, f32[128,256]{1,0:T(8,128)S(1)}, u32[]{:S(2)}, u32[]{:S(2)}) collective-permute-start(f32[128,256]{1,0:T(8,128)S(1)} %get-tuple-element.50), channel_id=1, source_target_pairs={{0,24},{4,28},{8,16},{12,20},{16,8},{20,12},{24,0},{28,4},{32,56},... | collective-permute-start | bytes 393224 | tf_op jit(solution)/shard_map/gather/ppermute | solution.py:325
  74.1 4.7 %collective-permute-start.13 = (f32[128,256]{1,0:T(8,128)S(1)}, f32[128,256]{1,0:T(8,128)S(1)}, u32[]{:S(2)}, u32[]{:S(2)}) collective-permute-start(f32[128,256]{1,0:T(8,128)S(1)} %get-tuple-element.51), channel_id=1, source_target_pairs={{0,8},{4,12},{8,0},{12,4},{16,24},{20,28},{24,16},{28,20},{32,40},... | collective-permute-start | bytes 393224 | tf_op jit(solution)/shard_map/gather/ppermute | solution.py:325
  78.9 8.9 %collective-permute-start.16 = (f32[256,256]{1,0:T(8,128)S(1)}, f32[256,256]{1,0:T(8,128)S(1)}, u32[]{:S(2)}, u32[]{:S(2)}) collective-permute-start(f32[256,256]{1,0:T(8,128)S(1)} %pad_maximum_fusion.a0), channel_id=1, source_target_pairs={{0,8},{4,12},{8,0},{12,4},{16,24},{20,28},{24,16},{28,20},{32,40},... | collective-permute-start | bytes 786440 | tf_op jit(solution)/shard_map/gather/ppermute | solution.py:325
  79.5 5.4 %collective-permute-start.14 = (f32[256,256]{1,0:T(8,128)S(1)}, f32[256,256]{1,0:T(8,128)S(1)}, u32[]{:S(2)}, u32[]{:S(2)}) collective-permute-start(f32[256,256]{1,0:T(8,128)S(1)} %pad_maximum_fusion.a0), channel_id=1, source_target_pairs={{0,4},{4,0},{8,12},{12,8},{16,20},{20,16},{24,28},{28,24},{32,36},... | collective-permute-start | bytes 786440 | tf_op jit(solution)/shard_map/gather/ppermute | solution.py:320
  80.4 9.1 %collective-permute-start.17 = (f32[256,256]{1,0:T(8,128)S(1)}, f32[256,256]{1,0:T(8,128)S(1)}, u32[]{:S(2)}, u32[]{:S(2)}) collective-permute-start(f32[256,256]{1,0:T(8,128)S(1)} %pad_maximum_fusion.1.a1), channel_id=1, source_target_pairs={{0,24},{4,28},{8,16},{12,20},{16,8},{20,12},{24,0},{28,4},{32,56},... | collective-permute-start | bytes 786440 | tf_op jit(solution)/shard_map/gather/ppermute | solution.py:325
  81.6 3.4 %collective-permute-start.15 = (f32[256,256]{1,0:T(8,128)S(1)}, f32[256,256]{1,0:T(8,128)S(1)}, u32[]{:S(2)}, u32[]{:S(2)}) collective-permute-start(f32[256,256]{1,0:T(8,128)S(1)} %pad_maximum_fusion.1.a1), channel_id=1, source_target_pairs={{0,4},{4,0},{8,12},{12,8},{16,20},{20,16},{24,28},{28,24},{32,36},... | collective-permute-start | bytes 786440 | tf_op jit(solution)/shard_map/gather/ppermute | solution.py:320
  89.6 1.9 %collective-permute-start.18 = (f32[256,256]{1,0:T(8,128)S(1)}, f32[256,256]{1,0:T(8,128)S(1)}, u32[]{:S(2)}, u32[]{:S(2)}) collective-permute-start(f32[256,256]{1,0:T(8,128)S(1)} %collective-permute-done.16.a0), channel_id=1, source_target_pairs={{0,4},{4,0},{8,12},{12,8},{16,20},{20,16},{24,28},{28,24},{32,36},... | collective-permute-start | bytes 786440 | tf_op jit(solution)/shard_map/gather/ppermute | solution.py:320
  90.4 1.5 %collective-permute-start.19 = (f32[256,256]{1,0:T(8,128)S(1)}, f32[256,256]{1,0:T(8,128)S(1)}, u32[]{:S(2)}, u32[]{:S(2)}) collective-permute-start(f32[256,256]{1,0:T(8,128)S(1)} %collective-permute-done.17.a1), channel_id=1, source_target_pairs={{0,4},{4,0},{8,12},{12,8},{16,20},{20,16},{24,28},{28,24},{32,36},... | collective-permute-start | bytes 786440 | tf_op jit(solution)/shard_map/gather/ppermute | solution.py:320
  92.4 2.6 %collective-permute-start.20 = (f32[2,8,128]{2,1,0:T(8,128)S(1)}, f32[2,8,128]{2,1,0:T(8,128)S(1)}, u32[]{:S(2)}, u32[]{:S(2)}) collective-permute-start(f32[2,8,128]{2,1,0:T(8,128)S(1)} %get-tuple-element.65), channel_id=1, source_target_pairs={{0,1},{1,0},{2,3},{3,2},{4,5},{5,4},{6,7},{7,6},{8,9},{9,8},{10,11... | collective-permute-start | bytes 24584 | tf_op jit(solution)/shard_map/update/ppermute | solution.py:334
  95.0 3.7 %collective-permute-start.21 = (f32[2,8,128]{2,1,0:T(8,128)S(1)}, f32[2,8,128]{2,1,0:T(8,128)S(1)}, u32[]{:S(2)}, u32[]{:S(2)}) collective-permute-start(f32[2,8,128]{2,1,0:T(8,128)S(1)} %add.49.s0), channel_id=1, source_target_pairs={{0,3},{1,2},{2,1},{3,0},{4,7},{5,6},{6,5},{7,4},{8,11},{9,10},{10,... | collective-permute-start | bytes 24584 | tf_op jit(solution)/shard_map/update/ppermute | solution.py:334
  95.3 3.4 %copy-start = (f32[2,128,2048]{2,1,0:T(8,128)S(1)}, f32[2,128,2048]{2,1,0:T(8,128)}, u32[]{:S(2)}) copy-start(f32[2,128,2048]{2,1,0:T(8,128)} %weight.1) | copy-start | bytes 6291460

commit v2 on v1

v2 whole, which is shorter than its diff:
```python
import math

import jax
import jax.numpy as jnp
from jax import lax
from jax.experimental import pallas as pl
from jax.experimental.pallas import tpu as pltpu
from jax.sharding import PartitionSpec as P

D = 8192
R = 128
LAYERS = 2
ROWS = 128
COLS = 2048
PIECE = 256
BAND = 16
GRAM = 32
CHUNK = 2 * BAND + 8
BLOCK = 8

HIGHEST = lax.Precision.HIGHEST
F32 = jnp.float32
BF16 = jnp.bfloat16

VM = pl.BlockSpec(memory_space=pltpu.VMEM)
SM = pl.BlockSpec(memory_space=pltpu.SMEM)
ANY = pl.BlockSpec(memory_space=pl.ANY)
HBM = pl.BlockSpec(memory_space=pltpu.HBM)


def struct(*shape, dtype=F32):
    return jax.ShapeDtypeStruct(shape, dtype)


def call(kernel, outs, ins, args, flops=1 << 20, nbytes=1 << 20, scratch=(), out_specs=None, limit=16 << 20, aliases=None):
    return pl.pallas_call(
        kernel,
        out_shape=outs,
        in_specs=ins,
        out_specs=out_specs or jax.tree.map(lambda _: VM, outs),
        scratch_shapes=list(scratch),
        input_output_aliases=aliases or {},
        compiler_params=pltpu.CompilerParams(vmem_limit_bytes=limit),
        cost_estimate=pl.CostEstimate(flops=flops, bytes_accessed=nbytes, transcendentals=0),
    )(*args)


def split2(a):
    high = a.astype(BF16)
    return high, (a - high.astype(F32)).astype(BF16)


def split3(a):
    high = a.astype(BF16)
    rest = a - high.astype(F32)
    mid = rest.astype(BF16)
    return high, mid, (rest - mid.astype(F32)).astype(BF16)


def dot(a, b, dims):
    return lax.dot_general(a, b, (dims, ((), ())), preferred_element_type=F32)


def dot_x3(a, b, dims):
    ah, al = split2(a)
    bh, bl = split2(b)
    return dot(ah, bh, dims) + (dot(ah, bl, dims) + dot(al, bh, dims))


def panel_kernel(momentum, gradient, right, out, mom_v, grad_v, right_v, sems):
    pieces = 2
    width = COLS // pieces
    copies = []
    for layer in range(LAYERS):
        for piece in range(pieces):
            cut = slice(piece * width, (piece + 1) * width)
            slot = len(copies)
            group = [
                pltpu.make_async_copy(momentum.at[layer, :, cut], mom_v.at[layer, :, cut], sems.at[slot, 0]),
                pltpu.make_async_copy(gradient.at[layer, :, cut], grad_v.at[layer, :, cut], sems.at[slot, 1]),
                pltpu.make_async_copy(right.at[layer, cut, :], right_v.at[layer, cut, :], sems.at[slot, 2]),
            ]
            for item in group:
                item.start()
            copies.append(group)
    for layer in range(LAYERS):
        total = jnp.zeros((ROWS, R), F32)
        for piece in range(pieces):
            for item in copies[layer * pieces + piece]:
                item.wait()
            cut = slice(piece * width, (piece + 1) * width)
            buffer = mom_v[layer, :, cut] + grad_v[layer, :, cut].astype(F32)
            factor = right_v[layer, cut, :]
            both = dot(jnp.concatenate(split2(buffer), axis=0), factor, ((1,), (0,)))
            total += both[0:ROWS] + both[ROWS:]
        out[layer] = total


def chunk_of(ids, core, rel):
    return core * 4 + lax.bitwise_xor(ids[1], rel)


def columns(ids, core, rel):
    return pl.ds(pl.multiple_of(chunk_of(ids, core, rel) * PIECE, PIECE), PIECE)


FIRST, SECOND = (1, 3), (3, 1)
NEAR, FAR = [(0, rel) for rel in SECOND], [(rel, 2) for rel in FIRST]


def gram_of(panel):
    return lax.dot_general(panel, panel, (((0,), (0,)), ((), ())), precision=HIGHEST, preferred_element_type=F32)


def product(ids, core, rels, lefts, buffer, out):
    for layer in range(LAYERS):
        left = lefts[layer]
        for slot, rel in enumerate(rels[layer]):
            out[layer, slot * R : (slot + 1) * R] = wide_dot(left, buffer[layer, :, columns(ids, core, rel)])


def begin_kernel(ids, p0, p1, p2, p3, buffer, panel, lefts, packed, out):
    for layer in range(LAYERS):
        whole = (p0[layer] + p1[layer]) + (p2[layer] + p3[layer])
        panel[layer] = whole
        lefts[layer] = wide_left(whole.T)
        gram = gram_of(whole)
        packed[layer, :, 0:R] = gram[0 : R // 2]
        packed[layer, :, R:] = gram[R // 2 :]
        out[layer, 2 * R :] = packed[layer, pl.ds(pl.multiple_of((1 - ids[0]) * GRAM, GRAM), GRAM)]
    product(ids, 1 - ids[0], FAR, lefts, buffer, out)


def begin_own_kernel(ids, lefts, packed, buffer, out):
    for layer in range(LAYERS):
        out[layer, 2 * R :] = packed[layer, pl.ds(pl.multiple_of(ids[0] * GRAM, GRAM), GRAM)]
    product(ids, ids[0], FAR, lefts, buffer, out)


def rest_kernel(flip, ids, lefts, buffer, out):
    product(ids, 1 - ids[0] if flip else ids[0], NEAR, lefts, buffer, out)


def sum_x_kernel(a0, b0, a1, b1, out):
    for layer, (left, right) in enumerate(((a0, b0), (a1, b1))):
        total = left[...] + right[...]
        for z in range(8):
            out[z, layer * BAND : (layer + 1) * BAND] = total[z * BAND : (z + 1) * BAND]
            start = 2 * BAND + 4 * layer
            out[z, start : start + 4] = total[R + 4 * z : R + 4 * z + 4]


def sum_z_kernel(got, out):
    total = (got[0] + got[1]) + (got[2] + got[3]) + ((got[4] + got[5]) + (got[6] + got[7]))
    for z in range(8):
        out[z] = total


def spread_kernel(got, out, gram):
    for layer in range(LAYERS):
        for z in range(8):
            out[layer, z * BAND : (z + 1) * BAND] = got[z, layer * BAND : (layer + 1) * BAND]
            start = 2 * BAND + 4 * layer
            gram[layer, 4 * z : 4 * z + 4] = got[z, start : start + 4]


def factor_kernel(ids, own, other, out, work):
    core = ids[0]
    for index, gram in ((core, own), (1 - core, other)):
        for half in range(2):
            rows = pl.ds(pl.multiple_of(index * GRAM + half * (R // 2), GRAM), GRAM)
            for layer in range(LAYERS):
                work[layer, rows, :] = gram[layer, :, half * R : (half + 1) * R]
    factor(work, out, 0, R)


def factor(work, out, begin, end):
    lane = lax.broadcasted_iota(jnp.int32, (1, R), 1)
    for base in range(begin, end, BLOCK):
        after = base + BLOCK
        inside = (lane >= base) & (lane < after)
        rows = [
            jnp.concatenate([work[layer, base + i : base + i + 1, :] for layer in range(LAYERS)], axis=0)
            for i in range(BLOCK)
        ]
        square = [
            [jnp.broadcast_to(rows[i][:, base + j : base + j + 1], (LAYERS, R)) for j in range(i + 1)]
            for i in range(BLOCK)
        ]
        rows = [jnp.where(inside, jnp.where(lane == base + i, 1.0, 0.0), rows[i]) for i in range(BLOCK)]
        for j in range(BLOCK):
            inverse = lax.rsqrt(square[j][j])
            rows[j] = rows[j] * inverse
            for i in range(j + 1, BLOCK):
                square[i][j] = square[i][j] * inverse
            for i in range(j + 1, BLOCK):
                for k in range(j + 1, i + 1):
                    square[i][k] = square[i][k] - square[i][j] * square[k][j]
                rows[i] = rows[i] - square[i][j] * rows[j]
        for layer in range(LAYERS):
            done = jnp.concatenate([row[layer : layer + 1] for row in rows], axis=0)
            out[layer, base:after, :] = jnp.where(lane < after, done, 0.0)
            if after < R:
                high, mid, low = split3(done)
                left = jnp.concatenate([high, mid, high, mid, low, high], axis=0)
                right = jnp.concatenate([high, high, mid, mid, high, low], axis=0)
                change = dot(left, right, ((0,), (0,)))
                work[layer, after:, :] = jnp.where(inside, 0.0, work[layer, after:, :]) - change[after:, :]


def wide_left(a):
    high, low = split2(a)
    top = jnp.concatenate([high, high], axis=1)
    bottom = jnp.concatenate([low, jnp.zeros_like(low)], axis=1)
    return jnp.concatenate([top, bottom], axis=0)


def wide_dot(left, b):
    high, low = split2(b)
    both = dot(left, jnp.concatenate([high, low], axis=0), ((1,), (0,)))
    half = both.shape[0] // 2
    return both[0:half] + both[half:]


EARLY = [(0, 0), (0, 1), (0, 3)]
REST = [(0, 2), (1, 0), (1, 1), (1, 3), (1, 2)]


def spots(ids, where):
    return [(slot, columns(ids, 1 - ids[0] if side else ids[0], rel)) for slot, (side, rel) in enumerate(where)]


def reduce_layer(left, sources, reduced, layer):
    total = jnp.zeros((R, R), F32)
    for slot, source in enumerate(sources):
        part = wide_dot(left, source)
        reduced[layer, slot] = part
        square = part * part
        total += square[:, 0:R] + square[:, R:]
    return total


def update_momentum(ids, layer, where, basis, reduced, buffer, new_momentum, staged, sems):
    wide = wide_left(basis * 0.05)
    copies = []
    for slot, cut in spots(ids, where):
        staged[layer, slot] = buffer[layer, :, cut] - wide_dot(wide, reduced[layer, slot])
        copies.append(
            pltpu.make_async_copy(staged.at[layer, slot], new_momentum.at[layer, :, cut], sems.at[layer, slot])
        )
        copies[-1].start()
    return copies


def early_kernel(ids, panel, inverse, a0, a1, a3, buffer, left, reduced, total, new_momentum, staged, sems):
    copies = []
    for layer in range(LAYERS):
        sources = [piece[layer] for piece in (a0, a1, a3)]
        total[layer] = reduce_layer(wide_left(inverse[layer]), sources, reduced, layer)
        basis = lax.dot_general(
            panel[layer], inverse[layer], (((1,), (1,)), ((), ())), precision=HIGHEST, preferred_element_type=F32
        )
        left[layer] = basis
        copies += update_momentum(ids, layer, EARLY, basis, reduced, buffer, new_momentum, staged, sems)
    for item in copies:
        item.wait()


def rest_of_kernel(inverse, a20, a21, b0, b1, b3, b20, b21, before, reduced, squares):
    for layer, (own, other) in enumerate(((a20, b20), (a21, b21))):
        sources = [own[...], b0[layer], b1[layer], b3[layer], other[...]]
        total = before[layer] + reduce_layer(wide_left(inverse[layer]), sources, reduced, layer)
        squares[layer] = jnp.broadcast_to(jnp.sum(total.T, axis=0, keepdims=True), (8, R))


def momentum_kernel(ids, left, early, rest, buffer, begun, new_momentum, turned, staged, sems):
    del begun
    copies = []
    for layer in range(LAYERS):
        copies += update_momentum(ids, layer, REST, left[layer], rest, buffer, new_momentum, staged, sems)
    for layer in range(LAYERS):
        for where, source in ((EARLY, early), (REST, rest)):
            for slot, cut in spots(ids, where):
                turned[layer, cut, :] = source[layer, slot].T
    for item in copies:
        item.wait()


def weight_kernel(
    ids, left, early, rest, turned, s0, s1, s2, s3, weight, new_weight, new_basis, weight_v, basis_v, sems, basis_sems
):
    copies = []
    for layer in range(LAYERS):
        squares = (s0[layer, 0:1, :] + s1[layer, 0:1, :]) + (s2[layer, 0:1, :] + s3[layer, 0:1, :])
        scale = lax.rsqrt(squares * (1.0 / D) + 1e-06)
        wide = wide_left(left[layer] * (scale * (0.05 * math.sqrt(D / R))))
        for where, source in ((EARLY, early), (REST, rest)):
            for slot, cut in spots(ids, where):
                index = len(copies) - layer
                change = wide_dot(wide, source[layer, slot])
                weight_v[index] = (1.0 - 0.05 * 0.1) * weight[layer, :, cut] - change
                copies.append(pltpu.make_async_copy(weight_v.at[index], new_weight.at[layer, :, cut], sems.at[index]))
                copies[-1].start()
        basis_v[layer] = (turned[layer] * scale).astype(BF16)
        copies.append(pltpu.make_async_copy(basis_v.at[layer], new_basis.at[layer], basis_sems.at[layer]))
        copies[-1].start()
    for item in copies:
        item.wait()


def place(z, x, core):
    return (z * 4 + x) * 2 + core


def move_core(a):
    return lax.ppermute(a, "fsdp", [(i, i ^ 1) for i in range(64)])


def move_x(a, flip):
    moves = [(place(z, x, c), place(z, x ^ flip, c)) for z in range(8) for x in range(4) for c in range(2)]
    return lax.ppermute(a, "fsdp", moves)


def swap_z(a):
    groups = [[place(z, x, c) for z in range(8)] for x in range(4) for c in range(2)]
    return lax.all_to_all(a, "fsdp", 0, 0, axis_index_groups=groups, tiled=True)


def move_tp(a, flip):
    return lax.ppermute(a, "tp", [(i, i ^ flip) for i in range(4)])


def body(weight, gradient, momentum, right_basis):
    index = lax.axis_index("fsdp")
    core = index % 2
    ids = jnp.stack([core, (index // 2) % 4]).astype(jnp.int32)

    with jax.named_scope("panel"):
        part = call(
            panel_kernel, struct(LAYERS, ROWS, R), [HBM] * 3, (momentum, gradient, right_basis), 300 << 20, 4 << 20,
            scratch=[
                pltpu.VMEM((LAYERS, ROWS, COLS), F32), pltpu.VMEM((LAYERS, ROWS, COLS), BF16),
                pltpu.VMEM((LAYERS, COLS, R), BF16), pltpu.SemaphoreType.DMA((4, 3)),
            ],
            limit=107 << 19,
        )
        parts = [move_tp(part, flip) for flip in (3, 2, 1)]
        buffer = momentum + gradient.astype(F32)
    with jax.named_scope("product"):
        long, short = struct(LAYERS, 2 * R + GRAM, PIECE), struct(LAYERS, 2 * R, PIECE)
        panel, lefts, packed, begun = call(
            begin_kernel,
            (
                struct(LAYERS, ROWS, R), struct(LAYERS, 2 * R, 2 * R, dtype=BF16), struct(LAYERS, R // 2, PIECE),
                long,
            ),
            [SM] + [VM] * 5,
            (ids, part, *parts, buffer), 300 << 20, 3 << 20,
        )
        begun_own = call(
            begin_own_kernel, long, [SM] + [VM] * 3, (ids, lefts, packed, buffer), 300 << 20, 2 << 20
        )
        begun = move_core(begun)
        sends = [begun_own[layer] + begun[layer] for layer in range(LAYERS)]
        rest, rest_own = [
            call(
                lambda *refs, flip=flip: rest_kernel(flip, *refs), short, [SM] + [VM] * 2,
                (ids, lefts, buffer), 300 << 20, 2 << 20,
            )
            for flip in (True, False)
        ]
        rest = move_core(rest)
    with jax.named_scope("scatter"):
        pairs = []
        for layer in range(LAYERS):
            send = sends[layer]
            got = move_x(send, FIRST[layer])
            gram = send[2 * R :] + got[2 * R :]
            keep = rest_own[layer] + rest[layer] + got[0 : 2 * R]
            pairs += [
                jnp.concatenate([keep[0:R], gram]),
                move_x(jnp.concatenate([keep[R:], gram]), SECOND[layer]),
            ]
        chunks = swap_z(call(sum_x_kernel, struct(8, CHUNK, PIECE), [VM] * 4, pairs))
    with jax.named_scope("gather"):
        chunks = swap_z(call(sum_z_kernel, struct(8, CHUNK, PIECE), [VM], (chunks,)))
        whole, gram = call(spread_kernel, (struct(LAYERS, R, PIECE), struct(LAYERS, GRAM, PIECE)), [VM], (chunks,))
        group = [whole, move_x(whole, 1), move_x(whole, 3)]
        inverse = call(
            factor_kernel, struct(LAYERS, R, R), [SM] + [VM] * 2, (ids, gram, move_core(gram)), 8 << 30,
            scratch=[pltpu.VMEM((LAYERS, R, R), F32)],
        )
        inverse, *group[1:] = lax.optimization_barrier((inverse, *group[1:]))
        last = [move_x(group[2][0], 1), move_x(group[1][1], 3)]
        moved = struct(LAYERS, ROWS, COLS)

        def staging(count):
            return [pltpu.VMEM((LAYERS, count, ROWS, PIECE), F32), pltpu.SemaphoreType.DMA((LAYERS, count))]

        left, early, total, new_momentum = call(
            early_kernel,
            (struct(LAYERS, ROWS, R), struct(LAYERS, 3, R, PIECE), struct(LAYERS, R, R), moved), [SM] + [VM] * 6,
            (ids, panel, inverse, *group, buffer), 3 << 30, 3 << 20, scratch=staging(3), out_specs=(VM, VM, VM, HBM),
        )
        total, *last = lax.optimization_barrier((total, *last))
        total, *group[1:] = lax.optimization_barrier((total, *group[1:]))
        others = [move_core(item) for item in (*group, *last)]
    with jax.named_scope("update"):
        rest, squares = call(
            rest_of_kernel, (struct(LAYERS, 5, R, PIECE), struct(LAYERS, 8, R)), [VM] * 9,
            (inverse, *last, *others, total), 1 << 30,
        )
        shares = [squares] + [move_tp(squares, flip) for flip in (1, 2, 3)]
        new_momentum, turned = call(
            momentum_kernel, (moved, struct(LAYERS, COLS, R)), [SM] + [VM] * 4 + [HBM],
            (ids, left, early, rest, buffer, new_momentum), 3 << 30, 2 << 20,
            scratch=staging(5), out_specs=(HBM, VM), aliases={5: 0},
        )
        new_weight, new_basis = call(
            weight_kernel, (moved, struct(LAYERS, COLS, R, dtype=BF16)), [SM] + [VM] * 9,
            (ids, left, early, rest, turned, *shares, weight), 800 << 20, 6 << 20,
            scratch=[
                pltpu.VMEM((16, ROWS, PIECE), F32), pltpu.VMEM((LAYERS, COLS, R), BF16),
                pltpu.SemaphoreType.DMA((16,)), pltpu.SemaphoreType.DMA((LAYERS,)),
            ],
            out_specs=(HBM,) * 2,
        )
    return (new_weight, new_momentum, new_basis)


def solution(mesh):
    return jax.shard_map(
        body,
        mesh=mesh,
        in_specs=(
            P(None, "fsdp", "tp"),
            P(None, "fsdp", "tp"),
            P(None, "fsdp", "tp"),
            P(None, "tp", None),
        ),
        out_specs=(P(None, "fsdp", "tp"), P(None, "fsdp", "tp"), P(None, "tp", None)),
        check_vma=False,
    )
```

time: 102 us -> 101 us (level)
  starting transfers between devices: 22.7 us -> 27 us
  waiting for transfers between devices: 24.3 us -> 21.4 us
  Pallas kernels: 22.2 us -> 19.9 us
    ppermute x5 -> x6, starting transfers between devices: 5.24 us -> 8.18 us  [move_tp(): return lax.ppermute(a, 'tp', [(i, i ^ flip) for i in range(4)])]
    ppermute x5 -> x6, waiting for transfers between devices: 10.8 us -> 7.85 us  [move_tp(): return lax.ppermute(a, 'tp', [(i, i ^ flip) for i in range(4)])]
    pallas_call x1 -> x0, Pallas kernels: 1.83 us -> none  [body(): pl.pallas_call(momentum_kernel, out_shape=moved, in_specs=[SM] + [VM] * 3...]
    ppermute x8, starting transfers between devices: 7.58 us -> 8.66 us  [move_x(): return lax.ppermute(a, 'fsdp', moves)]
    ppermute x9 -> x8, waiting for transfers between devices: 2.31 us -> 1.41 us  [move_core(): return lax.ppermute(a, 'fsdp', [(i, i ^ 1) for i in range(64)])]
    pallas_call x14 -> x13, Pallas kernels: 20.4 us -> 19.9 us  [call(): pl.pallas_call(kernel, out_shape=outs, in_specs=ins, out_specs=out_specs...]
    ppermute x9 -> x8, starting transfers between devices: 9.88 us -> 10.2 us  [move_core(): return lax.ppermute(a, 'fsdp', [(i, i ^ 1) for i in range(64)])]
  transfers between devices with their start and end apart: 22 -> 22, of which waited for: 15 -> 11; matrix products, arithmetic and copies ran while one was open for 0% -> 0% of each run, Pallas kernels for 15% -> 13%
where the time goes in v2:
time: 101 us
  blocking collectives  30.5 us (30%)
  starting transfers between devices  27 us (27%)
  waiting for transfers between devices  21.4 us (21%)
  Pallas kernels  19.9 us (20%)
  between operations  1.08 us (1%)
    all_to_all x2, blocking collectives, swap_z(): return lax.all_to_all(a, 'fsdp', 0, 0, axis_index_groups=groups, tiled=True)  30.5 us
    pallas_call x13, Pallas kernels, call(): pl.pallas_call(kernel, out_shape=outs, in_specs=ins, out_specs=out_specs...  19.9 us
    ppermute x8, waiting for transfers between devices, move_x(): return lax.ppermute(a, 'fsdp', moves)  12.1 us
    ppermute x8, starting transfers between devices, move_core(): return lax.ppermute(a, 'fsdp', [(i, i ^ 1) for i in range(64)])  10.2 us
    ppermute x8, starting transfers between devices, move_x(): return lax.ppermute(a, 'fsdp', moves)  8.66 us
    ppermute x6, starting transfers between devices, move_tp(): return lax.ppermute(a, 'tp', [(i, i ^ flip) for i in range(4)])  8.18 us
    ppermute x6, waiting for transfers between devices, move_tp(): return lax.ppermute(a, 'tp', [(i, i ^ flip) for i in range(4)])  7.85 us
  transfers between devices with their start and end apart: 22, of which 11 were waited for; matrix products, arithmetic and copies ran while one was open for 0% of the time, Pallas kernels for 13%

profile of v2, /device:TPU:1, one launch (start us, length us, event | category | flops | bytes accessed | tf_op | source)
XLA Modules:
  0.0 100.6 jit_solution(1181510730496804156)
XLA Ops:
  0.7 2.7 %panel.1.p0 = f32[2,128,128]{2,1,0:T(8,128)S(1)} custom-call(f32[2,128,2048]{2,1,0:T(8,128)} %momentum.1, bf16[2,128,2048]{2,1,0:T(8,128)(2,1)} %gradient.1, bf16[2,2048,128]{2,1,0:T(8,128)(2,1)} %right.1), custom_call_target="tpu_custom_call" | custom-call | flops 314572800 | bytes 4194304 | tf_op jit(solution)/shard_map/panel/pallas_call | solution.py:36
  3.3 2.2 %collective-permute-start.2 = (f32[2,128,128]{2,1,0:T(8,128)S(1)}, f32[2,128,128]{2,1,0:T(8,128)S(1)}, u32[]{:S(2)}, u32[]{:S(2)}) collective-permute-start(f32[2,128,128]{2,1,0:T(8,128)S(1)} %panel.1.p0), channel_id=1, source_target_pairs={{0,1},{1,0},{2,3},{3,2},{4,5},{5,4},{6,7},{7,6},{8,9},{9,8},{10,11... | collective-permute-start | bytes 393224 | tf_op jit(solution)/shard_map/panel/ppermute | solution.py:330
  5.6 2.6 %collective-permute-start.1 = (f32[2,128,128]{2,1,0:T(8,128)S(1)}, f32[2,128,128]{2,1,0:T(8,128)S(1)}, u32[]{:S(2)}, u32[]{:S(2)}) collective-permute-start(f32[2,128,128]{2,1,0:T(8,128)S(1)} %panel.1.p0), channel_id=1, source_target_pairs={{0,2},{1,3},{2,0},{3,1},{4,6},{5,7},{6,4},{7,5},{8,10},{9,11},{10,... | collective-permute-start | bytes 393224 | tf_op jit(solution)/shard_map/panel/ppermute | solution.py:330
  8.6 5.3 %collective-permute-done.1.p2 = f32[2,128,128]{2,1,0:T(8,128)S(1)} collective-permute-done((f32[2,128,128]{2,1,0:T(8,128)S(1)}, f32[2,128,128]{2,1,0:T(8,128)S(1)}, u32[]{:S(2)}, u32[]{:S(2)}) %collective-permute-start.1) | collective-permute-done | bytes 131104 | tf_op jit(solution)/shard_map/panel/ppermute | solution.py:330
  13.9 2.5 %collective-permute-done.p1 = f32[2,128,128]{2,1,0:T(8,128)S(1)} collective-permute-done((f32[2,128,128]{2,1,0:T(8,128)S(1)}, f32[2,128,128]{2,1,0:T(8,128)S(1)}, u32[]{:S(2)}, u32[]{:S(2)}) %collective-permute-start) | collective-permute-done | bytes 131104 | tf_op jit(solution)/shard_map/panel/ppermute | solution.py:330
  16.4 1.0 %product.4 = (f32[2,128,128]{2,1,0:T(8,128)S(1)}, bf16[2,256,256]{2,1,0:T(8,128)(2,1)S(1)}, f32[2,64,256]{2,1,0:T(8,128)S(1)}, f32[2,288,256]{2,1,0:T(8,128)S(1)}) custom-call(s32[2]{0:T(128)S(1)} %pad_add_fusion.ids.refs_0_, f32[2,128,128]{2,1,0:T(8,128)S(1)} %panel.1.p0, f32[2,128,128]{2,1,0:T(8,128)S(1)} %collective-permute-done.p1, ...), custom_call_target="tpu_custom_call" | custom-call | flops 314572800 | bytes 3145728 | tf_op jit(solution)/shard_map/product/pallas_call | solution.py:36
  17.4 1.3 %collective-permute-start.4 = (f32[2,288,256]{2,1,0:T(8,128)S(1)}, f32[2,288,256]{2,1,0:T(8,128)S(1)}, u32[]{:S(2)}, u32[]{:S(2)}) collective-permute-start(f32[2,288,256]{2,1,0:T(8,128)S(1)} %get-tuple-element.31), channel_id=1, source_target_pairs={{0,4},{4,0},{8,12},{12,8},{16,20},{20,16},{24,28},{28,24},{32,36},... | collective-permute-start | bytes 1769480 | tf_op jit(solution)/shard_map/product/ppermute | solution.py:316
  18.7 0.9 product.6
  19.7 0.9 product.7
  20.6 1.3 %collective-permute-start.5 = (f32[288,256]{1,0:T(8,128)S(1)}, f32[288,256]{1,0:T(8,128)S(1)}, u32[]{:S(2)}, u32[]{:S(2)}) collective-permute-start(f32[288,256]{1,0:T(8,128)S(1)} %bitcast.24), channel_id=1, source_target_pairs={{0,8},{4,12},{8,0},{12,4},{16,24},{20,28},{24,16},{28,20},{32,40},... | collective-permute-start | bytes 884744 | tf_op jit(solution)/shard_map/scatter/ppermute | solution.py:321
  21.9 1.8 %collective-permute-start.7 = (f32[288,256]{1,0:T(8,128)S(1)}, f32[288,256]{1,0:T(8,128)S(1)}, u32[]{:S(2)}, u32[]{:S(2)}) collective-permute-start(f32[288,256]{1,0:T(8,128)S(1)} %bitcast.25), channel_id=1, source_target_pairs={{0,24},{4,28},{8,16},{12,20},{16,8},{20,12},{24,0},{28,4},{32,56},... | collective-permute-start | bytes 884744 | tf_op jit(solution)/shard_map/scatter/ppermute | solution.py:321
  23.8 0.8 product.5
  24.6 4.2 %collective-permute-done.5 = f32[288,256]{1,0:T(8,128)S(1)} collective-permute-done((f32[288,256]{1,0:T(8,128)S(1)}, f32[288,256]{1,0:T(8,128)S(1)}, u32[]{:S(2)}, u32[]{:S(2)}) %collective-permute-start.5) | collective-permute-done | bytes 294944 | tf_op jit(solution)/shard_map/scatter/ppermute | solution.py:321
  28.8 2.1 %collective-permute-done.7 = f32[288,256]{1,0:T(8,128)S(1)} collective-permute-done((f32[288,256]{1,0:T(8,128)S(1)}, f32[288,256]{1,0:T(8,128)S(1)}, u32[]{:S(2)}, u32[]{:S(2)}) %collective-permute-start.7) | collective-permute-done | bytes 294944 | tf_op jit(solution)/shard_map/scatter/ppermute | solution.py:321
  31.2 1.9 %collective-permute-start.6 = (f32[160,256]{1,0:T(8,128)S(1)}, f32[160,256]{1,0:T(8,128)S(1)}, u32[]{:S(2)}, u32[]{:S(2)}) collective-permute-start(f32[160,256]{1,0:T(8,128)S(1)} %get-tuple-element.63), channel_id=1, source_target_pairs={{0,24},{4,28},{8,16},{12,20},{16,8},{20,12},{24,0},{28,4},{32,56},... | collective-permute-start | bytes 491528 | tf_op jit(solution)/shard_map/scatter/ppermute | solution.py:321
  33.2 2.2 %collective-permute-done.8.b1 = f32[160,256]{1,0:T(8,128)S(1)} collective-permute-done((f32[160,256]{1,0:T(8,128)S(1)}, f32[160,256]{1,0:T(8,128)S(1)}, u32[]{:S(2)}, u32[]{:S(2)}) %collective-permute-start.8) | collective-permute-done | bytes 163872 | tf_op jit(solution)/shard_map/scatter/ppermute | solution.py:321
  35.4 1.4 %collective-permute-done.6.b0 = f32[160,256]{1,0:T(8,128)S(1)} collective-permute-done((f32[160,256]{1,0:T(8,128)S(1)}, f32[160,256]{1,0:T(8,128)S(1)}, u32[]{:S(2)}, u32[]{:S(2)}) %collective-permute-start.6) | collective-permute-done | bytes 163872 | tf_op jit(solution)/shard_map/scatter/ppermute | solution.py:321
  36.8 18.0 %all_to_all.10.got = f32[8,40,256]{2,1,0:T(8,128)S(1)} all-to-all(f32[8,40,256]{2,1,0:T(8,128)S(1)} %scatter.1), channel_id=1, replica_groups={{0,32,64,96,128,160,192,224},{4,36,68,100,132,164,196,228},{8,40,72,104..., dimensions={0} | all-to-all | bytes 655360 | tf_op jit(solution)/shard_map/scatter/all_to_all | solution.py:326
  54.8 12.5 %all_to_all.11.got = f32[8,40,256]{2,1,0:T(8,128)S(1)} all-to-all(f32[8,40,256]{2,1,0:T(8,128)S(1)} %gather.4), channel_id=1, replica_groups={{0,32,64,96,128,160,192,224},{4,36,68,100,132,164,196,228},{8,40,72,104..., dimensions={0} | all-to-all | bytes 655360 | tf_op jit(solution)/shard_map/gather/all_to_all | solution.py:326
  67.4 5.4 %collective-permute-start.9 = (f32[2,32,256]{2,1,0:T(8,128)S(1)}, f32[2,32,256]{2,1,0:T(8,128)S(1)}, u32[]{:S(2)}, u32[]{:S(2)}) collective-permute-start(f32[2,32,256]{2,1,0:T(8,128)S(1)} %get-tuple-element.32.own), channel_id=1, source_target_pairs={{0,4},{4,0},{8,12},{12,8},{16,20},{20,16},{24,28},{28,24},{32,36},... | collective-permute-start | bytes 196616 | tf_op jit(solution)/shard_map/gather/ppermute | solution.py:316
  72.8 1.8 %collective-permute-start.11 = (f32[2,128,256]{2,1,0:T(8,128)S(1)}, f32[2,128,256]{2,1,0:T(8,128)S(1)}, u32[]{:S(2)}, u32[]{:S(2)}) collective-permute-start(f32[2,128,256]{2,1,0:T(8,128)S(1)} %get-tuple-element.33.a0), channel_id=1, source_target_pairs={{0,24},{4,28},{8,16},{12,20},{16,8},{20,12},{24,0},{28,4},{32,56},... | collective-permute-start | bytes 786440 | tf_op jit(solution)/shard_map/gather/ppermute | solution.py:321
  74.7 5.8 %gather.6.inverse = f32[2,128,128]{2,1,0:T(8,128)S(1)} custom-call(s32[2]{0:T(128)S(1)} %pad_add_fusion.ids.refs_0_, f32[2,32,256]{2,1,0:T(8,128)S(1)} %get-tuple-element.32.own, f32[2,32,256]{2,1,0:T(8,128)S(1)} %collective-permute-done.9.other), custom_call_target="tpu_custom_call" | custom-call | flops 8589934592 | bytes 1048576 | tf_op jit(solution)/shard_map/gather/pallas_call | solution.py:36
  80.5 1.0 %collective-permute-done.11.a3 = f32[2,128,256]{2,1,0:T(8,128)S(1)} collective-permute-done((f32[2,128,256]{2,1,0:T(8,128)S(1)}, f32[2,128,256]{2,1,0:T(8,128)S(1)}, u32[]{:S(2)}, u32[]{:S(2)}) %collective-permute-start.11) | collective-permute-done | bytes 262176 | tf_op jit(solution)/shard_map/gather/ppermute | solution.py:321
  82.1 1.5 %collective-permute-start.13 = (f32[128,256]{1,0:T(8,128)S(1)}, f32[128,256]{1,0:T(8,128)S(1)}, u32[]{:S(2)}, u32[]{:S(2)}) collective-permute-start(f32[128,256]{1,0:T(8,128)S(1)} %slice_bitcast_fusion), channel_id=1, source_target_pairs={{0,24},{4,28},{8,16},{12,20},{16,8},{20,12},{24,0},{28,4},{32,56},... | collective-permute-start | bytes 393224 | tf_op jit(solution)/shard_map/gather/ppermute | solution.py:321
  83.6 2.6 %gather.7 = (f32[2,128,128]{2,1,0:T(8,128)S(1)}, f32[2,3,128,256]{3,2,1,0:T(8,128)S(1)}, f32[2,128,128]{2,1,0:T(8,128)S(1)}, f32[2,128,2048]{2,1,0:T(8,128)}) custom-call(s32[2]{0:T(128)S(1)} %pad_add_fusion.ids.refs_0_, f32[2,128,128]{2,1,0:T(8,128)S(1)} %get-tuple-element.28.panel, f32[2,128,128]{2,1,0:T(8,128)S(1)} %gather.6.inverse, ...), custom_call_target="tpu_custom_call" | custom-call | flops 3221225472 | bytes 3145728 | tf_op jit(solution)/shard_map/gather/pallas_call | solution.py:36
  86.1 1.0 collective-permute-done.13.a21
  87.1 2.8 %collective-permute-start.15 = (f32[2,128,256]{2,1,0:T(8,128)S(1)}, f32[2,128,256]{2,1,0:T(8,128)S(1)}, u32[]{:S(2)}, u32[]{:S(2)}) collective-permute-start(f32[2,128,256]{2,1,0:T(8,128)S(1)} %collective-permute-done.10.a1), channel_id=1, source_target_pairs={{0,4},{4,0},{8,12},{12,8},{16,20},{20,16},{24,28},{28,24},{32,36},... | collective-permute-start | bytes 786440 | tf_op jit(solution)/shard_map/gather/ppermute | solution.py:316
  90.5 1.2 %collective-permute-done.17.b20 = f32[128,256]{1,0:T(8,128)S(1)} collective-permute-done((f32[128,256]{1,0:T(8,128)S(1)}, f32[128,256]{1,0:T(8,128)S(1)}, u32[]{:S(2)}, u32[]{:S(2)}) %collective-permute-start.17) | collective-permute-done | bytes 131104 | tf_op jit(solution)/shard_map/gather/ppermute | solution.py:316
  92.9 0.6 collective-permute-start.20
  93.5 2.3 %collective-permute-start.19 = (f32[2,8,128]{2,1,0:T(8,128)S(1)}, f32[2,8,128]{2,1,0:T(8,128)S(1)}, u32[]{:S(2)}, u32[]{:S(2)}) collective-permute-start(f32[2,8,128]{2,1,0:T(8,128)S(1)} %get-tuple-element.49.s0), channel_id=1, source_target_pairs={{0,1},{1,0},{2,3},{3,2},{4,5},{5,4},{6,7},{7,6},{8,9},{9,8},{10,11... | collective-permute-start | bytes 24584 | tf_op jit(solution)/shard_map/update/ppermute | solution.py:330
  95.8 1.9 %update.4 = (f32[2,128,2048]{2,1,0:T(8,128)}, f32[2,2048,128]{2,1,0:T(8,128)S(1)}) custom-call(s32[2]{0:T(128)S(1)} %pad_add_fusion.ids.refs_0_, f32[2,128,128]{2,1,0:T(8,128)S(1)} %get-tuple-element.37.left, f32[2,3,128,256]{3,2,1,0:T(8,128)S(1)} %get-tuple-element.38.early, ...), custom_call_target="tpu_custom_call", output_to_operand_aliasing={{0}: (5, {})} | custom-call | flops 3221225472 | bytes 2097152 | tf_op jit(solution)/shard_map/update/pallas_call | solution.py:36
  97.8 2.6 %update.5 = (f32[2,128,2048]{2,1,0:T(8,128)}, bf16[2,2048,128]{2,1,0:T(8,128)(2,1)}) custom-call(s32[2]{0:T(128)S(1)} %pad_add_fusion.ids.refs_0_, f32[2,128,128]{2,1,0:T(8,128)S(1)} %get-tuple-element.37.left, f32[2,3,128,256]{3,2,1,0:T(8,128)S(1)} %get-tuple-element.38.early, f32[2,5,128,256]{3,2,1,0:T(8,128)S(1)} %get-tuple-element.46.rest, ...), custom_call_target="tpu_custom_call" | custom-call | flops 838860800 | bytes 6291456 | tf_op jit(solution)/shard_map/update/pallas_call | solution.py:36
  (44 shorter events, 3.3 us)
Async XLA Ops:
  0.6 7.5 %copy-start.1 = (f32[2,128,2048]{2,1,0:T(8,128)S(1)}, f32[2,128,2048]{2,1,0:T(8,128)}, u32[]{:S(2)}) copy-start(f32[2,128,2048]{2,1,0:T(8,128)} %momentum.1) | copy-start | bytes 6291460
  0.6 7.5 %copy-start.2 = (bf16[2,128,2048]{2,1,0:T(8,128)(2,1)S(1)}, bf16[2,128,2048]{2,1,0:T(8,128)(2,1)}, u32[]{:S(2)}) copy-start(bf16[2,128,2048]{2,1,0:T(8,128)(2,1)} %gradient.1) | copy-start | bytes 3145732
  3.3 5.2 %collective-permute-start.2 = (f32[2,128,128]{2,1,0:T(8,128)S(1)}, f32[2,128,128]{2,1,0:T(8,128)S(1)}, u32[]{:S(2)}, u32[]{:S(2)}) collective-permute-start(f32[2,128,128]{2,1,0:T(8,128)S(1)} %panel.1.p0), channel_id=1, source_target_pairs={{0,1},{1,0},{2,3},{3,2},{4,5},{5,4},{6,7},{7,6},{8,9},{9,8},{10,11... | collective-permute-start | bytes 393224 | tf_op jit(solution)/shard_map/panel/ppermute | solution.py:330
  5.6 8.3 %collective-permute-start.1 = (f32[2,128,128]{2,1,0:T(8,128)S(1)}, f32[2,128,128]{2,1,0:T(8,128)S(1)}, u32[]{:S(2)}, u32[]{:S(2)}) collective-permute-start(f32[2,128,128]{2,1,0:T(8,128)S(1)} %panel.1.p0), channel_id=1, source_target_pairs={{0,2},{1,3},{2,0},{3,1},{4,6},{5,7},{6,4},{7,5},{8,10},{9,11},{10,... | collective-permute-start | bytes 393224 | tf_op jit(solution)/shard_map/panel/ppermute | solution.py:330
  8.2 8.2 %collective-permute-start = (f32[2,128,128]{2,1,0:T(8,128)S(1)}, f32[2,128,128]{2,1,0:T(8,128)S(1)}, u32[]{:S(2)}, u32[]{:S(2)}) collective-permute-start(f32[2,128,128]{2,1,0:T(8,128)S(1)} %panel.1.p0), channel_id=1, source_target_pairs={{0,3},{1,2},{2,1},{3,0},{4,7},{5,6},{6,5},{7,4},{8,11},{9,10},{10,... | collective-permute-start | bytes 393224 | tf_op jit(solution)/shard_map/panel/ppermute | solution.py:330
  17.4 3.1 %collective-permute-start.4 = (f32[2,288,256]{2,1,0:T(8,128)S(1)}, f32[2,288,256]{2,1,0:T(8,128)S(1)}, u32[]{:S(2)}, u32[]{:S(2)}) collective-permute-start(f32[2,288,256]{2,1,0:T(8,128)S(1)} %get-tuple-element.31), channel_id=1, source_target_pairs={{0,4},{4,0},{8,12},{12,8},{16,20},{20,16},{24,28},{28,24},{32,36},... | collective-permute-start | bytes 1769480 | tf_op jit(solution)/shard_map/product/ppermute | solution.py:316
  19.6 5.0 %collective-permute-start.3 = (f32[2,256,256]{2,1,0:T(8,128)S(1)}, f32[2,256,256]{2,1,0:T(8,128)S(1)}, u32[]{:S(2)}, u32[]{:S(2)}) collective-permute-start(f32[2,256,256]{2,1,0:T(8,128)S(1)} %product.6), channel_id=1, source_target_pairs={{0,4},{4,0},{8,12},{12,8},{16,20},{20,16},{24,28},{28,24},{32,36},... | collective-permute-start | bytes 1572872 | tf_op jit(solution)/shard_map/product/ppermute | solution.py:316
  20.6 8.2 %collective-permute-start.5 = (f32[288,256]{1,0:T(8,128)S(1)}, f32[288,256]{1,0:T(8,128)S(1)}, u32[]{:S(2)}, u32[]{:S(2)}) collective-permute-start(f32[288,256]{1,0:T(8,128)S(1)} %bitcast.24), channel_id=1, source_target_pairs={{0,8},{4,12},{8,0},{12,4},{16,24},{20,28},{24,16},{28,20},{32,40},... | collective-permute-start | bytes 884744 | tf_op jit(solution)/shard_map/scatter/ppermute | solution.py:321
  21.9 9.0 %collective-permute-start.7 = (f32[288,256]{1,0:T(8,128)S(1)}, f32[288,256]{1,0:T(8,128)S(1)}, u32[]{:S(2)}, u32[]{:S(2)}) collective-permute-start(f32[288,256]{1,0:T(8,128)S(1)} %bitcast.25), channel_id=1, source_target_pairs={{0,24},{4,28},{8,16},{12,20},{16,8},{20,12},{24,0},{28,4},{32,56},... | collective-permute-start | bytes 884744 | tf_op jit(solution)/shard_map/scatter/ppermute | solution.py:321
  31.1 4.3 %collective-permute-start.8 = (f32[160,256]{1,0:T(8,128)S(1)}, f32[160,256]{1,0:T(8,128)S(1)}, u32[]{:S(2)}, u32[]{:S(2)}) collective-permute-start(f32[160,256]{1,0:T(8,128)S(1)} %get-tuple-element.61), channel_id=1, source_target_pairs={{0,8},{4,12},{8,0},{12,4},{16,24},{20,28},{24,16},{28,20},{32,40},... | collective-permute-start | bytes 491528 | tf_op jit(solution)/shard_map/scatter/ppermute | solution.py:321
  31.2 5.5 %collective-permute-start.6 = (f32[160,256]{1,0:T(8,128)S(1)}, f32[160,256]{1,0:T(8,128)S(1)}, u32[]{:S(2)}, u32[]{:S(2)}) collective-permute-start(f32[160,256]{1,0:T(8,128)S(1)} %get-tuple-element.63), channel_id=1, source_target_pairs={{0,24},{4,28},{8,16},{12,20},{16,8},{20,12},{24,0},{28,4},{32,56},... | collective-permute-start | bytes 491528 | tf_op jit(solution)/shard_map/scatter/ppermute | solution.py:321
  67.4 7.3 %collective-permute-start.9 = (f32[2,32,256]{2,1,0:T(8,128)S(1)}, f32[2,32,256]{2,1,0:T(8,128)S(1)}, u32[]{:S(2)}, u32[]{:S(2)}) collective-permute-start(f32[2,32,256]{2,1,0:T(8,128)S(1)} %get-tuple-element.32.own), channel_id=1, source_target_pairs={{0,4},{4,0},{8,12},{12,8},{16,20},{20,16},{24,28},{28,24},{32,36},... | collective-permute-start | bytes 196616 | tf_op jit(solution)/shard_map/gather/ppermute | solution.py:316
  72.7 17.7 %collective-permute-start.14 = (f32[2,128,256]{2,1,0:T(8,128)S(1)}, f32[2,128,256]{2,1,0:T(8,128)S(1)}, u32[]{:S(2)}, u32[]{:S(2)}) collective-permute-start(f32[2,128,256]{2,1,0:T(8,128)S(1)} %get-tuple-element.33.a0), channel_id=1, source_target_pairs={{0,4},{4,0},{8,12},{12,8},{16,20},{20,16},{24,28},{28,24},{32,36},... | collective-permute-start | bytes 786440 | tf_op jit(solution)/shard_map/gather/ppermute | solution.py:316
  72.8 8.7 %collective-permute-start.11 = (f32[2,128,256]{2,1,0:T(8,128)S(1)}, f32[2,128,256]{2,1,0:T(8,128)S(1)}, u32[]{:S(2)}, u32[]{:S(2)}) collective-permute-start(f32[2,128,256]{2,1,0:T(8,128)S(1)} %get-tuple-element.33.a0), channel_id=1, source_target_pairs={{0,24},{4,28},{8,16},{12,20},{16,8},{20,12},{24,0},{28,4},{32,56},... | collective-permute-start | bytes 786440 | tf_op jit(solution)/shard_map/gather/ppermute | solution.py:321
  74.6 7.2 %collective-permute-start.10 = (f32[2,128,256]{2,1,0:T(8,128)S(1)}, f32[2,128,256]{2,1,0:T(8,128)S(1)}, u32[]{:S(2)}, u32[]{:S(2)}) collective-permute-start(f32[2,128,256]{2,1,0:T(8,128)S(1)} %get-tuple-element.33.a0), channel_id=1, source_target_pairs={{0,8},{4,12},{8,0},{12,4},{16,24},{20,28},{24,16},{28,20},{32,40},... | collective-permute-start | bytes 786440 | tf_op jit(solution)/shard_map/gather/ppermute | solution.py:321
  81.8 4.3 %collective-permute-start.12 = (f32[128,256]{1,0:T(8,128)S(1)}, f32[128,256]{1,0:T(8,128)S(1)}, u32[]{:S(2)}, u32[]{:S(2)}) collective-permute-start(f32[128,256]{1,0:T(8,128)S(1)} %slice_bitcast_fusion.1), channel_id=1, source_target_pairs={{0,8},{4,12},{8,0},{12,4},{16,24},{20,28},{24,16},{28,20},{32,40},... | collective-permute-start | bytes 393224 | tf_op jit(solution)/shard_map/gather/ppermute | solution.py:321
  82.1 5.0 %collective-permute-start.13 = (f32[128,256]{1,0:T(8,128)S(1)}, f32[128,256]{1,0:T(8,128)S(1)}, u32[]{:S(2)}, u32[]{:S(2)}) collective-permute-start(f32[128,256]{1,0:T(8,128)S(1)} %slice_bitcast_fusion), channel_id=1, source_target_pairs={{0,24},{4,28},{8,16},{12,20},{16,8},{20,12},{24,0},{28,4},{32,56},... | collective-permute-start | bytes 393224 | tf_op jit(solution)/shard_map/gather/ppermute | solution.py:321
  87.1 4.7 %collective-permute-start.15 = (f32[2,128,256]{2,1,0:T(8,128)S(1)}, f32[2,128,256]{2,1,0:T(8,128)S(1)}, u32[]{:S(2)}, u32[]{:S(2)}) collective-permute-start(f32[2,128,256]{2,1,0:T(8,128)S(1)} %collective-permute-done.10.a1), channel_id=1, source_target_pairs={{0,4},{4,0},{8,12},{12,8},{16,20},{20,16},{24,28},{28,24},{32,36},... | collective-permute-start | bytes 786440 | tf_op jit(solution)/shard_map/gather/ppermute | solution.py:316
  89.9 1.9 %collective-permute-start.16 = (f32[2,128,256]{2,1,0:T(8,128)S(1)}, f32[2,128,256]{2,1,0:T(8,128)S(1)}, u32[]{:S(2)}, u32[]{:S(2)}) collective-permute-start(f32[2,128,256]{2,1,0:T(8,128)S(1)} %collective-permute-done.11.a3), channel_id=1, source_target_pairs={{0,4},{4,0},{8,12},{12,8},{16,20},{20,16},{24,28},{28,24},{32,36},... | collective-permute-start | bytes 786440 | tf_op jit(solution)/shard_map/gather/ppermute | solution.py:316
  90.0 1.7 %collective-permute-start.17 = (f32[128,256]{1,0:T(8,128)S(1)}, f32[128,256]{1,0:T(8,128)S(1)}, u32[]{:S(2)}, u32[]{:S(2)}) collective-permute-start(f32[128,256]{1,0:T(8,128)S(1)} %collective-permute-done.12.a20), channel_id=1, source_target_pairs={{0,4},{4,0},{8,12},{12,8},{16,20},{20,16},{24,28},{28,24},{32,36},... | collective-permute-start | bytes 393224 | tf_op jit(solution)/shard_map/gather/ppermute | solution.py:316
  90.5 1.4 %collective-permute-start.18 = (f32[128,256]{1,0:T(8,128)S(1)}, f32[128,256]{1,0:T(8,128)S(1)}, u32[]{:S(2)}, u32[]{:S(2)}) collective-permute-start(f32[128,256]{1,0:T(8,128)S(1)} %collective-permute-done.13.a21), channel_id=1, source_target_pairs={{0,4},{4,0},{8,12},{12,8},{16,20},{20,16},{24,28},{28,24},{32,36},... | collective-permute-start | bytes 393224 | tf_op jit(solution)/shard_map/gather/ppermute | solution.py:316
  92.5 5.3 %collective-permute-start.21 = (f32[2,8,128]{2,1,0:T(8,128)S(1)}, f32[2,8,128]{2,1,0:T(8,128)S(1)}, u32[]{:S(2)}, u32[]{:S(2)}) collective-permute-start(f32[2,8,128]{2,1,0:T(8,128)S(1)} %get-tuple-element.49.s0), channel_id=1, source_target_pairs={{0,3},{1,2},{2,1},{3,0},{4,7},{5,6},{6,5},{7,4},{8,11},{9,10},{10,... | collective-permute-start | bytes 24584 | tf_op jit(solution)/shard_map/update/ppermute | solution.py:330
  92.9 4.9 %collective-permute-start.20 = (f32[2,8,128]{2,1,0:T(8,128)S(1)}, f32[2,8,128]{2,1,0:T(8,128)S(1)}, u32[]{:S(2)}, u32[]{:S(2)}) collective-permute-start(f32[2,8,128]{2,1,0:T(8,128)S(1)} %get-tuple-element.49.s0), channel_id=1, source_target_pairs={{0,2},{1,3},{2,0},{3,1},{4,6},{5,7},{6,4},{7,5},{8,10},{9,11},{10,... | collective-permute-start | bytes 24584 | tf_op jit(solution)/shard_map/update/ppermute | solution.py:330
  93.5 4.3 %collective-permute-start.19 = (f32[2,8,128]{2,1,0:T(8,128)S(1)}, f32[2,8,128]{2,1,0:T(8,128)S(1)}, u32[]{:S(2)}, u32[]{:S(2)}) collective-permute-start(f32[2,8,128]{2,1,0:T(8,128)S(1)} %get-tuple-element.49.s0), channel_id=1, source_target_pairs={{0,1},{1,0},{2,3},{3,2},{4,5},{5,4},{6,7},{7,6},{8,9},{9,8},{10,11... | collective-permute-start | bytes 24584 | tf_op jit(solution)/shard_map/update/ppermute | solution.py:330
  95.8 2.0 %copy-start = (f32[2,128,2048]{2,1,0:T(8,128)S(1)}, f32[2,128,2048]{2,1,0:T(8,128)}, u32[]{:S(2)}) copy-start(f32[2,128,2048]{2,1,0:T(8,128)} %weight.1) | copy-start | bytes 6291460

commit v3 on v2

--- a/solution.py
+++ b/solution.py
@@ -104,8 +104,8 @@
     return pl.ds(pl.multiple_of(chunk_of(ids, core, rel) * PIECE, PIECE), PIECE)
 
 
-FIRST, SECOND = (1, 3), (3, 1)
-NEAR, FAR = [(0, rel) for rel in SECOND], [(rel, 2) for rel in FIRST]
+FIRST = (1, 3)
+FAR, REST_OF_X = (2,), (0, 1, 3)
 
 
 def gram_of(panel):
@@ -115,7 +115,7 @@
 def product(ids, core, rels, lefts, buffer, out):
     for layer in range(LAYERS):
         left = lefts[layer]
-        for slot, rel in enumerate(rels[layer]):
+        for slot, rel in enumerate(rels):
             out[layer, slot * R : (slot + 1) * R] = wide_dot(left, buffer[layer, :, columns(ids, core, rel)])
 
 
@@ -127,27 +127,29 @@
         gram = gram_of(whole)
         packed[layer, :, 0:R] = gram[0 : R // 2]
         packed[layer, :, R:] = gram[R // 2 :]
-        out[layer, 2 * R :] = packed[layer, pl.ds(pl.multiple_of((1 - ids[0]) * GRAM, GRAM), GRAM)]
+        out[layer, R:] = packed[layer, pl.ds(pl.multiple_of((1 - ids[0]) * GRAM, GRAM), GRAM)]
     product(ids, 1 - ids[0], FAR, lefts, buffer, out)
 
 
 def begin_own_kernel(ids, lefts, packed, buffer, out):
     for layer in range(LAYERS):
-        out[layer, 2 * R :] = packed[layer, pl.ds(pl.multiple_of(ids[0] * GRAM, GRAM), GRAM)]
+        out[layer, R:] = packed[layer, pl.ds(pl.multiple_of(ids[0] * GRAM, GRAM), GRAM)]
     product(ids, ids[0], FAR, lefts, buffer, out)
 
 
 def rest_kernel(flip, ids, lefts, buffer, out):
-    product(ids, 1 - ids[0] if flip else ids[0], NEAR, lefts, buffer, out)
-
-
-def sum_x_kernel(a0, b0, a1, b1, out):
-    for layer, (left, right) in enumerate(((a0, b0), (a1, b1))):
-        total = left[...] + right[...]
+    product(ids, 1 - ids[0] if flip else ids[0], REST_OF_X, lefts, buffer, out)
+
+
+def sum_x_kernel(own, got1, got3, gram, out):
+    for layer, last in enumerate((got3, got1)):
+        rows = slice(layer * R, (layer + 1) * R)
+        total = own[layer] + (got1[rows] + got3[rows])
+        grams = gram[layer] + last[2 * R :]
         for z in range(8):
             out[z, layer * BAND : (layer + 1) * BAND] = total[z * BAND : (z + 1) * BAND]
             start = 2 * BAND + 4 * layer
-            out[z, start : start + 4] = total[R + 4 * z : R + 4 * z + 4]
+            out[z, start : start + 4] = grams[4 * z : 4 * z + 4]
 
 
 def sum_z_kernel(got, out):
@@ -344,10 +346,10 @@
             ],
             limit=107 << 19,
         )
-        parts = [move_tp(part, flip) for flip in (3, 2, 1)]
+        parts = [move_tp(part, flip) for flip in (1, 3, 2)]
         buffer = momentum + gradient.astype(F32)
     with jax.named_scope("product"):
-        long, short = struct(LAYERS, 2 * R + GRAM, PIECE), struct(LAYERS, 2 * R, PIECE)
+        long, short = struct(LAYERS, R + GRAM, PIECE), struct(LAYERS, 3 * R, PIECE)
         panel, lefts, packed, begun = call(
             begin_kernel,
             (
@@ -371,17 +373,14 @@
         ]
         rest = move_core(rest)
     with jax.named_scope("scatter"):
-        pairs = []
-        for layer in range(LAYERS):
-            send = sends[layer]
-            got = move_x(send, FIRST[layer])
-            gram = send[2 * R :] + got[2 * R :]
-            keep = rest_own[layer] + rest[layer] + got[0 : 2 * R]
-            pairs += [
-                jnp.concatenate([keep[0:R], gram]),
-                move_x(jnp.concatenate([keep[R:], gram]), SECOND[layer]),
-            ]
-        chunks = swap_z(call(sum_x_kernel, struct(8, CHUNK, PIECE), [VM] * 4, pairs))
+        got = [move_x(send, flip) for send, flip in zip(sends, FIRST)]
+        gram = jnp.stack([send[R:] + more[R:] for send, more in zip(sends, got)])
+        rest = rest_own + rest
+        own, to1, to3 = rest[:, 0:R], rest[:, R : 2 * R], rest[:, 2 * R :]
+        to1 = jnp.concatenate([to1[0], to1[1] + got[1][0:R], gram[1]])
+        to3 = jnp.concatenate([to3[0] + got[0][0:R], to3[1], gram[0]])
+        chunks = call(sum_x_kernel, struct(8, CHUNK, PIECE), [VM] * 4, (own, move_x(to1, 1), move_x(to3, 3), gram))
+        chunks = swap_z(chunks)
     with jax.named_scope("gather"):
         chunks = swap_z(call(sum_z_kernel, struct(8, CHUNK, PIECE), [VM], (chunks,)))
         whole, gram = call(spread_kernel, (struct(LAYERS, R, PIECE), struct(LAYERS, GRAM, PIECE)), [VM], (chunks,))

time: 101 us -> 99.1 us (0.981)
  starting transfers between devices: 27 us -> 22.9 us
  waiting for transfers between devices: 21.4 us -> 23.8 us
    ppermute x8, starting transfers between devices: 8.66 us -> 5.6 us  [move_x(): return lax.ppermute(a, 'fsdp', moves)]
    ppermute x8, waiting for transfers between devices: 12.1 us -> 14.6 us  [move_x(): return lax.ppermute(a, 'fsdp', moves)]
  transfers between devices with their start and end apart: 22 -> 22, of which waited for: 11 -> 12; matrix products, arithmetic and copies ran while one was open for 0% -> 0% of each run, Pallas kernels for 13% -> 13%
where the time goes in v3:
time: 99.1 us; the launch traced here: 98.9 us
  blocking collectives  30.6 us (31%)
  waiting for transfers between devices  23.8 us (24%)
  starting transfers between devices  22.9 us (23%)
  Pallas kernels  19.9 us (20%)
  between operations  1.04 us (1%)
    all_to_all x2, blocking collectives, swap_z(): return lax.all_to_all(a, 'fsdp', 0, 0, axis_index_groups=groups, tiled=True)  30.6 us
    pallas_call x13, Pallas kernels, call(): pl.pallas_call(kernel, out_shape=outs, in_specs=ins, out_specs=out_specs...  19.9 us
    ppermute x8, waiting for transfers between devices, move_x(): return lax.ppermute(a, 'fsdp', moves)  14.6 us
    ppermute x8, starting transfers between devices, move_core(): return lax.ppermute(a, 'fsdp', [(i, i ^ 1) for i in range(64)])  9.35 us
    ppermute x6, starting transfers between devices, move_tp(): return lax.ppermute(a, 'tp', [(i, i ^ flip) for i in range(4)])  7.95 us
    ppermute x6, waiting for transfers between devices, move_tp(): return lax.ppermute(a, 'tp', [(i, i ^ flip) for i in range(4)])  7.75 us
    ppermute x8, starting transfers between devices, move_x(): return lax.ppermute(a, 'fsdp', moves)  5.6 us
  transfers between devices with their start and end apart: 22, of which 12 were waited for; matrix products, arithmetic and copies ran while one was open for 0% of the time, Pallas kernels for 13%

profile of v3, /device:TPU:1, one launch (start us, length us, event | category | flops | bytes accessed | tf_op | source)
XLA Modules:
  0.0 98.9 jit_solution(17480752103840804316)
XLA Ops:
  0.7 2.7 %panel.1.p0 = f32[2,128,128]{2,1,0:T(8,128)S(1)} custom-call(f32[2,128,2048]{2,1,0:T(8,128)} %momentum.1, bf16[2,128,2048]{2,1,0:T(8,128)(2,1)} %gradient.1, bf16[2,2048,128]{2,1,0:T(8,128)(2,1)} %right.1), custom_call_target="tpu_custom_call" | custom-call | flops 314572800 | bytes 4194304 | tf_op jit(solution)/shard_map/panel/pallas_call | solution.py:36
  3.3 3.8 %collective-permute-start.2 = (f32[2,128,128]{2,1,0:T(8,128)S(1)}, f32[2,128,128]{2,1,0:T(8,128)S(1)}, u32[]{:S(2)}, u32[]{:S(2)}) collective-permute-start(f32[2,128,128]{2,1,0:T(8,128)S(1)} %panel.1.p0), channel_id=1, source_target_pairs={{0,2},{1,3},{2,0},{3,1},{4,6},{5,7},{6,4},{7,5},{8,10},{9,11},{10,... | collective-permute-start | bytes 393224 | tf_op jit(solution)/shard_map/panel/ppermute | solution.py:332
  7.2 0.8 collective-permute-start.1
  8.3 1.2 %collective-permute-done.2.p3 = f32[2,128,128]{2,1,0:T(8,128)S(1)} collective-permute-done((f32[2,128,128]{2,1,0:T(8,128)S(1)}, f32[2,128,128]{2,1,0:T(8,128)S(1)}, u32[]{:S(2)}, u32[]{:S(2)}) %collective-permute-start.2) | collective-permute-done | bytes 131104 | tf_op jit(solution)/shard_map/panel/ppermute | solution.py:332
  9.5 5.3 %collective-permute-done.1.p2 = f32[2,128,128]{2,1,0:T(8,128)S(1)} collective-permute-done((f32[2,128,128]{2,1,0:T(8,128)S(1)}, f32[2,128,128]{2,1,0:T(8,128)S(1)}, u32[]{:S(2)}, u32[]{:S(2)}) %collective-permute-start.1) | collective-permute-done | bytes 131104 | tf_op jit(solution)/shard_map/panel/ppermute | solution.py:332
  14.9 1.0 product.4
  15.8 0.9 collective-permute-start.4
  16.7 0.9 product.6
  17.8 0.8 product.7
  18.6 1.7 %collective-permute-start.5 = (f32[160,256]{1,0:T(8,128)S(1)}, f32[160,256]{1,0:T(8,128)S(1)}, u32[]{:S(2)}, u32[]{:S(2)}) collective-permute-start(f32[160,256]{1,0:T(8,128)S(1)} %bitcast.33), channel_id=1, source_target_pairs={{0,24},{4,28},{8,16},{12,20},{16,8},{20,12},{24,0},{28,4},{32,56},... | collective-permute-start | bytes 491528 | tf_op jit(solution)/shard_map/scatter/ppermute | solution.py:323
  20.3 0.9 product.5
  21.3 3.9 %collective-permute-done.5 = f32[160,256]{1,0:T(8,128)S(1)} collective-permute-done((f32[160,256]{1,0:T(8,128)S(1)}, f32[160,256]{1,0:T(8,128)S(1)}, u32[]{:S(2)}, u32[]{:S(2)}) %collective-permute-start.5) | collective-permute-done | bytes 163872 | tf_op jit(solution)/shard_map/scatter/ppermute | solution.py:323
  25.2 1.1 %collective-permute-done.7 = f32[160,256]{1,0:T(8,128)S(1)} collective-permute-done((f32[160,256]{1,0:T(8,128)S(1)}, f32[160,256]{1,0:T(8,128)S(1)}, u32[]{:S(2)}, u32[]{:S(2)}) %collective-permute-start.7) | collective-permute-done | bytes 163872 | tf_op jit(solution)/shard_map/scatter/ppermute | solution.py:323
  26.7 1.4 %collective-permute-start.8 = (f32[288,256]{1,0:T(8,128)S(1)}, f32[288,256]{1,0:T(8,128)S(1)}, u32[]{:S(2)}, u32[]{:S(2)}) collective-permute-start(f32[288,256]{1,0:T(8,128)S(1)} %pad_maximum_fusion.1), channel_id=1, source_target_pairs={{0,24},{4,28},{8,16},{12,20},{16,8},{20,12},{24,0},{28,4},{32,56},... | collective-permute-start | bytes 884744 | tf_op jit(solution)/shard_map/scatter/ppermute | solution.py:323
  28.1 5.3 %collective-permute-done.6.got1 = f32[288,256]{1,0:T(8,128)S(1)} collective-permute-done((f32[288,256]{1,0:T(8,128)S(1)}, f32[288,256]{1,0:T(8,128)S(1)}, u32[]{:S(2)}, u32[]{:S(2)}) %collective-permute-start.6) | collective-permute-done | bytes 294944 | tf_op jit(solution)/shard_map/scatter/ppermute | solution.py:323
  33.4 1.2 %collective-permute-done.8.got3 = f32[288,256]{1,0:T(8,128)S(1)} collective-permute-done((f32[288,256]{1,0:T(8,128)S(1)}, f32[288,256]{1,0:T(8,128)S(1)}, u32[]{:S(2)}, u32[]{:S(2)}) %collective-permute-start.8) | collective-permute-done | bytes 294944 | tf_op jit(solution)/shard_map/scatter/ppermute | solution.py:323
  34.7 18.1 %all_to_all.10.got = f32[8,40,256]{2,1,0:T(8,128)S(1)} all-to-all(f32[8,40,256]{2,1,0:T(8,128)S(1)} %scatter.1), channel_id=1, replica_groups={{0,32,64,96,128,160,192,224},{4,36,68,100,132,164,196,228},{8,40,72,104..., dimensions={0} | all-to-all | bytes 655360 | tf_op jit(solution)/shard_map/scatter/all_to_all | solution.py:328
  52.8 12.5 %all_to_all.11.got = f32[8,40,256]{2,1,0:T(8,128)S(1)} all-to-all(f32[8,40,256]{2,1,0:T(8,128)S(1)} %gather.4), channel_id=1, replica_groups={{0,32,64,96,128,160,192,224},{4,36,68,100,132,164,196,228},{8,40,72,104..., dimensions={0} | all-to-all | bytes 655360 | tf_op jit(solution)/shard_map/gather/all_to_all | solution.py:328
  65.3 5.3 %collective-permute-start.9 = (f32[2,32,256]{2,1,0:T(8,128)S(1)}, f32[2,32,256]{2,1,0:T(8,128)S(1)}, u32[]{:S(2)}, u32[]{:S(2)}) collective-permute-start(f32[2,32,256]{2,1,0:T(8,128)S(1)} %get-tuple-element.32.own), channel_id=1, source_target_pairs={{0,4},{4,0},{8,12},{12,8},{16,20},{20,16},{24,28},{28,24},{32,36},... | collective-permute-start | bytes 196616 | tf_op jit(solution)/shard_map/gather/ppermute | solution.py:318
  70.8 0.7 collective-permute-start.11
  71.6 5.8 %gather.6.inverse = f32[2,128,128]{2,1,0:T(8,128)S(1)} custom-call(s32[2]{0:T(128)S(1)} %pad_add_fusion.ids.refs_0_, f32[2,32,256]{2,1,0:T(8,128)S(1)} %get-tuple-element.32.own, f32[2,32,256]{2,1,0:T(8,128)S(1)} %collective-permute-done.9.other), custom_call_target="tpu_custom_call" | custom-call | flops 8589934592 | bytes 1048576 | tf_op jit(solution)/shard_map/gather/pallas_call | solution.py:36
  77.4 2.1 %collective-permute-done.11.a3 = f32[2,128,256]{2,1,0:T(8,128)S(1)} collective-permute-done((f32[2,128,256]{2,1,0:T(8,128)S(1)}, f32[2,128,256]{2,1,0:T(8,128)S(1)}, u32[]{:S(2)}, u32[]{:S(2)}) %collective-permute-start.11) | collective-permute-done | bytes 262176 | tf_op jit(solution)/shard_map/gather/ppermute | solution.py:323
  79.6 1.5 %collective-permute-start.13 = (f32[128,256]{1,0:T(8,128)S(1)}, f32[128,256]{1,0:T(8,128)S(1)}, u32[]{:S(2)}, u32[]{:S(2)}) collective-permute-start(f32[128,256]{1,0:T(8,128)S(1)} %slice_bitcast_fusion.4), channel_id=1, source_target_pairs={{0,24},{4,28},{8,16},{12,20},{16,8},{20,12},{24,0},{28,4},{32,56},... | collective-permute-start | bytes 393224 | tf_op jit(solution)/shard_map/gather/ppermute | solution.py:323
  81.0 2.6 %gather.7 = (f32[2,128,128]{2,1,0:T(8,128)S(1)}, f32[2,3,128,256]{3,2,1,0:T(8,128)S(1)}, f32[2,128,128]{2,1,0:T(8,128)S(1)}, f32[2,128,2048]{2,1,0:T(8,128)}) custom-call(s32[2]{0:T(128)S(1)} %pad_add_fusion.ids.refs_0_, f32[2,128,128]{2,1,0:T(8,128)S(1)} %get-tuple-element.28.panel, f32[2,128,128]{2,1,0:T(8,128)S(1)} %gather.6.inverse, ...), custom_call_target="tpu_custom_call" | custom-call | flops 3221225472 | bytes 3145728 | tf_op jit(solution)/shard_map/gather/pallas_call | solution.py:36
  83.6 1.1 %collective-permute-done.13.a21 = f32[128,256]{1,0:T(8,128)S(1)} collective-permute-done((f32[128,256]{1,0:T(8,128)S(1)}, f32[128,256]{1,0:T(8,128)S(1)}, u32[]{:S(2)}, u32[]{:S(2)}) %collective-permute-start.13) | collective-permute-done | bytes 131104 | tf_op jit(solution)/shard_map/gather/ppermute | solution.py:323
  84.7 2.4 %collective-permute-start.15 = (f32[2,128,256]{2,1,0:T(8,128)S(1)}, f32[2,128,256]{2,1,0:T(8,128)S(1)}, u32[]{:S(2)}, u32[]{:S(2)}) collective-permute-start(f32[2,128,256]{2,1,0:T(8,128)S(1)} %collective-permute-done.10.a1), channel_id=1, source_target_pairs={{0,4},{4,0},{8,12},{12,8},{16,20},{20,16},{24,28},{28,24},{32,36},... | collective-permute-start | bytes 786440 | tf_op jit(solution)/shard_map/gather/ppermute | solution.py:318
  87.6 1.2 %collective-permute-done.17.b20 = f32[128,256]{1,0:T(8,128)S(1)} collective-permute-done((f32[128,256]{1,0:T(8,128)S(1)}, f32[128,256]{1,0:T(8,128)S(1)}, u32[]{:S(2)}, u32[]{:S(2)}) %collective-permute-start.17) | collective-permute-done | bytes 131104 | tf_op jit(solution)/shard_map/gather/ppermute | solution.py:318
  89.0 0.6 update.3
  89.6 2.5 %collective-permute-start.21 = (f32[2,8,128]{2,1,0:T(8,128)S(1)}, f32[2,8,128]{2,1,0:T(8,128)S(1)}, u32[]{:S(2)}, u32[]{:S(2)}) collective-permute-start(f32[2,8,128]{2,1,0:T(8,128)S(1)} %get-tuple-element.49.s0), channel_id=1, source_target_pairs={{0,3},{1,2},{2,1},{3,0},{4,7},{5,6},{6,5},{7,4},{8,11},{9,10},{10,... | collective-permute-start | bytes 24584 | tf_op jit(solution)/shard_map/update/ppermute | solution.py:332
  93.0 1.9 %update.4 = (f32[2,128,2048]{2,1,0:T(8,128)}, f32[2,2048,128]{2,1,0:T(8,128)S(1)}) custom-call(s32[2]{0:T(128)S(1)} %pad_add_fusion.ids.refs_0_, f32[2,128,128]{2,1,0:T(8,128)S(1)} %get-tuple-element.37.left, f32[2,3,128,256]{3,2,1,0:T(8,128)S(1)} %get-tuple-element.38.early, ...), custom_call_target="tpu_custom_call", output_to_operand_aliasing={{0}: (5, {})} | custom-call | flops 3221225472 | bytes 2097152 | tf_op jit(solution)/shard_map/update/pallas_call | solution.py:36
  94.9 1.2 %collective-permute-done.20.s2 = f32[2,8,128]{2,1,0:T(8,128)S(1)} collective-permute-done((f32[2,8,128]{2,1,0:T(8,128)S(1)}, f32[2,8,128]{2,1,0:T(8,128)S(1)}, u32[]{:S(2)}, u32[]{:S(2)}) %collective-permute-start.20) | collective-permute-done | bytes 8224 | tf_op jit(solution)/shard_map/update/ppermute | solution.py:332
  96.1 2.6 %update.5 = (f32[2,128,2048]{2,1,0:T(8,128)}, bf16[2,2048,128]{2,1,0:T(8,128)(2,1)}) custom-call(s32[2]{0:T(128)S(1)} %pad_add_fusion.ids.refs_0_, f32[2,128,128]{2,1,0:T(8,128)S(1)} %get-tuple-element.37.left, f32[2,3,128,256]{3,2,1,0:T(8,128)S(1)} %get-tuple-element.38.early, f32[2,5,128,256]{3,2,1,0:T(8,128)S(1)} %get-tuple-element.46.rest, ...), custom_call_target="tpu_custom_call" | custom-call | flops 838860800 | bytes 6291456 | tf_op jit(solution)/shard_map/update/pallas_call | solution.py:36
  (47 shorter events, 3.0 us)
Async XLA Ops:
  0.6 7.3 %copy-start.1 = (f32[2,128,2048]{2,1,0:T(8,128)S(1)}, f32[2,128,2048]{2,1,0:T(8,128)}, u32[]{:S(2)}) copy-start(f32[2,128,2048]{2,1,0:T(8,128)} %momentum.1) | copy-start | bytes 6291460
  0.6 7.3 %copy-start.2 = (bf16[2,128,2048]{2,1,0:T(8,128)(2,1)S(1)}, bf16[2,128,2048]{2,1,0:T(8,128)(2,1)}, u32[]{:S(2)}) copy-start(bf16[2,128,2048]{2,1,0:T(8,128)(2,1)} %gradient.1) | copy-start | bytes 3145732
  3.3 6.2 %collective-permute-start.2 = (f32[2,128,128]{2,1,0:T(8,128)S(1)}, f32[2,128,128]{2,1,0:T(8,128)S(1)}, u32[]{:S(2)}, u32[]{:S(2)}) collective-permute-start(f32[2,128,128]{2,1,0:T(8,128)S(1)} %panel.1.p0), channel_id=1, source_target_pairs={{0,2},{1,3},{2,0},{3,1},{4,6},{5,7},{6,4},{7,5},{8,10},{9,11},{10,... | collective-permute-start | bytes 393224 | tf_op jit(solution)/shard_map/panel/ppermute | solution.py:332
  7.2 7.7 %collective-permute-start.1 = (f32[2,128,128]{2,1,0:T(8,128)S(1)}, f32[2,128,128]{2,1,0:T(8,128)S(1)}, u32[]{:S(2)}, u32[]{:S(2)}) collective-permute-start(f32[2,128,128]{2,1,0:T(8,128)S(1)} %panel.1.p0), channel_id=1, source_target_pairs={{0,3},{1,2},{2,1},{3,0},{4,7},{5,6},{6,5},{7,4},{8,11},{9,10},{10,... | collective-permute-start | bytes 393224 | tf_op jit(solution)/shard_map/panel/ppermute | solution.py:332
  7.9 6.9 %collective-permute-start = (f32[2,128,128]{2,1,0:T(8,128)S(1)}, f32[2,128,128]{2,1,0:T(8,128)S(1)}, u32[]{:S(2)}, u32[]{:S(2)}) collective-permute-start(f32[2,128,128]{2,1,0:T(8,128)S(1)} %panel.1.p0), channel_id=1, source_target_pairs={{0,1},{1,0},{2,3},{3,2},{4,5},{5,4},{6,7},{7,6},{8,9},{9,8},{10,11... | collective-permute-start | bytes 393224 | tf_op jit(solution)/shard_map/panel/ppermute | solution.py:332
  15.8 2.7 %collective-permute-start.4 = (f32[2,160,256]{2,1,0:T(8,128)S(1)}, f32[2,160,256]{2,1,0:T(8,128)S(1)}, u32[]{:S(2)}, u32[]{:S(2)}) collective-permute-start(f32[2,160,256]{2,1,0:T(8,128)S(1)} %get-tuple-element.31), channel_id=1, source_target_pairs={{0,4},{4,0},{8,12},{12,8},{16,20},{20,16},{24,28},{28,24},{32,36},... | collective-permute-start | bytes 983048 | tf_op jit(solution)/shard_map/product/ppermute | solution.py:318
  17.7 8.6 %collective-permute-start.3 = (f32[2,384,256]{2,1,0:T(8,128)S(1)}, f32[2,384,256]{2,1,0:T(8,128)S(1)}, u32[]{:S(2)}, u32[]{:S(2)}) collective-permute-start(f32[2,384,256]{2,1,0:T(8,128)S(1)} %product.6), channel_id=1, source_target_pairs={{0,4},{4,0},{8,12},{12,8},{16,20},{20,16},{24,28},{28,24},{32,36},... | collective-permute-start | bytes 2359304 | tf_op jit(solution)/shard_map/product/ppermute | solution.py:318
  18.6 6.6 %collective-permute-start.5 = (f32[160,256]{1,0:T(8,128)S(1)}, f32[160,256]{1,0:T(8,128)S(1)}, u32[]{:S(2)}, u32[]{:S(2)}) collective-permute-start(f32[160,256]{1,0:T(8,128)S(1)} %bitcast.33), channel_id=1, source_target_pairs={{0,24},{4,28},{8,16},{12,20},{16,8},{20,12},{24,0},{28,4},{32,56},... | collective-permute-start | bytes 491528 | tf_op jit(solution)/shard_map/scatter/ppermute | solution.py:323
  21.2 5.0 %collective-permute-start.7 = (f32[160,256]{1,0:T(8,128)S(1)}, f32[160,256]{1,0:T(8,128)S(1)}, u32[]{:S(2)}, u32[]{:S(2)}) collective-permute-start(f32[160,256]{1,0:T(8,128)S(1)} %bitcast.32), channel_id=1, source_target_pairs={{0,8},{4,12},{8,0},{12,4},{16,24},{20,28},{24,16},{28,20},{32,40},... | collective-permute-start | bytes 491528 | tf_op jit(solution)/shard_map/scatter/ppermute | solution.py:323
  26.5 6.9 %collective-permute-start.6 = (f32[288,256]{1,0:T(8,128)S(1)}, f32[288,256]{1,0:T(8,128)S(1)}, u32[]{:S(2)}, u32[]{:S(2)}) collective-permute-start(f32[288,256]{1,0:T(8,128)S(1)} %pad_maximum_fusion), channel_id=1, source_target_pairs={{0,8},{4,12},{8,0},{12,4},{16,24},{20,28},{24,16},{28,20},{32,40},... | collective-permute-start | bytes 884744 | tf_op jit(solution)/shard_map/scatter/ppermute | solution.py:323
  26.7 7.9 %collective-permute-start.8 = (f32[288,256]{1,0:T(8,128)S(1)}, f32[288,256]{1,0:T(8,128)S(1)}, u32[]{:S(2)}, u32[]{:S(2)}) collective-permute-start(f32[288,256]{1,0:T(8,128)S(1)} %pad_maximum_fusion.1), channel_id=1, source_target_pairs={{0,24},{4,28},{8,16},{12,20},{16,8},{20,12},{24,0},{28,4},{32,56},... | collective-permute-start | bytes 884744 | tf_op jit(solution)/shard_map/scatter/ppermute | solution.py:323
  65.3 6.2 %collective-permute-start.9 = (f32[2,32,256]{2,1,0:T(8,128)S(1)}, f32[2,32,256]{2,1,0:T(8,128)S(1)}, u32[]{:S(2)}, u32[]{:S(2)}) collective-permute-start(f32[2,32,256]{2,1,0:T(8,128)S(1)} %get-tuple-element.32.own), channel_id=1, source_target_pairs={{0,4},{4,0},{8,12},{12,8},{16,20},{20,16},{24,28},{28,24},{32,36},... | collective-permute-start | bytes 196616 | tf_op jit(solution)/shard_map/gather/ppermute | solution.py:318
  70.7 17.0 %collective-permute-start.14 = (f32[2,128,256]{2,1,0:T(8,128)S(1)}, f32[2,128,256]{2,1,0:T(8,128)S(1)}, u32[]{:S(2)}, u32[]{:S(2)}) collective-permute-start(f32[2,128,256]{2,1,0:T(8,128)S(1)} %get-tuple-element.33.a0), channel_id=1, source_target_pairs={{0,4},{4,0},{8,12},{12,8},{16,20},{20,16},{24,28},{28,24},{32,36},... | collective-permute-start | bytes 786440 | tf_op jit(solution)/shard_map/gather/ppermute | solution.py:318
  70.8 8.7 %collective-permute-start.11 = (f32[2,128,256]{2,1,0:T(8,128)S(1)}, f32[2,128,256]{2,1,0:T(8,128)S(1)}, u32[]{:S(2)}, u32[]{:S(2)}) collective-permute-start(f32[2,128,256]{2,1,0:T(8,128)S(1)} %get-tuple-element.33.a0), channel_id=1, source_target_pairs={{0,24},{4,28},{8,16},{12,20},{16,8},{20,12},{24,0},{28,4},{32,56},... | collective-permute-start | bytes 786440 | tf_op jit(solution)/shard_map/gather/ppermute | solution.py:323
  71.5 8.0 %collective-permute-start.10 = (f32[2,128,256]{2,1,0:T(8,128)S(1)}, f32[2,128,256]{2,1,0:T(8,128)S(1)}, u32[]{:S(2)}, u32[]{:S(2)}) collective-permute-start(f32[2,128,256]{2,1,0:T(8,128)S(1)} %get-tuple-element.33.a0), channel_id=1, source_target_pairs={{0,8},{4,12},{8,0},{12,4},{16,24},{20,28},{24,16},{28,20},{32,40},... | collective-permute-start | bytes 786440 | tf_op jit(solution)/shard_map/gather/ppermute | solution.py:323
  79.5 4.1 %collective-permute-start.12 = (f32[128,256]{1,0:T(8,128)S(1)}, f32[128,256]{1,0:T(8,128)S(1)}, u32[]{:S(2)}, u32[]{:S(2)}) collective-permute-start(f32[128,256]{1,0:T(8,128)S(1)} %slice_bitcast_fusion.5), channel_id=1, source_target_pairs={{0,8},{4,12},{8,0},{12,4},{16,24},{20,28},{24,16},{28,20},{32,40},... | collective-permute-start | bytes 393224 | tf_op jit(solution)/shard_map/gather/ppermute | solution.py:323
  79.6 5.1 %collective-permute-start.13 = (f32[128,256]{1,0:T(8,128)S(1)}, f32[128,256]{1,0:T(8,128)S(1)}, u32[]{:S(2)}, u32[]{:S(2)}) collective-permute-start(f32[128,256]{1,0:T(8,128)S(1)} %slice_bitcast_fusion.4), channel_id=1, source_target_pairs={{0,24},{4,28},{8,16},{12,20},{16,8},{20,12},{24,0},{28,4},{32,56},... | collective-permute-start | bytes 393224 | tf_op jit(solution)/shard_map/gather/ppermute | solution.py:323
  84.7 4.3 %collective-permute-start.15 = (f32[2,128,256]{2,1,0:T(8,128)S(1)}, f32[2,128,256]{2,1,0:T(8,128)S(1)}, u32[]{:S(2)}, u32[]{:S(2)}) collective-permute-start(f32[2,128,256]{2,1,0:T(8,128)S(1)} %collective-permute-done.10.a1), channel_id=1, source_target_pairs={{0,4},{4,0},{8,12},{12,8},{16,20},{20,16},{24,28},{28,24},{32,36},... | collective-permute-start | bytes 786440 | tf_op jit(solution)/shard_map/gather/ppermute | solution.py:318
  87.1 1.9 %collective-permute-start.16 = (f32[2,128,256]{2,1,0:T(8,128)S(1)}, f32[2,128,256]{2,1,0:T(8,128)S(1)}, u32[]{:S(2)}, u32[]{:S(2)}) collective-permute-start(f32[2,128,256]{2,1,0:T(8,128)S(1)} %collective-permute-done.11.a3), channel_id=1, source_target_pairs={{0,4},{4,0},{8,12},{12,8},{16,20},{20,16},{24,28},{28,24},{32,36},... | collective-permute-start | bytes 786440 | tf_op jit(solution)/shard_map/gather/ppermute | solution.py:318
  87.1 1.7 %collective-permute-start.17 = (f32[128,256]{1,0:T(8,128)S(1)}, f32[128,256]{1,0:T(8,128)S(1)}, u32[]{:S(2)}, u32[]{:S(2)}) collective-permute-start(f32[128,256]{1,0:T(8,128)S(1)} %collective-permute-done.12.a20), channel_id=1, source_target_pairs={{0,4},{4,0},{8,12},{12,8},{16,20},{20,16},{24,28},{28,24},{32,36},... | collective-permute-start | bytes 393224 | tf_op jit(solution)/shard_map/gather/ppermute | solution.py:318
  87.6 1.4 %collective-permute-start.18 = (f32[128,256]{1,0:T(8,128)S(1)}, f32[128,256]{1,0:T(8,128)S(1)}, u32[]{:S(2)}, u32[]{:S(2)}) collective-permute-start(f32[128,256]{1,0:T(8,128)S(1)} %collective-permute-done.13.a21), channel_id=1, source_target_pairs={{0,4},{4,0},{8,12},{12,8},{16,20},{20,16},{24,28},{28,24},{32,36},... | collective-permute-start | bytes 393224 | tf_op jit(solution)/shard_map/gather/ppermute | solution.py:318
  89.6 5.3 %collective-permute-start.21 = (f32[2,8,128]{2,1,0:T(8,128)S(1)}, f32[2,8,128]{2,1,0:T(8,128)S(1)}, u32[]{:S(2)}, u32[]{:S(2)}) collective-permute-start(f32[2,8,128]{2,1,0:T(8,128)S(1)} %get-tuple-element.49.s0), channel_id=1, source_target_pairs={{0,3},{1,2},{2,1},{3,0},{4,7},{5,6},{6,5},{7,4},{8,11},{9,10},{10,... | collective-permute-start | bytes 24584 | tf_op jit(solution)/shard_map/update/ppermute | solution.py:332
  92.1 4.0 %collective-permute-start.20 = (f32[2,8,128]{2,1,0:T(8,128)S(1)}, f32[2,8,128]{2,1,0:T(8,128)S(1)}, u32[]{:S(2)}, u32[]{:S(2)}) collective-permute-start(f32[2,8,128]{2,1,0:T(8,128)S(1)} %get-tuple-element.49.s0), channel_id=1, source_target_pairs={{0,2},{1,3},{2,0},{3,1},{4,6},{5,7},{6,4},{7,5},{8,10},{9,11},{10,... | collective-permute-start | bytes 24584 | tf_op jit(solution)/shard_map/update/ppermute | solution.py:332
  92.6 3.5 %collective-permute-start.19 = (f32[2,8,128]{2,1,0:T(8,128)S(1)}, f32[2,8,128]{2,1,0:T(8,128)S(1)}, u32[]{:S(2)}, u32[]{:S(2)}) collective-permute-start(f32[2,8,128]{2,1,0:T(8,128)S(1)} %get-tuple-element.49.s0), channel_id=1, source_target_pairs={{0,1},{1,0},{2,3},{3,2},{4,5},{5,4},{6,7},{7,6},{8,9},{9,8},{10,11... | collective-permute-start | bytes 24584 | tf_op jit(solution)/shard_map/update/ppermute | solution.py:332
  93.0 3.1 %copy-start = (f32[2,128,2048]{2,1,0:T(8,128)S(1)}, f32[2,128,2048]{2,1,0:T(8,128)}, u32[]{:S(2)}) copy-start(f32[2,128,2048]{2,1,0:T(8,128)} %weight.1) | copy-start | bytes 6291460

commit v4 on v3

--- a/solution.py
+++ b/solution.py
@@ -217,15 +217,22 @@
     return jnp.concatenate([top, bottom], axis=0)
 
 
-def wide_dot(left, b):
-    high, low = split2(b)
-    both = dot(left, jnp.concatenate([high, low], axis=0), ((1,), (0,)))
+def stacked(b):
+    return jnp.concatenate(split2(b), axis=0)
+
+
+def stacked_dot(left, b):
+    both = dot(left, b, ((1,), (0,)))
     half = both.shape[0] // 2
     return both[0:half] + both[half:]
 
 
-EARLY = [(0, 0), (0, 1), (0, 3)]
-REST = [(0, 2), (1, 0), (1, 1), (1, 3), (1, 2)]
+def wide_dot(left, b):
+    return stacked_dot(left, stacked(b))
+
+
+EARLY = [(0, 0), (0, 1), (0, 3), (1, 0)]
+REST = [(0, 2), (1, 1), (1, 3), (1, 2)]
 
 
 def spots(ids, where):
@@ -236,7 +243,7 @@
     total = jnp.zeros((R, R), F32)
     for slot, source in enumerate(sources):
         part = wide_dot(left, source)
-        reduced[layer, slot] = part
+        reduced[layer, slot] = stacked(part)
         square = part * part
         total += square[:, 0:R] + square[:, R:]
     return total
@@ -246,7 +253,7 @@
     wide = wide_left(basis * 0.05)
     copies = []
     for slot, cut in spots(ids, where):
-        staged[layer, slot] = buffer[layer, :, cut] - wide_dot(wide, reduced[layer, slot])
+        staged[layer, slot] = buffer[layer, :, cut] - stacked_dot(wide, reduced[layer, slot])
         copies.append(
             pltpu.make_async_copy(staged.at[layer, slot], new_momentum.at[layer, :, cut], sems.at[layer, slot])
         )
@@ -254,56 +261,62 @@
     return copies
 
 
-def early_kernel(ids, panel, inverse, a0, a1, a3, buffer, left, reduced, total, new_momentum, staged, sems):
+def turn(reduced, turned):
+    for layer in range(LAYERS):
+        for slot in range(4):
+            turned[layer, slot] = (reduced[layer, slot, 0:R].astype(F32) + reduced[layer, slot, R:].astype(F32)).T
+
+
+def early_kernel(
+    ids, panel, inverse, a0, a1, a3, b0, buffer, left, reduced, total, turned, new_momentum, staged, sems
+):
     copies = []
     for layer in range(LAYERS):
-        sources = [piece[layer] for piece in (a0, a1, a3)]
+        sources = [piece[layer] for piece in (a0, a1, a3, b0)]
         total[layer] = reduce_layer(wide_left(inverse[layer]), sources, reduced, layer)
         basis = lax.dot_general(
             panel[layer], inverse[layer], (((1,), (1,)), ((), ())), precision=HIGHEST, preferred_element_type=F32
         )
         left[layer] = basis
         copies += update_momentum(ids, layer, EARLY, basis, reduced, buffer, new_momentum, staged, sems)
+    turn(reduced, turned)
     for item in copies:
         item.wait()
 
 
-def rest_of_kernel(inverse, a20, a21, b0, b1, b3, b20, b21, before, reduced, squares):
+def rest_of_kernel(inverse, a20, a21, b1, b3, b20, b21, before, reduced, squares):
     for layer, (own, other) in enumerate(((a20, b20), (a21, b21))):
-        sources = [own[...], b0[layer], b1[layer], b3[layer], other[...]]
+        sources = [own[...], b1[layer], b3[layer], other[...]]
         total = before[layer] + reduce_layer(wide_left(inverse[layer]), sources, reduced, layer)
         squares[layer] = jnp.broadcast_to(jnp.sum(total.T, axis=0, keepdims=True), (8, R))
 
 
-def momentum_kernel(ids, left, early, rest, buffer, begun, new_momentum, turned, staged, sems):
+def momentum_kernel(ids, left, rest, buffer, begun, new_momentum, turned, staged, sems):
     del begun
     copies = []
     for layer in range(LAYERS):
         copies += update_momentum(ids, layer, REST, left[layer], rest, buffer, new_momentum, staged, sems)
-    for layer in range(LAYERS):
-        for where, source in ((EARLY, early), (REST, rest)):
-            for slot, cut in spots(ids, where):
-                turned[layer, cut, :] = source[layer, slot].T
+    turn(rest, turned)
     for item in copies:
         item.wait()
 
 
 def weight_kernel(
-    ids, left, early, rest, turned, s0, s1, s2, s3, weight, new_weight, new_basis, weight_v, basis_v, sems, basis_sems
+    ids, left, early, rest, turned, turned_rest, s0, s1, s2, s3, weight, new_weight, new_basis, weight_v, basis_v, sems, basis_sems
 ):
     copies = []
     for layer in range(LAYERS):
         squares = (s0[layer, 0:1, :] + s1[layer, 0:1, :]) + (s2[layer, 0:1, :] + s3[layer, 0:1, :])
         scale = lax.rsqrt(squares * (1.0 / D) + 1e-06)
         wide = wide_left(left[layer] * (scale * (0.05 * math.sqrt(D / R))))
-        for where, source in ((EARLY, early), (REST, rest)):
+        for where, source, columned in ((EARLY, early, turned), (REST, rest, turned_rest)):
             for slot, cut in spots(ids, where):
+                basis_v[layer, cut, :] = (columned[layer, slot] * scale).astype(BF16)
                 index = len(copies) - layer
-                change = wide_dot(wide, source[layer, slot])
+                change = stacked_dot(wide, source[layer, slot])
                 weight_v[index] = (1.0 - 0.05 * 0.1) * weight[layer, :, cut] - change
                 copies.append(pltpu.make_async_copy(weight_v.at[index], new_weight.at[layer, :, cut], sems.at[index]))
                 copies[-1].start()
-        basis_v[layer] = (turned[layer] * scale).astype(BF16)
         copies.append(pltpu.make_async_copy(basis_v.at[layer], new_basis.at[layer], basis_sems.at[layer]))
         copies[-1].start()
     for item in copies:
@@ -396,28 +409,30 @@
         def staging(count):
             return [pltpu.VMEM((LAYERS, count, ROWS, PIECE), F32), pltpu.SemaphoreType.DMA((LAYERS, count))]
 
-        left, early, total, new_momentum = call(
-            early_kernel,
-            (struct(LAYERS, ROWS, R), struct(LAYERS, 3, R, PIECE), struct(LAYERS, R, R), moved), [SM] + [VM] * 6,
-            (ids, panel, inverse, *group, buffer), 3 << 30, 3 << 20, scratch=staging(3), out_specs=(VM, VM, VM, HBM),
+        four, four_turned = struct(LAYERS, 4, 2 * R, PIECE, dtype=BF16), struct(LAYERS, 4, PIECE, R)
+        other = move_core(whole)
+        left, early, total, turned, new_momentum = call(
+            early_kernel, (struct(LAYERS, ROWS, R), four, struct(LAYERS, R, R), four_turned, moved), [SM] + [VM] * 7,
+            (ids, panel, inverse, *group, other, buffer), 3 << 30, 3 << 20, scratch=staging(4),
+            out_specs=(VM, VM, VM, VM, HBM),
         )
         total, *last = lax.optimization_barrier((total, *last))
         total, *group[1:] = lax.optimization_barrier((total, *group[1:]))
-        others = [move_core(item) for item in (*group, *last)]
+        others = [move_core(item) for item in (*group[1:], *last)]
     with jax.named_scope("update"):
         rest, squares = call(
-            rest_of_kernel, (struct(LAYERS, 5, R, PIECE), struct(LAYERS, 8, R)), [VM] * 9,
+            rest_of_kernel, (four, struct(LAYERS, 8, R)), [VM] * 8,
             (inverse, *last, *others, total), 1 << 30,
         )
         shares = [squares] + [move_tp(squares, flip) for flip in (1, 2, 3)]
-        new_momentum, turned = call(
-            momentum_kernel, (moved, struct(LAYERS, COLS, R)), [SM] + [VM] * 4 + [HBM],
-            (ids, left, early, rest, buffer, new_momentum), 3 << 30, 2 << 20,
-            scratch=staging(5), out_specs=(HBM, VM), aliases={5: 0},
+        new_momentum, turned_rest = call(
+            momentum_kernel, (moved, four_turned), [SM] + [VM] * 3 + [HBM],
+            (ids, left, rest, buffer, new_momentum), 3 << 30, 2 << 20,
+            scratch=staging(4), out_specs=(HBM, VM), aliases={4: 0},
         )
         new_weight, new_basis = call(
-            weight_kernel, (moved, struct(LAYERS, COLS, R, dtype=BF16)), [SM] + [VM] * 9,
-            (ids, left, early, rest, turned, *shares, weight), 800 << 20, 6 << 20,
+            weight_kernel, (moved, struct(LAYERS, COLS, R, dtype=BF16)), [SM] + [VM] * 10,
+            (ids, left, early, rest, turned, turned_rest, *shares, weight), 800 << 20, 6 << 20,
             scratch=[
                 pltpu.VMEM((16, ROWS, PIECE), F32), pltpu.VMEM((LAYERS, COLS, R), BF16),
                 pltpu.SemaphoreType.DMA((16,)), pltpu.SemaphoreType.DMA((LAYERS,)),

time: 99.1 us -> 99 us (level)
  no operation moved by 1% of the time
where the time goes in v4:
time: 99 us; the launch traced here: 98.8 us
  blocking collectives  30.6 us (31%)
  waiting for transfers between devices  23.6 us (24%)
  starting transfers between devices  23 us (23%)
  Pallas kernels  20 us (20%)
  between operations  1.04 us (1%)
    all_to_all x2, blocking collectives, swap_z(): return lax.all_to_all(a, 'fsdp', 0, 0, axis_index_groups=groups, tiled=True)  30.6 us
    pallas_call x13, Pallas kernels, call(): pl.pallas_call(kernel, out_shape=outs, in_specs=ins, out_specs=out_specs...  20 us
    ppermute x8, waiting for transfers between devices, move_x(): return lax.ppermute(a, 'fsdp', moves)  14.2 us
    ppermute x8, starting transfers between devices, move_core(): return lax.ppermute(a, 'fsdp', [(i, i ^ 1) for i in range(64)])  9.35 us
    ppermute x6, starting transfers between devices, move_tp(): return lax.ppermute(a, 'tp', [(i, i ^ flip) for i in range(4)])  7.95 us
    ppermute x6, waiting for transfers between devices, move_tp(): return lax.ppermute(a, 'tp', [(i, i ^ flip) for i in range(4)])  7.85 us
    ppermute x8, starting transfers between devices, move_x(): return lax.ppermute(a, 'fsdp', moves)  5.68 us
  transfers between devices with their start and end apart: 22, of which 12 were waited for; matrix products, arithmetic and copies ran while one was open for 0% of the time, Pallas kernels for 13%

profile of v4, /device:TPU:1, one launch (start us, length us, event | category | flops | bytes accessed | tf_op | source)
XLA Modules:
  0.0 98.8 jit_solution(16005769796633831689)
XLA Ops:
  0.7 2.7 %panel.1.p0 = f32[2,128,128]{2,1,0:T(8,128)S(1)} custom-call(f32[2,128,2048]{2,1,0:T(8,128)} %momentum.1, bf16[2,128,2048]{2,1,0:T(8,128)(2,1)} %gradient.1, bf16[2,2048,128]{2,1,0:T(8,128)(2,1)} %right.1), custom_call_target="tpu_custom_call" | custom-call | flops 314572800 | bytes 4194304 | tf_op jit(solution)/shard_map/panel/pallas_call | solution.py:36
  3.3 3.8 %collective-permute-start.2 = (f32[2,128,128]{2,1,0:T(8,128)S(1)}, f32[2,128,128]{2,1,0:T(8,128)S(1)}, u32[]{:S(2)}, u32[]{:S(2)}) collective-permute-start(f32[2,128,128]{2,1,0:T(8,128)S(1)} %panel.1.p0), channel_id=1, source_target_pairs={{0,2},{1,3},{2,0},{3,1},{4,6},{5,7},{6,4},{7,5},{8,10},{9,11},{10,... | collective-permute-start | bytes 393224 | tf_op jit(solution)/shard_map/panel/ppermute | solution.py:345
  7.2 0.8 collective-permute-start.1
  8.3 1.2 %collective-permute-done.2.p3 = f32[2,128,128]{2,1,0:T(8,128)S(1)} collective-permute-done((f32[2,128,128]{2,1,0:T(8,128)S(1)}, f32[2,128,128]{2,1,0:T(8,128)S(1)}, u32[]{:S(2)}, u32[]{:S(2)}) %collective-permute-start.2) | collective-permute-done | bytes 131104 | tf_op jit(solution)/shard_map/panel/ppermute | solution.py:345
  9.5 5.3 %collective-permute-done.1.p2 = f32[2,128,128]{2,1,0:T(8,128)S(1)} collective-permute-done((f32[2,128,128]{2,1,0:T(8,128)S(1)}, f32[2,128,128]{2,1,0:T(8,128)S(1)}, u32[]{:S(2)}, u32[]{:S(2)}) %collective-permute-start.1) | collective-permute-done | bytes 131104 | tf_op jit(solution)/shard_map/panel/ppermute | solution.py:345
  14.9 1.0 product.4
  15.8 0.9 collective-permute-start.4
  16.7 0.9 product.6
  17.8 0.8 product.7
  18.6 1.7 %collective-permute-start.5 = (f32[160,256]{1,0:T(8,128)S(1)}, f32[160,256]{1,0:T(8,128)S(1)}, u32[]{:S(2)}, u32[]{:S(2)}) collective-permute-start(f32[160,256]{1,0:T(8,128)S(1)} %bitcast.33), channel_id=1, source_target_pairs={{0,24},{4,28},{8,16},{12,20},{16,8},{20,12},{24,0},{28,4},{32,56},... | collective-permute-start | bytes 491528 | tf_op jit(solution)/shard_map/scatter/ppermute | solution.py:336
  20.3 0.9 product.5
  21.3 3.9 %collective-permute-done.5 = f32[160,256]{1,0:T(8,128)S(1)} collective-permute-done((f32[160,256]{1,0:T(8,128)S(1)}, f32[160,256]{1,0:T(8,128)S(1)}, u32[]{:S(2)}, u32[]{:S(2)}) %collective-permute-start.5) | collective-permute-done | bytes 163872 | tf_op jit(solution)/shard_map/scatter/ppermute | solution.py:336
  25.2 1.1 %collective-permute-done.7 = f32[160,256]{1,0:T(8,128)S(1)} collective-permute-done((f32[160,256]{1,0:T(8,128)S(1)}, f32[160,256]{1,0:T(8,128)S(1)}, u32[]{:S(2)}, u32[]{:S(2)}) %collective-permute-start.7) | collective-permute-done | bytes 163872 | tf_op jit(solution)/shard_map/scatter/ppermute | solution.py:336
  26.7 1.4 %collective-permute-start.8 = (f32[288,256]{1,0:T(8,128)S(1)}, f32[288,256]{1,0:T(8,128)S(1)}, u32[]{:S(2)}, u32[]{:S(2)}) collective-permute-start(f32[288,256]{1,0:T(8,128)S(1)} %pad_maximum_fusion.1), channel_id=1, source_target_pairs={{0,24},{4,28},{8,16},{12,20},{16,8},{20,12},{24,0},{28,4},{32,56},... | collective-permute-start | bytes 884744 | tf_op jit(solution)/shard_map/scatter/ppermute | solution.py:336
  28.1 5.3 %collective-permute-done.6.got1 = f32[288,256]{1,0:T(8,128)S(1)} collective-permute-done((f32[288,256]{1,0:T(8,128)S(1)}, f32[288,256]{1,0:T(8,128)S(1)}, u32[]{:S(2)}, u32[]{:S(2)}) %collective-permute-start.6) | collective-permute-done | bytes 294944 | tf_op jit(solution)/shard_map/scatter/ppermute | solution.py:336
  33.4 1.2 %collective-permute-done.8.got3 = f32[288,256]{1,0:T(8,128)S(1)} collective-permute-done((f32[288,256]{1,0:T(8,128)S(1)}, f32[288,256]{1,0:T(8,128)S(1)}, u32[]{:S(2)}, u32[]{:S(2)}) %collective-permute-start.8) | collective-permute-done | bytes 294944 | tf_op jit(solution)/shard_map/scatter/ppermute | solution.py:336
  34.7 18.1 %all_to_all.10.got = f32[8,40,256]{2,1,0:T(8,128)S(1)} all-to-all(f32[8,40,256]{2,1,0:T(8,128)S(1)} %scatter.1), channel_id=1, replica_groups={{0,32,64,96,128,160,192,224},{4,36,68,100,132,164,196,228},{8,40,72,104..., dimensions={0} | all-to-all | bytes 655360 | tf_op jit(solution)/shard_map/scatter/all_to_all | solution.py:341
  52.8 12.5 %all_to_all.11.got = f32[8,40,256]{2,1,0:T(8,128)S(1)} all-to-all(f32[8,40,256]{2,1,0:T(8,128)S(1)} %gather.4), channel_id=1, replica_groups={{0,32,64,96,128,160,192,224},{4,36,68,100,132,164,196,228},{8,40,72,104..., dimensions={0} | all-to-all | bytes 655360 | tf_op jit(solution)/shard_map/gather/all_to_all | solution.py:341
  65.3 5.3 %collective-permute-start.9 = (f32[2,32,256]{2,1,0:T(8,128)S(1)}, f32[2,32,256]{2,1,0:T(8,128)S(1)}, u32[]{:S(2)}, u32[]{:S(2)}) collective-permute-start(f32[2,32,256]{2,1,0:T(8,128)S(1)} %get-tuple-element.33.own), channel_id=1, source_target_pairs={{0,4},{4,0},{8,12},{12,8},{16,20},{20,16},{24,28},{28,24},{32,36},... | collective-permute-start | bytes 196616 | tf_op jit(solution)/shard_map/gather/ppermute | solution.py:331
  70.8 0.7 collective-permute-start.11
  71.6 5.8 %gather.6.inverse = f32[2,128,128]{2,1,0:T(8,128)S(1)} custom-call(s32[2]{0:T(128)S(1)} %pad_add_fusion.ids.refs_0_, f32[2,32,256]{2,1,0:T(8,128)S(1)} %get-tuple-element.33.own, f32[2,32,256]{2,1,0:T(8,128)S(1)} %collective-permute-done.9.other), custom_call_target="tpu_custom_call" | custom-call | flops 8589934592 | bytes 1048576 | tf_op jit(solution)/shard_map/gather/pallas_call | solution.py:36
  77.4 2.1 %collective-permute-done.11.a3 = f32[2,128,256]{2,1,0:T(8,128)S(1)} collective-permute-done((f32[2,128,256]{2,1,0:T(8,128)S(1)}, f32[2,128,256]{2,1,0:T(8,128)S(1)}, u32[]{:S(2)}, u32[]{:S(2)}) %collective-permute-start.11) | collective-permute-done | bytes 262176 | tf_op jit(solution)/shard_map/gather/ppermute | solution.py:336
  79.6 1.5 %collective-permute-start.14 = (f32[128,256]{1,0:T(8,128)S(1)}, f32[128,256]{1,0:T(8,128)S(1)}, u32[]{:S(2)}, u32[]{:S(2)}) collective-permute-start(f32[128,256]{1,0:T(8,128)S(1)} %slice_bitcast_fusion.4), channel_id=1, source_target_pairs={{0,24},{4,28},{8,16},{12,20},{16,8},{20,12},{24,0},{28,4},{32,56},... | collective-permute-start | bytes 393224 | tf_op jit(solution)/shard_map/gather/ppermute | solution.py:336
  81.1 2.8 %gather.7 = (f32[2,128,128]{2,1,0:T(8,128)S(1)}, bf16[2,4,256,256]{3,2,1,0:T(8,128)(2,1)S(1)}, f32[2,128,128]{2,1,0:T(8,128)S(1)}, f32[2,4,256,128]{3,2,1,0:T(8,128)S(1)}, f32[2,128,2048]{2,1,0:T(8,128)}) custom-call(s32[2]{0:T(128)S(1)} %pad_add_fusion.ids.refs_0_, f32[2,128,128]{2,1,0:T(8,128)S(1)} %get-tuple-element.29.panel, ...), custom_call_target="tpu_custom_call" | custom-call | flops 3221225472 | bytes 3145728 | tf_op jit(solution)/shard_map/gather/pallas_call | solution.py:36
  84.0 0.7 collective-permute-done.14.a21
  84.7 2.4 %collective-permute-start.15 = (f32[2,128,256]{2,1,0:T(8,128)S(1)}, f32[2,128,256]{2,1,0:T(8,128)S(1)}, u32[]{:S(2)}, u32[]{:S(2)}) collective-permute-start(f32[2,128,256]{2,1,0:T(8,128)S(1)} %collective-permute-done.10.a1), channel_id=1, source_target_pairs={{0,4},{4,0},{8,12},{12,8},{16,20},{20,16},{24,28},{28,24},{32,36},... | collective-permute-start | bytes 786440 | tf_op jit(solution)/shard_map/gather/ppermute | solution.py:331
  87.6 1.2 %collective-permute-done.17.b20 = f32[128,256]{1,0:T(8,128)S(1)} collective-permute-done((f32[128,256]{1,0:T(8,128)S(1)}, f32[128,256]{1,0:T(8,128)S(1)}, u32[]{:S(2)}, u32[]{:S(2)}) %collective-permute-start.17) | collective-permute-done | bytes 131104 | tf_op jit(solution)/shard_map/gather/ppermute | solution.py:331
  89.0 0.6 update.3
  89.6 2.5 %collective-permute-start.21 = (f32[2,8,128]{2,1,0:T(8,128)S(1)}, f32[2,8,128]{2,1,0:T(8,128)S(1)}, u32[]{:S(2)}, u32[]{:S(2)}) collective-permute-start(f32[2,8,128]{2,1,0:T(8,128)S(1)} %get-tuple-element.51.s0), channel_id=1, source_target_pairs={{0,3},{1,2},{2,1},{3,0},{4,7},{5,6},{6,5},{7,4},{8,11},{9,10},{10,... | collective-permute-start | bytes 24584 | tf_op jit(solution)/shard_map/update/ppermute | solution.py:345
  92.9 1.8 %update.4 = (f32[2,128,2048]{2,1,0:T(8,128)}, f32[2,4,256,128]{3,2,1,0:T(8,128)S(1)}) custom-call(s32[2]{0:T(128)S(1)} %pad_add_fusion.ids.refs_0_, f32[2,128,128]{2,1,0:T(8,128)S(1)} %get-tuple-element.38.left, bf16[2,4,256,256]{3,2,1,0:T(8,128)(2,1)S(1)} %get-tuple-element.47.rest, ...), custom_call_target="tpu_custom_call", output_to_operand_aliasing={{0}: (4, {})} | custom-call | flops 3221225472 | bytes 2097152 | tf_op jit(solution)/shard_map/update/pallas_call | solution.py:36
  94.7 1.3 %collective-permute-done.20.s2 = f32[2,8,128]{2,1,0:T(8,128)S(1)} collective-permute-done((f32[2,8,128]{2,1,0:T(8,128)S(1)}, f32[2,8,128]{2,1,0:T(8,128)S(1)}, u32[]{:S(2)}, u32[]{:S(2)}) %collective-permute-start.20) | collective-permute-done | bytes 8224 | tf_op jit(solution)/shard_map/update/ppermute | solution.py:345
  96.0 2.6 %update.5 = (f32[2,128,2048]{2,1,0:T(8,128)}, bf16[2,2048,128]{2,1,0:T(8,128)(2,1)}) custom-call(s32[2]{0:T(128)S(1)} %pad_add_fusion.ids.refs_0_, f32[2,128,128]{2,1,0:T(8,128)S(1)} %get-tuple-element.38.left, bf16[2,4,256,256]{3,2,1,0:T(8,128)(2,1)S(1)} %get-tuple-element.39.early, bf16[2,4,256,256]{3,2,1,0:T(8,128)(2,1)S(1)} %get-tuple-element.47.rest, ...), custom_call_target="tpu_custom_call" | custom-call | flops 838860800 | bytes 6291456 | tf_op jit(solution)/shard_map/update/pallas_call | solution.py:36
  (47 shorter events, 3.0 us)
Async XLA Ops:
  0.6 7.3 %copy-start.1 = (f32[2,128,2048]{2,1,0:T(8,128)S(1)}, f32[2,128,2048]{2,1,0:T(8,128)}, u32[]{:S(2)}) copy-start(f32[2,128,2048]{2,1,0:T(8,128)} %momentum.1) | copy-start | bytes 6291460
  0.6 7.3 %copy-start.2 = (bf16[2,128,2048]{2,1,0:T(8,128)(2,1)S(1)}, bf16[2,128,2048]{2,1,0:T(8,128)(2,1)}, u32[]{:S(2)}) copy-start(bf16[2,128,2048]{2,1,0:T(8,128)(2,1)} %gradient.1) | copy-start | bytes 3145732
  3.3 6.2 %collective-permute-start.2 = (f32[2,128,128]{2,1,0:T(8,128)S(1)}, f32[2,128,128]{2,1,0:T(8,128)S(1)}, u32[]{:S(2)}, u32[]{:S(2)}) collective-permute-start(f32[2,128,128]{2,1,0:T(8,128)S(1)} %panel.1.p0), channel_id=1, source_target_pairs={{0,2},{1,3},{2,0},{3,1},{4,6},{5,7},{6,4},{7,5},{8,10},{9,11},{10,... | collective-permute-start | bytes 393224 | tf_op jit(solution)/shard_map/panel/ppermute | solution.py:345
  7.2 7.7 %collective-permute-start.1 = (f32[2,128,128]{2,1,0:T(8,128)S(1)}, f32[2,128,128]{2,1,0:T(8,128)S(1)}, u32[]{:S(2)}, u32[]{:S(2)}) collective-permute-start(f32[2,128,128]{2,1,0:T(8,128)S(1)} %panel.1.p0), channel_id=1, source_target_pairs={{0,3},{1,2},{2,1},{3,0},{4,7},{5,6},{6,5},{7,4},{8,11},{9,10},{10,... | collective-permute-start | bytes 393224 | tf_op jit(solution)/shard_map/panel/ppermute | solution.py:345
  7.9 6.9 %collective-permute-start = (f32[2,128,128]{2,1,0:T(8,128)S(1)}, f32[2,128,128]{2,1,0:T(8,128)S(1)}, u32[]{:S(2)}, u32[]{:S(2)}) collective-permute-start(f32[2,128,128]{2,1,0:T(8,128)S(1)} %panel.1.p0), channel_id=1, source_target_pairs={{0,1},{1,0},{2,3},{3,2},{4,5},{5,4},{6,7},{7,6},{8,9},{9,8},{10,11... | collective-permute-start | bytes 393224 | tf_op jit(solution)/shard_map/panel/ppermute | solution.py:345
  15.8 2.7 %collective-permute-start.4 = (f32[2,160,256]{2,1,0:T(8,128)S(1)}, f32[2,160,256]{2,1,0:T(8,128)S(1)}, u32[]{:S(2)}, u32[]{:S(2)}) collective-permute-start(f32[2,160,256]{2,1,0:T(8,128)S(1)} %get-tuple-element.32), channel_id=1, source_target_pairs={{0,4},{4,0},{8,12},{12,8},{16,20},{20,16},{24,28},{28,24},{32,36},... | collective-permute-start | bytes 983048 | tf_op jit(solution)/shard_map/product/ppermute | solution.py:331
  17.7 8.6 %collective-permute-start.3 = (f32[2,384,256]{2,1,0:T(8,128)S(1)}, f32[2,384,256]{2,1,0:T(8,128)S(1)}, u32[]{:S(2)}, u32[]{:S(2)}) collective-permute-start(f32[2,384,256]{2,1,0:T(8,128)S(1)} %product.6), channel_id=1, source_target_pairs={{0,4},{4,0},{8,12},{12,8},{16,20},{20,16},{24,28},{28,24},{32,36},... | collective-permute-start | bytes 2359304 | tf_op jit(solution)/shard_map/product/ppermute | solution.py:331
  18.6 6.6 %collective-permute-start.5 = (f32[160,256]{1,0:T(8,128)S(1)}, f32[160,256]{1,0:T(8,128)S(1)}, u32[]{:S(2)}, u32[]{:S(2)}) collective-permute-start(f32[160,256]{1,0:T(8,128)S(1)} %bitcast.33), channel_id=1, source_target_pairs={{0,24},{4,28},{8,16},{12,20},{16,8},{20,12},{24,0},{28,4},{32,56},... | collective-permute-start | bytes 491528 | tf_op jit(solution)/shard_map/scatter/ppermute | solution.py:336
  21.2 5.0 %collective-permute-start.7 = (f32[160,256]{1,0:T(8,128)S(1)}, f32[160,256]{1,0:T(8,128)S(1)}, u32[]{:S(2)}, u32[]{:S(2)}) collective-permute-start(f32[160,256]{1,0:T(8,128)S(1)} %bitcast.32), channel_id=1, source_target_pairs={{0,8},{4,12},{8,0},{12,4},{16,24},{20,28},{24,16},{28,20},{32,40},... | collective-permute-start | bytes 491528 | tf_op jit(solution)/shard_map/scatter/ppermute | solution.py:336
  26.5 6.9 %collective-permute-start.6 = (f32[288,256]{1,0:T(8,128)S(1)}, f32[288,256]{1,0:T(8,128)S(1)}, u32[]{:S(2)}, u32[]{:S(2)}) collective-permute-start(f32[288,256]{1,0:T(8,128)S(1)} %pad_maximum_fusion), channel_id=1, source_target_pairs={{0,8},{4,12},{8,0},{12,4},{16,24},{20,28},{24,16},{28,20},{32,40},... | collective-permute-start | bytes 884744 | tf_op jit(solution)/shard_map/scatter/ppermute | solution.py:336
  26.7 7.9 %collective-permute-start.8 = (f32[288,256]{1,0:T(8,128)S(1)}, f32[288,256]{1,0:T(8,128)S(1)}, u32[]{:S(2)}, u32[]{:S(2)}) collective-permute-start(f32[288,256]{1,0:T(8,128)S(1)} %pad_maximum_fusion.1), channel_id=1, source_target_pairs={{0,24},{4,28},{8,16},{12,20},{16,8},{20,12},{24,0},{28,4},{32,56},... | collective-permute-start | bytes 884744 | tf_op jit(solution)/shard_map/scatter/ppermute | solution.py:336
  65.3 6.2 %collective-permute-start.9 = (f32[2,32,256]{2,1,0:T(8,128)S(1)}, f32[2,32,256]{2,1,0:T(8,128)S(1)}, u32[]{:S(2)}, u32[]{:S(2)}) collective-permute-start(f32[2,32,256]{2,1,0:T(8,128)S(1)} %get-tuple-element.33.own), channel_id=1, source_target_pairs={{0,4},{4,0},{8,12},{12,8},{16,20},{20,16},{24,28},{28,24},{32,36},... | collective-permute-start | bytes 196616 | tf_op jit(solution)/shard_map/gather/ppermute | solution.py:331
  70.7 10.5 %collective-permute-start.12 = (f32[2,128,256]{2,1,0:T(8,128)S(1)}, f32[2,128,256]{2,1,0:T(8,128)S(1)}, u32[]{:S(2)}, u32[]{:S(2)}) collective-permute-start(f32[2,128,256]{2,1,0:T(8,128)S(1)} %get-tuple-element.34.a0), channel_id=1, source_target_pairs={{0,4},{4,0},{8,12},{12,8},{16,20},{20,16},{24,28},{28,24},{32,36},... | collective-permute-start | bytes 786440 | tf_op jit(solution)/shard_map/gather/ppermute | solution.py:331
  70.8 8.7 %collective-permute-start.11 = (f32[2,128,256]{2,1,0:T(8,128)S(1)}, f32[2,128,256]{2,1,0:T(8,128)S(1)}, u32[]{:S(2)}, u32[]{:S(2)}) collective-permute-start(f32[2,128,256]{2,1,0:T(8,128)S(1)} %get-tuple-element.34.a0), channel_id=1, source_target_pairs={{0,24},{4,28},{8,16},{12,20},{16,8},{20,12},{24,0},{28,4},{32,56},... | collective-permute-start | bytes 786440 | tf_op jit(solution)/shard_map/gather/ppermute | solution.py:336
  71.5 8.0 %collective-permute-start.10 = (f32[2,128,256]{2,1,0:T(8,128)S(1)}, f32[2,128,256]{2,1,0:T(8,128)S(1)}, u32[]{:S(2)}, u32[]{:S(2)}) collective-permute-start(f32[2,128,256]{2,1,0:T(8,128)S(1)} %get-tuple-element.34.a0), channel_id=1, source_target_pairs={{0,8},{4,12},{8,0},{12,4},{16,24},{20,28},{24,16},{28,20},{32,40},... | collective-permute-start | bytes 786440 | tf_op jit(solution)/shard_map/gather/ppermute | solution.py:336
  79.5 4.5 %collective-permute-start.13 = (f32[128,256]{1,0:T(8,128)S(1)}, f32[128,256]{1,0:T(8,128)S(1)}, u32[]{:S(2)}, u32[]{:S(2)}) collective-permute-start(f32[128,256]{1,0:T(8,128)S(1)} %slice_bitcast_fusion.5), channel_id=1, source_target_pairs={{0,8},{4,12},{8,0},{12,4},{16,24},{20,28},{24,16},{28,20},{32,40},... | collective-permute-start | bytes 393224 | tf_op jit(solution)/shard_map/gather/ppermute | solution.py:336
  79.6 5.1 %collective-permute-start.14 = (f32[128,256]{1,0:T(8,128)S(1)}, f32[128,256]{1,0:T(8,128)S(1)}, u32[]{:S(2)}, u32[]{:S(2)}) collective-permute-start(f32[128,256]{1,0:T(8,128)S(1)} %slice_bitcast_fusion.4), channel_id=1, source_target_pairs={{0,24},{4,28},{8,16},{12,20},{16,8},{20,12},{24,0},{28,4},{32,56},... | collective-permute-start | bytes 393224 | tf_op jit(solution)/shard_map/gather/ppermute | solution.py:336
  84.7 4.3 %collective-permute-start.15 = (f32[2,128,256]{2,1,0:T(8,128)S(1)}, f32[2,128,256]{2,1,0:T(8,128)S(1)}, u32[]{:S(2)}, u32[]{:S(2)}) collective-permute-start(f32[2,128,256]{2,1,0:T(8,128)S(1)} %collective-permute-done.10.a1), channel_id=1, source_target_pairs={{0,4},{4,0},{8,12},{12,8},{16,20},{20,16},{24,28},{28,24},{32,36},... | collective-permute-start | bytes 786440 | tf_op jit(solution)/shard_map/gather/ppermute | solution.py:331
  87.1 1.9 %collective-permute-start.16 = (f32[2,128,256]{2,1,0:T(8,128)S(1)}, f32[2,128,256]{2,1,0:T(8,128)S(1)}, u32[]{:S(2)}, u32[]{:S(2)}) collective-permute-start(f32[2,128,256]{2,1,0:T(8,128)S(1)} %collective-permute-done.11.a3), channel_id=1, source_target_pairs={{0,4},{4,0},{8,12},{12,8},{16,20},{20,16},{24,28},{28,24},{32,36},... | collective-permute-start | bytes 786440 | tf_op jit(solution)/shard_map/gather/ppermute | solution.py:331
  87.1 1.7 %collective-permute-start.17 = (f32[128,256]{1,0:T(8,128)S(1)}, f32[128,256]{1,0:T(8,128)S(1)}, u32[]{:S(2)}, u32[]{:S(2)}) collective-permute-start(f32[128,256]{1,0:T(8,128)S(1)} %collective-permute-done.13.a20), channel_id=1, source_target_pairs={{0,4},{4,0},{8,12},{12,8},{16,20},{20,16},{24,28},{28,24},{32,36},... | collective-permute-start | bytes 393224 | tf_op jit(solution)/shard_map/gather/ppermute | solution.py:331
  87.6 1.4 %collective-permute-start.18 = (f32[128,256]{1,0:T(8,128)S(1)}, f32[128,256]{1,0:T(8,128)S(1)}, u32[]{:S(2)}, u32[]{:S(2)}) collective-permute-start(f32[128,256]{1,0:T(8,128)S(1)} %collective-permute-done.14.a21), channel_id=1, source_target_pairs={{0,4},{4,0},{8,12},{12,8},{16,20},{20,16},{24,28},{28,24},{32,36},... | collective-permute-start | bytes 393224 | tf_op jit(solution)/shard_map/gather/ppermute | solution.py:331
  89.6 5.2 %collective-permute-start.21 = (f32[2,8,128]{2,1,0:T(8,128)S(1)}, f32[2,8,128]{2,1,0:T(8,128)S(1)}, u32[]{:S(2)}, u32[]{:S(2)}) collective-permute-start(f32[2,8,128]{2,1,0:T(8,128)S(1)} %get-tuple-element.51.s0), channel_id=1, source_target_pairs={{0,3},{1,2},{2,1},{3,0},{4,7},{5,6},{6,5},{7,4},{8,11},{9,10},{10,... | collective-permute-start | bytes 24584 | tf_op jit(solution)/shard_map/update/ppermute | solution.py:345
  92.0 4.0 %collective-permute-start.20 = (f32[2,8,128]{2,1,0:T(8,128)S(1)}, f32[2,8,128]{2,1,0:T(8,128)S(1)}, u32[]{:S(2)}, u32[]{:S(2)}) collective-permute-start(f32[2,8,128]{2,1,0:T(8,128)S(1)} %get-tuple-element.51.s0), channel_id=1, source_target_pairs={{0,2},{1,3},{2,0},{3,1},{4,6},{5,7},{6,4},{7,5},{8,10},{9,11},{10,... | collective-permute-start | bytes 24584 | tf_op jit(solution)/shard_map/update/ppermute | solution.py:345
  92.5 3.5 %collective-permute-start.19 = (f32[2,8,128]{2,1,0:T(8,128)S(1)}, f32[2,8,128]{2,1,0:T(8,128)S(1)}, u32[]{:S(2)}, u32[]{:S(2)}) collective-permute-start(f32[2,8,128]{2,1,0:T(8,128)S(1)} %get-tuple-element.51.s0), channel_id=1, source_target_pairs={{0,1},{1,0},{2,3},{3,2},{4,5},{5,4},{6,7},{7,6},{8,9},{9,8},{10,11... | collective-permute-start | bytes 24584 | tf_op jit(solution)/shard_map/update/ppermute | solution.py:345
  92.9 3.1 %copy-start = (f32[2,128,2048]{2,1,0:T(8,128)S(1)}, f32[2,128,2048]{2,1,0:T(8,128)}, u32[]{:S(2)}) copy-start(f32[2,128,2048]{2,1,0:T(8,128)} %weight.1) | copy-start | bytes 6291460

commit v5 on v4

--- a/solution.py
+++ b/solution.py
@@ -109,7 +109,10 @@
 
 
 def gram_of(panel):
-    return lax.dot_general(panel, panel, (((0,), (0,)), ((), ())), precision=HIGHEST, preferred_element_type=F32)
+    high, mid, low = split3(panel)
+    left = jnp.concatenate([high, mid, high, mid, low, high], axis=0)
+    right = jnp.concatenate([high, high, mid, mid, high, low], axis=0)
+    return dot(left, right, ((0,), (0,)))
 
 
 def product(ids, core, rels, lefts, buffer, out):

time: 99 us -> 98.9 us (level)
  transfers between devices with their start and end apart: 22 -> 22, of which waited for: 12 -> 11; matrix products, arithmetic and copies ran while one was open for 0% -> 0% of each run, Pallas kernels for 13% -> 13%
where the time goes in v5:
time: 98.9 us; the launch traced here: 98.8 us
  blocking collectives  30.5 us (31%)
  waiting for transfers between devices  23.6 us (24%)
  starting transfers between devices  23 us (23%)
  Pallas kernels  20 us (20%)
  between operations  1.04 us (1%)
    all_to_all x2, blocking collectives, swap_z(): return lax.all_to_all(a, 'fsdp', 0, 0, axis_index_groups=groups, tiled=True)  30.5 us
    pallas_call x13, Pallas kernels, call(): pl.pallas_call(kernel, out_shape=outs, in_specs=ins, out_specs=out_specs...  20 us
    ppermute x8, waiting for transfers between devices, move_x(): return lax.ppermute(a, 'fsdp', moves)  14.3 us
    ppermute x8, starting transfers between devices, move_core(): return lax.ppermute(a, 'fsdp', [(i, i ^ 1) for i in range(64)])  9.36 us
    ppermute x6, starting transfers between devices, move_tp(): return lax.ppermute(a, 'tp', [(i, i ^ flip) for i in range(4)])  7.95 us
    ppermute x6, waiting for transfers between devices, move_tp(): return lax.ppermute(a, 'tp', [(i, i ^ flip) for i in range(4)])  7.88 us
    ppermute x8, starting transfers between devices, move_x(): return lax.ppermute(a, 'fsdp', moves)  5.71 us
  transfers between devices with their start and end apart: 22, of which 11 were waited for; matrix products, arithmetic and copies ran while one was open for 0% of the time, Pallas kernels for 13%

profile of v5, /device:TPU:1, one launch (start us, length us, event | category | flops | bytes accessed | tf_op | source)
XLA Modules:
  0.0 98.8 jit_solution(17599905735845837792)
XLA Ops:
  0.7 2.7 %panel.1.p0 = f32[2,128,128]{2,1,0:T(8,128)S(1)} custom-call(f32[2,128,2048]{2,1,0:T(8,128)} %momentum.1, bf16[2,128,2048]{2,1,0:T(8,128)(2,1)} %gradient.1, bf16[2,2048,128]{2,1,0:T(8,128)(2,1)} %right.1), custom_call_target="tpu_custom_call" | custom-call | flops 314572800 | bytes 4194304 | tf_op jit(solution)/shard_map/panel/pallas_call | solution.py:36
  3.3 3.8 %collective-permute-start.2 = (f32[2,128,128]{2,1,0:T(8,128)S(1)}, f32[2,128,128]{2,1,0:T(8,128)S(1)}, u32[]{:S(2)}, u32[]{:S(2)}) collective-permute-start(f32[2,128,128]{2,1,0:T(8,128)S(1)} %panel.1.p0), channel_id=1, source_target_pairs={{0,2},{1,3},{2,0},{3,1},{4,6},{5,7},{6,4},{7,5},{8,10},{9,11},{10,... | collective-permute-start | bytes 393224 | tf_op jit(solution)/shard_map/panel/ppermute | solution.py:348
  7.2 0.8 collective-permute-start.1
  8.3 1.2 %collective-permute-done.2.p3 = f32[2,128,128]{2,1,0:T(8,128)S(1)} collective-permute-done((f32[2,128,128]{2,1,0:T(8,128)S(1)}, f32[2,128,128]{2,1,0:T(8,128)S(1)}, u32[]{:S(2)}, u32[]{:S(2)}) %collective-permute-start.2) | collective-permute-done | bytes 131104 | tf_op jit(solution)/shard_map/panel/ppermute | solution.py:348
  9.5 5.3 %collective-permute-done.1.p2 = f32[2,128,128]{2,1,0:T(8,128)S(1)} collective-permute-done((f32[2,128,128]{2,1,0:T(8,128)S(1)}, f32[2,128,128]{2,1,0:T(8,128)S(1)}, u32[]{:S(2)}, u32[]{:S(2)}) %collective-permute-start.1) | collective-permute-done | bytes 131104 | tf_op jit(solution)/shard_map/panel/ppermute | solution.py:348
  14.9 0.9 product.4
  15.8 0.9 collective-permute-start.4
  16.7 0.9 product.6
  17.7 0.8 product.7
  18.6 1.7 %collective-permute-start.5 = (f32[160,256]{1,0:T(8,128)S(1)}, f32[160,256]{1,0:T(8,128)S(1)}, u32[]{:S(2)}, u32[]{:S(2)}) collective-permute-start(f32[160,256]{1,0:T(8,128)S(1)} %bitcast.33), channel_id=1, source_target_pairs={{0,24},{4,28},{8,16},{12,20},{16,8},{20,12},{24,0},{28,4},{32,56},... | collective-permute-start | bytes 491528 | tf_op jit(solution)/shard_map/scatter/ppermute | solution.py:339
  20.3 0.9 product.5
  21.3 3.8 %collective-permute-done.5 = f32[160,256]{1,0:T(8,128)S(1)} collective-permute-done((f32[160,256]{1,0:T(8,128)S(1)}, f32[160,256]{1,0:T(8,128)S(1)}, u32[]{:S(2)}, u32[]{:S(2)}) %collective-permute-start.5) | collective-permute-done | bytes 163872 | tf_op jit(solution)/shard_map/scatter/ppermute | solution.py:339
  25.2 1.1 %collective-permute-done.7 = f32[160,256]{1,0:T(8,128)S(1)} collective-permute-done((f32[160,256]{1,0:T(8,128)S(1)}, f32[160,256]{1,0:T(8,128)S(1)}, u32[]{:S(2)}, u32[]{:S(2)}) %collective-permute-start.7) | collective-permute-done | bytes 163872 | tf_op jit(solution)/shard_map/scatter/ppermute | solution.py:339
  26.7 1.4 %collective-permute-start.8 = (f32[288,256]{1,0:T(8,128)S(1)}, f32[288,256]{1,0:T(8,128)S(1)}, u32[]{:S(2)}, u32[]{:S(2)}) collective-permute-start(f32[288,256]{1,0:T(8,128)S(1)} %pad_maximum_fusion.1), channel_id=1, source_target_pairs={{0,24},{4,28},{8,16},{12,20},{16,8},{20,12},{24,0},{28,4},{32,56},... | collective-permute-start | bytes 884744 | tf_op jit(solution)/shard_map/scatter/ppermute | solution.py:339
  28.1 5.3 %collective-permute-done.6.got1 = f32[288,256]{1,0:T(8,128)S(1)} collective-permute-done((f32[288,256]{1,0:T(8,128)S(1)}, f32[288,256]{1,0:T(8,128)S(1)}, u32[]{:S(2)}, u32[]{:S(2)}) %collective-permute-start.6) | collective-permute-done | bytes 294944 | tf_op jit(solution)/shard_map/scatter/ppermute | solution.py:339
  33.4 1.2 %collective-permute-done.8.got3 = f32[288,256]{1,0:T(8,128)S(1)} collective-permute-done((f32[288,256]{1,0:T(8,128)S(1)}, f32[288,256]{1,0:T(8,128)S(1)}, u32[]{:S(2)}, u32[]{:S(2)}) %collective-permute-start.8) | collective-permute-done | bytes 294944 | tf_op jit(solution)/shard_map/scatter/ppermute | solution.py:339
  34.7 18.0 %all_to_all.10.got = f32[8,40,256]{2,1,0:T(8,128)S(1)} all-to-all(f32[8,40,256]{2,1,0:T(8,128)S(1)} %scatter.1), channel_id=1, replica_groups={{0,32,64,96,128,160,192,224},{4,36,68,100,132,164,196,228},{8,40,72,104..., dimensions={0} | all-to-all | bytes 655360 | tf_op jit(solution)/shard_map/scatter/all_to_all | solution.py:344
  52.7 12.5 %all_to_all.11.got = f32[8,40,256]{2,1,0:T(8,128)S(1)} all-to-all(f32[8,40,256]{2,1,0:T(8,128)S(1)} %gather.4), channel_id=1, replica_groups={{0,32,64,96,128,160,192,224},{4,36,68,100,132,164,196,228},{8,40,72,104..., dimensions={0} | all-to-all | bytes 655360 | tf_op jit(solution)/shard_map/gather/all_to_all | solution.py:344
  65.2 5.3 %collective-permute-start.9 = (f32[2,32,256]{2,1,0:T(8,128)S(1)}, f32[2,32,256]{2,1,0:T(8,128)S(1)}, u32[]{:S(2)}, u32[]{:S(2)}) collective-permute-start(f32[2,32,256]{2,1,0:T(8,128)S(1)} %get-tuple-element.33.own), channel_id=1, source_target_pairs={{0,4},{4,0},{8,12},{12,8},{16,20},{20,16},{24,28},{28,24},{32,36},... | collective-permute-start | bytes 196616 | tf_op jit(solution)/shard_map/gather/ppermute | solution.py:334
  70.7 0.8 collective-permute-start.11
  71.5 5.8 %gather.6.inverse = f32[2,128,128]{2,1,0:T(8,128)S(1)} custom-call(s32[2]{0:T(128)S(1)} %pad_add_fusion.ids.refs_0_, f32[2,32,256]{2,1,0:T(8,128)S(1)} %get-tuple-element.33.own, f32[2,32,256]{2,1,0:T(8,128)S(1)} %collective-permute-done.9.other), custom_call_target="tpu_custom_call" | custom-call | flops 8589934592 | bytes 1048576 | tf_op jit(solution)/shard_map/gather/pallas_call | solution.py:36
  77.3 2.1 %collective-permute-done.11.a3 = f32[2,128,256]{2,1,0:T(8,128)S(1)} collective-permute-done((f32[2,128,256]{2,1,0:T(8,128)S(1)}, f32[2,128,256]{2,1,0:T(8,128)S(1)}, u32[]{:S(2)}, u32[]{:S(2)}) %collective-permute-start.11) | collective-permute-done | bytes 262176 | tf_op jit(solution)/shard_map/gather/ppermute | solution.py:339
  79.5 1.5 %collective-permute-start.14 = (f32[128,256]{1,0:T(8,128)S(1)}, f32[128,256]{1,0:T(8,128)S(1)}, u32[]{:S(2)}, u32[]{:S(2)}) collective-permute-start(f32[128,256]{1,0:T(8,128)S(1)} %slice_bitcast_fusion.4), channel_id=1, source_target_pairs={{0,24},{4,28},{8,16},{12,20},{16,8},{20,12},{24,0},{28,4},{32,56},... | collective-permute-start | bytes 393224 | tf_op jit(solution)/shard_map/gather/ppermute | solution.py:339
  81.0 2.8 %gather.7 = (f32[2,128,128]{2,1,0:T(8,128)S(1)}, bf16[2,4,256,256]{3,2,1,0:T(8,128)(2,1)S(1)}, f32[2,128,128]{2,1,0:T(8,128)S(1)}, f32[2,4,256,128]{3,2,1,0:T(8,128)S(1)}, f32[2,128,2048]{2,1,0:T(8,128)}) custom-call(s32[2]{0:T(128)S(1)} %pad_add_fusion.ids.refs_0_, f32[2,128,128]{2,1,0:T(8,128)S(1)} %get-tuple-element.29.panel, ...), custom_call_target="tpu_custom_call" | custom-call | flops 3221225472 | bytes 3145728 | tf_op jit(solution)/shard_map/gather/pallas_call | solution.py:36
  83.9 0.7 collective-permute-done.14.a21
  84.6 2.4 %collective-permute-start.15 = (f32[2,128,256]{2,1,0:T(8,128)S(1)}, f32[2,128,256]{2,1,0:T(8,128)S(1)}, u32[]{:S(2)}, u32[]{:S(2)}) collective-permute-start(f32[2,128,256]{2,1,0:T(8,128)S(1)} %collective-permute-done.10.a1), channel_id=1, source_target_pairs={{0,4},{4,0},{8,12},{12,8},{16,20},{20,16},{24,28},{28,24},{32,36},... | collective-permute-start | bytes 786440 | tf_op jit(solution)/shard_map/gather/ppermute | solution.py:334
  87.5 1.2 %collective-permute-done.17.b20 = f32[128,256]{1,0:T(8,128)S(1)} collective-permute-done((f32[128,256]{1,0:T(8,128)S(1)}, f32[128,256]{1,0:T(8,128)S(1)}, u32[]{:S(2)}, u32[]{:S(2)}) %collective-permute-start.17) | collective-permute-done | bytes 131104 | tf_op jit(solution)/shard_map/gather/ppermute | solution.py:334
  88.9 0.6 update.3
  89.5 2.5 %collective-permute-start.21 = (f32[2,8,128]{2,1,0:T(8,128)S(1)}, f32[2,8,128]{2,1,0:T(8,128)S(1)}, u32[]{:S(2)}, u32[]{:S(2)}) collective-permute-start(f32[2,8,128]{2,1,0:T(8,128)S(1)} %get-tuple-element.51.s0), channel_id=1, source_target_pairs={{0,3},{1,2},{2,1},{3,0},{4,7},{5,6},{6,5},{7,4},{8,11},{9,10},{10,... | collective-permute-start | bytes 24584 | tf_op jit(solution)/shard_map/update/ppermute | solution.py:348
  92.8 1.8 %update.4 = (f32[2,128,2048]{2,1,0:T(8,128)}, f32[2,4,256,128]{3,2,1,0:T(8,128)S(1)}) custom-call(s32[2]{0:T(128)S(1)} %pad_add_fusion.ids.refs_0_, f32[2,128,128]{2,1,0:T(8,128)S(1)} %get-tuple-element.38.left, bf16[2,4,256,256]{3,2,1,0:T(8,128)(2,1)S(1)} %get-tuple-element.47.rest, ...), custom_call_target="tpu_custom_call", output_to_operand_aliasing={{0}: (4, {})} | custom-call | flops 3221225472 | bytes 2097152 | tf_op jit(solution)/shard_map/update/pallas_call | solution.py:36
  94.7 1.3 %collective-permute-done.20.s2 = f32[2,8,128]{2,1,0:T(8,128)S(1)} collective-permute-done((f32[2,8,128]{2,1,0:T(8,128)S(1)}, f32[2,8,128]{2,1,0:T(8,128)S(1)}, u32[]{:S(2)}, u32[]{:S(2)}) %collective-permute-start.20) | collective-permute-done | bytes 8224 | tf_op jit(solution)/shard_map/update/ppermute | solution.py:348
  96.0 2.6 %update.5 = (f32[2,128,2048]{2,1,0:T(8,128)}, bf16[2,2048,128]{2,1,0:T(8,128)(2,1)}) custom-call(s32[2]{0:T(128)S(1)} %pad_add_fusion.ids.refs_0_, f32[2,128,128]{2,1,0:T(8,128)S(1)} %get-tuple-element.38.left, bf16[2,4,256,256]{3,2,1,0:T(8,128)(2,1)S(1)} %get-tuple-element.39.early, bf16[2,4,256,256]{3,2,1,0:T(8,128)(2,1)S(1)} %get-tuple-element.47.rest, ...), custom_call_target="tpu_custom_call" | custom-call | flops 838860800 | bytes 6291456 | tf_op jit(solution)/shard_map/update/pallas_call | solution.py:36
  (47 shorter events, 2.9 us)
Async XLA Ops:
  0.6 7.3 %copy-start.1 = (f32[2,128,2048]{2,1,0:T(8,128)S(1)}, f32[2,128,2048]{2,1,0:T(8,128)}, u32[]{:S(2)}) copy-start(f32[2,128,2048]{2,1,0:T(8,128)} %momentum.1) | copy-start | bytes 6291460
  0.6 7.3 %copy-start.2 = (bf16[2,128,2048]{2,1,0:T(8,128)(2,1)S(1)}, bf16[2,128,2048]{2,1,0:T(8,128)(2,1)}, u32[]{:S(2)}) copy-start(bf16[2,128,2048]{2,1,0:T(8,128)(2,1)} %gradient.1) | copy-start | bytes 3145732
  3.3 6.2 %collective-permute-start.2 = (f32[2,128,128]{2,1,0:T(8,128)S(1)}, f32[2,128,128]{2,1,0:T(8,128)S(1)}, u32[]{:S(2)}, u32[]{:S(2)}) collective-permute-start(f32[2,128,128]{2,1,0:T(8,128)S(1)} %panel.1.p0), channel_id=1, source_target_pairs={{0,2},{1,3},{2,0},{3,1},{4,6},{5,7},{6,4},{7,5},{8,10},{9,11},{10,... | collective-permute-start | bytes 393224 | tf_op jit(solution)/shard_map/panel/ppermute | solution.py:348
  7.2 7.7 %collective-permute-start.1 = (f32[2,128,128]{2,1,0:T(8,128)S(1)}, f32[2,128,128]{2,1,0:T(8,128)S(1)}, u32[]{:S(2)}, u32[]{:S(2)}) collective-permute-start(f32[2,128,128]{2,1,0:T(8,128)S(1)} %panel.1.p0), channel_id=1, source_target_pairs={{0,3},{1,2},{2,1},{3,0},{4,7},{5,6},{6,5},{7,4},{8,11},{9,10},{10,... | collective-permute-start | bytes 393224 | tf_op jit(solution)/shard_map/panel/ppermute | solution.py:348
  7.9 6.9 %collective-permute-start = (f32[2,128,128]{2,1,0:T(8,128)S(1)}, f32[2,128,128]{2,1,0:T(8,128)S(1)}, u32[]{:S(2)}, u32[]{:S(2)}) collective-permute-start(f32[2,128,128]{2,1,0:T(8,128)S(1)} %panel.1.p0), channel_id=1, source_target_pairs={{0,1},{1,0},{2,3},{3,2},{4,5},{5,4},{6,7},{7,6},{8,9},{9,8},{10,11... | collective-permute-start | bytes 393224 | tf_op jit(solution)/shard_map/panel/ppermute | solution.py:348
  15.8 2.7 %collective-permute-start.4 = (f32[2,160,256]{2,1,0:T(8,128)S(1)}, f32[2,160,256]{2,1,0:T(8,128)S(1)}, u32[]{:S(2)}, u32[]{:S(2)}) collective-permute-start(f32[2,160,256]{2,1,0:T(8,128)S(1)} %get-tuple-element.32), channel_id=1, source_target_pairs={{0,4},{4,0},{8,12},{12,8},{16,20},{20,16},{24,28},{28,24},{32,36},... | collective-permute-start | bytes 983048 | tf_op jit(solution)/shard_map/product/ppermute | solution.py:334
  17.6 8.6 %collective-permute-start.3 = (f32[2,384,256]{2,1,0:T(8,128)S(1)}, f32[2,384,256]{2,1,0:T(8,128)S(1)}, u32[]{:S(2)}, u32[]{:S(2)}) collective-permute-start(f32[2,384,256]{2,1,0:T(8,128)S(1)} %product.6), channel_id=1, source_target_pairs={{0,4},{4,0},{8,12},{12,8},{16,20},{20,16},{24,28},{28,24},{32,36},... | collective-permute-start | bytes 2359304 | tf_op jit(solution)/shard_map/product/ppermute | solution.py:334
  18.6 6.6 %collective-permute-start.5 = (f32[160,256]{1,0:T(8,128)S(1)}, f32[160,256]{1,0:T(8,128)S(1)}, u32[]{:S(2)}, u32[]{:S(2)}) collective-permute-start(f32[160,256]{1,0:T(8,128)S(1)} %bitcast.33), channel_id=1, source_target_pairs={{0,24},{4,28},{8,16},{12,20},{16,8},{20,12},{24,0},{28,4},{32,56},... | collective-permute-start | bytes 491528 | tf_op jit(solution)/shard_map/scatter/ppermute | solution.py:339
  21.2 5.1 %collective-permute-start.7 = (f32[160,256]{1,0:T(8,128)S(1)}, f32[160,256]{1,0:T(8,128)S(1)}, u32[]{:S(2)}, u32[]{:S(2)}) collective-permute-start(f32[160,256]{1,0:T(8,128)S(1)} %bitcast.32), channel_id=1, source_target_pairs={{0,8},{4,12},{8,0},{12,4},{16,24},{20,28},{24,16},{28,20},{32,40},... | collective-permute-start | bytes 491528 | tf_op jit(solution)/shard_map/scatter/ppermute | solution.py:339
  26.5 6.9 %collective-permute-start.6 = (f32[288,256]{1,0:T(8,128)S(1)}, f32[288,256]{1,0:T(8,128)S(1)}, u32[]{:S(2)}, u32[]{:S(2)}) collective-permute-start(f32[288,256]{1,0:T(8,128)S(1)} %pad_maximum_fusion), channel_id=1, source_target_pairs={{0,8},{4,12},{8,0},{12,4},{16,24},{20,28},{24,16},{28,20},{32,40},... | collective-permute-start | bytes 884744 | tf_op jit(solution)/shard_map/scatter/ppermute | solution.py:339
  26.7 8.0 %collective-permute-start.8 = (f32[288,256]{1,0:T(8,128)S(1)}, f32[288,256]{1,0:T(8,128)S(1)}, u32[]{:S(2)}, u32[]{:S(2)}) collective-permute-start(f32[288,256]{1,0:T(8,128)S(1)} %pad_maximum_fusion.1), channel_id=1, source_target_pairs={{0,24},{4,28},{8,16},{12,20},{16,8},{20,12},{24,0},{28,4},{32,56},... | collective-permute-start | bytes 884744 | tf_op jit(solution)/shard_map/scatter/ppermute | solution.py:339
  65.2 6.2 %collective-permute-start.9 = (f32[2,32,256]{2,1,0:T(8,128)S(1)}, f32[2,32,256]{2,1,0:T(8,128)S(1)}, u32[]{:S(2)}, u32[]{:S(2)}) collective-permute-start(f32[2,32,256]{2,1,0:T(8,128)S(1)} %get-tuple-element.33.own), channel_id=1, source_target_pairs={{0,4},{4,0},{8,12},{12,8},{16,20},{20,16},{24,28},{28,24},{32,36},... | collective-permute-start | bytes 196616 | tf_op jit(solution)/shard_map/gather/ppermute | solution.py:334
  70.6 10.5 %collective-permute-start.12 = (f32[2,128,256]{2,1,0:T(8,128)S(1)}, f32[2,128,256]{2,1,0:T(8,128)S(1)}, u32[]{:S(2)}, u32[]{:S(2)}) collective-permute-start(f32[2,128,256]{2,1,0:T(8,128)S(1)} %get-tuple-element.34.a0), channel_id=1, source_target_pairs={{0,4},{4,0},{8,12},{12,8},{16,20},{20,16},{24,28},{28,24},{32,36},... | collective-permute-start | bytes 786440 | tf_op jit(solution)/shard_map/gather/ppermute | solution.py:334
  70.7 8.7 %collective-permute-start.11 = (f32[2,128,256]{2,1,0:T(8,128)S(1)}, f32[2,128,256]{2,1,0:T(8,128)S(1)}, u32[]{:S(2)}, u32[]{:S(2)}) collective-permute-start(f32[2,128,256]{2,1,0:T(8,128)S(1)} %get-tuple-element.34.a0), channel_id=1, source_target_pairs={{0,24},{4,28},{8,16},{12,20},{16,8},{20,12},{24,0},{28,4},{32,56},... | collective-permute-start | bytes 786440 | tf_op jit(solution)/shard_map/gather/ppermute | solution.py:339
  71.4 7.9 %collective-permute-start.10 = (f32[2,128,256]{2,1,0:T(8,128)S(1)}, f32[2,128,256]{2,1,0:T(8,128)S(1)}, u32[]{:S(2)}, u32[]{:S(2)}) collective-permute-start(f32[2,128,256]{2,1,0:T(8,128)S(1)} %get-tuple-element.34.a0), channel_id=1, source_target_pairs={{0,8},{4,12},{8,0},{12,4},{16,24},{20,28},{24,16},{28,20},{32,40},... | collective-permute-start | bytes 786440 | tf_op jit(solution)/shard_map/gather/ppermute | solution.py:339
  79.4 4.5 %collective-permute-start.13 = (f32[128,256]{1,0:T(8,128)S(1)}, f32[128,256]{1,0:T(8,128)S(1)}, u32[]{:S(2)}, u32[]{:S(2)}) collective-permute-start(f32[128,256]{1,0:T(8,128)S(1)} %slice_bitcast_fusion.5), channel_id=1, source_target_pairs={{0,8},{4,12},{8,0},{12,4},{16,24},{20,28},{24,16},{28,20},{32,40},... | collective-permute-start | bytes 393224 | tf_op jit(solution)/shard_map/gather/ppermute | solution.py:339
  79.5 5.1 %collective-permute-start.14 = (f32[128,256]{1,0:T(8,128)S(1)}, f32[128,256]{1,0:T(8,128)S(1)}, u32[]{:S(2)}, u32[]{:S(2)}) collective-permute-start(f32[128,256]{1,0:T(8,128)S(1)} %slice_bitcast_fusion.4), channel_id=1, source_target_pairs={{0,24},{4,28},{8,16},{12,20},{16,8},{20,12},{24,0},{28,4},{32,56},... | collective-permute-start | bytes 393224 | tf_op jit(solution)/shard_map/gather/ppermute | solution.py:339
  84.6 4.3 %collective-permute-start.15 = (f32[2,128,256]{2,1,0:T(8,128)S(1)}, f32[2,128,256]{2,1,0:T(8,128)S(1)}, u32[]{:S(2)}, u32[]{:S(2)}) collective-permute-start(f32[2,128,256]{2,1,0:T(8,128)S(1)} %collective-permute-done.10.a1), channel_id=1, source_target_pairs={{0,4},{4,0},{8,12},{12,8},{16,20},{20,16},{24,28},{28,24},{32,36},... | collective-permute-start | bytes 786440 | tf_op jit(solution)/shard_map/gather/ppermute | solution.py:334
  87.0 1.9 %collective-permute-start.16 = (f32[2,128,256]{2,1,0:T(8,128)S(1)}, f32[2,128,256]{2,1,0:T(8,128)S(1)}, u32[]{:S(2)}, u32[]{:S(2)}) collective-permute-start(f32[2,128,256]{2,1,0:T(8,128)S(1)} %collective-permute-done.11.a3), channel_id=1, source_target_pairs={{0,4},{4,0},{8,12},{12,8},{16,20},{20,16},{24,28},{28,24},{32,36},... | collective-permute-start | bytes 786440 | tf_op jit(solution)/shard_map/gather/ppermute | solution.py:334
  87.0 1.7 %collective-permute-start.17 = (f32[128,256]{1,0:T(8,128)S(1)}, f32[128,256]{1,0:T(8,128)S(1)}, u32[]{:S(2)}, u32[]{:S(2)}) collective-permute-start(f32[128,256]{1,0:T(8,128)S(1)} %collective-permute-done.13.a20), channel_id=1, source_target_pairs={{0,4},{4,0},{8,12},{12,8},{16,20},{20,16},{24,28},{28,24},{32,36},... | collective-permute-start | bytes 393224 | tf_op jit(solution)/shard_map/gather/ppermute | solution.py:334
  87.5 1.4 %collective-permute-start.18 = (f32[128,256]{1,0:T(8,128)S(1)}, f32[128,256]{1,0:T(8,128)S(1)}, u32[]{:S(2)}, u32[]{:S(2)}) collective-permute-start(f32[128,256]{1,0:T(8,128)S(1)} %collective-permute-done.14.a21), channel_id=1, source_target_pairs={{0,4},{4,0},{8,12},{12,8},{16,20},{20,16},{24,28},{28,24},{32,36},... | collective-permute-start | bytes 393224 | tf_op jit(solution)/shard_map/gather/ppermute | solution.py:334
  89.5 5.2 %collective-permute-start.21 = (f32[2,8,128]{2,1,0:T(8,128)S(1)}, f32[2,8,128]{2,1,0:T(8,128)S(1)}, u32[]{:S(2)}, u32[]{:S(2)}) collective-permute-start(f32[2,8,128]{2,1,0:T(8,128)S(1)} %get-tuple-element.51.s0), channel_id=1, source_target_pairs={{0,3},{1,2},{2,1},{3,0},{4,7},{5,6},{6,5},{7,4},{8,11},{9,10},{10,... | collective-permute-start | bytes 24584 | tf_op jit(solution)/shard_map/update/ppermute | solution.py:348
  92.0 4.0 %collective-permute-start.20 = (f32[2,8,128]{2,1,0:T(8,128)S(1)}, f32[2,8,128]{2,1,0:T(8,128)S(1)}, u32[]{:S(2)}, u32[]{:S(2)}) collective-permute-start(f32[2,8,128]{2,1,0:T(8,128)S(1)} %get-tuple-element.51.s0), channel_id=1, source_target_pairs={{0,2},{1,3},{2,0},{3,1},{4,6},{5,7},{6,4},{7,5},{8,10},{9,11},{10,... | collective-permute-start | bytes 24584 | tf_op jit(solution)/shard_map/update/ppermute | solution.py:348
  92.5 3.5 %collective-permute-start.19 = (f32[2,8,128]{2,1,0:T(8,128)S(1)}, f32[2,8,128]{2,1,0:T(8,128)S(1)}, u32[]{:S(2)}, u32[]{:S(2)}) collective-permute-start(f32[2,8,128]{2,1,0:T(8,128)S(1)} %get-tuple-element.51.s0), channel_id=1, source_target_pairs={{0,1},{1,0},{2,3},{3,2},{4,5},{5,4},{6,7},{7,6},{8,9},{9,8},{10,11... | collective-permute-start | bytes 24584 | tf_op jit(solution)/shard_map/update/ppermute | solution.py:348
  92.8 3.2 %copy-start = (f32[2,128,2048]{2,1,0:T(8,128)S(1)}, f32[2,128,2048]{2,1,0:T(8,128)}, u32[]{:S(2)}) copy-start(f32[2,128,2048]{2,1,0:T(8,128)} %weight.1) | copy-start | bytes 6291460
